TPU v7x, 512 devices: a whole 4x4x16 slice. The times are simulated.
512 devices in a mesh: ctx: 64 (over z, x), tp: 8 (over y, core).
Axes of the slice: x: 4, y: 4, z: 16, core: 2. Of those that a mesh axis runs over, the one named last changes fastest.
Arguments:
- query_rows: bfloat16 [24576, 2048], P('ctx', 'tp'), may hold values from -24 to 24
- key_rows: bfloat16 [24576, 1024], P('ctx', 'tp'), may hold values from -6 to 6
- value_rows: bfloat16 [24576, 1024], P('ctx', 'tp'), may hold values from -6 to 6
- grad_out: bfloat16 [24576, 4608], P('ctx', 'tp'), may hold values from -6 to 6
- out_weight: bfloat16 [2048, 4608], P('tp'), may hold values from -0.125 to 0.125
- doc_lengths: int32 [18], replicated, may hold values from 1 to 2689, 24576 in all
- doc_order: int32 [18], replicated, may hold values from 0 to 17, each once
Outputs:
- query_grads: bfloat16 [24576, 2048], P('ctx', 'tp')
- key_grads: bfloat16 [24576, 1024], P('ctx', 'tp')
- value_grads: bfloat16 [24576, 1024], P('ctx', 'tp')
Inputs may be any that keep to these rules, and one draw needn't show every extreme that they name: `doc_lengths`: the lengths sum to 24576; the longest has exactly 2689 tokens. `doc_order`: each of 0 to 17 appears once.
All inputs are finite; a program needn't handle non-finite values.
Results may differ from a plain program's by a relative error of at most 0.012.
Values may be sent and summed in bfloat16 or wider, within the bound.
No kernel may reach another device: no remote copies, remote signals or barrier semaphores. Data moves between devices by JAX's collectives and lax.ppermute only.
A program may use at most 64 MiB of HBM per device.

v0:
```python
import jax
import jax.numpy as jnp
from jax import lax
from jax.sharding import PartitionSpec as P

HD = 128


SOFT_CAP = 50.0
SCORE_SCALE = 1.0 / 12.0


def passed_along(block, axis, distance):
    devices = range(lax.axis_size(axis))
    route = [(i - distance, i) for i in devices if i - distance in devices]
    return lax.ppermute(block, axis, route)


def doc_index(places, doc_lengths, doc_order):
    numbers = jnp.arange(doc_lengths.shape[0], dtype=jnp.int32)
    picked = (doc_order[:, None] == numbers[None, :]).astype(jnp.int32)
    ordered = jnp.sum(picked * doc_lengths[None, :], axis=1, dtype=jnp.int32)
    bounds = jnp.cumsum(ordered, dtype=jnp.int32)
    return jnp.sum((places[:, None] >= bounds[None, :]).astype(jnp.int32), axis=1, dtype=jnp.int32)


def visible_pairs(query_places, key_places, query_docs, key_docs):
    same_doc = query_docs[:, None] == key_docs[None, :]
    causal = key_places[None, :] <= query_places[:, None]
    return same_doc & causal & (key_places[None, :] >= 0)


def capped_scores(query_block, key_block):
    raw_scores = jnp.einsum(
        "qhe,khe->hqk", query_block, key_block, preferred_element_type=jnp.float32
    )
    return SOFT_CAP * jnp.tanh(raw_scores * (SCORE_SCALE / SOFT_CAP))


def widen(block, group):
    return jnp.repeat(block, group, axis=1)


def fold_group(terms, kv_count, group):
    return jnp.sum(terms.reshape(terms.shape[0], kv_count, group, terms.shape[2]), axis=2)


def key_window(key_pairs, reach_count):
    blocks = [key_pairs]
    moving = key_pairs
    for offset in range(reach_count):
        moving = passed_along(moving, "ctx", 1)
        blocks.append(moving)
    return jnp.stack(blocks, 0)


def return_grads(pieces, reach_count):
    summed = pieces[reach_count]
    for offset in range(reach_count - 1, -1, -1):
        summed = (
            passed_along(summed.astype(jnp.bfloat16), "ctx", -1).astype(summed.dtype)
            + pieces[offset]
        )
    return summed


def on_device(query_rows, key_rows, value_rows, grad_out, out_weight, doc_lengths, doc_order):
    row_count = query_rows.shape[0]
    head_count = query_rows.shape[1] // HD
    kv_count = key_rows.shape[1] // HD
    group = head_count // kv_count
    reach_count = 2 ** min(3, lax.axis_size("ctx") // 8) - 1
    local_places = lax.axis_index("ctx") * row_count + jnp.arange(row_count, dtype=jnp.int32)
    local_docs = doc_index(local_places, doc_lengths, doc_order)
    head_grads = lax.dot_general(
        lax.all_gather(grad_out, "tp", axis=1, tiled=True),
        out_weight,
        (((1,), (1,)), ((), ())),
        preferred_element_type=jnp.float32,
    ).astype(jnp.bfloat16)
    grad_heads = head_grads.reshape(row_count, head_count, HD)
    queries = query_rows.reshape(row_count, head_count, HD)
    keys_local = key_rows.reshape(row_count, kv_count, HD)
    values_local = value_rows.reshape(row_count, kv_count, HD)
    key_pairs = jnp.stack([keys_local, values_local], 0)
    window = key_window(key_pairs, reach_count)
    offsets = jnp.arange(reach_count + 1, dtype=jnp.int32)

    def block_mask(offset):
        key_places = local_places - offset * row_count
        return visible_pairs(
            local_places, key_places, local_docs, doc_index(key_places, doc_lengths, doc_order)
        )

    def first_pass(state_pair, inputs):
        pair_block, offset = inputs
        visible = block_mask(offset)

        def attend(current):
            sum_now, accum_now = current
            scores = capped_scores(queries, widen(pair_block[0], group))
            exponentials = jnp.where(visible[None], jnp.exp(scores), 0.0)
            weights = exponentials.astype(jnp.bfloat16)
            gathered = jnp.einsum(
                "hqk,khe->qhe",
                weights,
                widen(pair_block[1], group),
                preferred_element_type=jnp.float32,
            )
            return (sum_now + jnp.sum(exponentials, axis=2), accum_now + gathered)

        def unchanged(current):
            return current

        return (lax.cond(jnp.any(visible), attend, unchanged, state_pair), None)

    start_pair = (
        jnp.zeros((head_count, row_count), jnp.float32),
        jnp.zeros((row_count, head_count, HD), jnp.float32),
    )
    (exp_sums, accum), unused_out = lax.scan(first_pass, start_pair, (window, offsets))
    log_sums = jnp.log(exp_sums)
    attended = accum / exp_sums.T[:, :, None]
    deltas = jnp.sum(grad_heads.astype(jnp.float32) * attended, axis=2).T

    def second_pass(query_acc, inputs):
        pair_block, offset = inputs
        visible = block_mask(offset)

        def backward(acc_now):
            wide_keys = widen(pair_block[0], group)
            scores = capped_scores(queries, wide_keys)
            probs = jnp.where(visible[None], jnp.exp(scores - log_sums[:, :, None]), 0.0)
            dprob = jnp.einsum(
                "qhe,khe->hqk",
                grad_heads,
                widen(pair_block[1], group),
                preferred_element_type=jnp.float32,
            )
            ratio = scores / SOFT_CAP
            slopes = (
                probs * (dprob - deltas[:, :, None]) * (1.0 - ratio * ratio) * SCORE_SCALE
            ).astype(jnp.bfloat16)
            acc_next = acc_now + jnp.einsum(
                "hqk,khe->qhe", slopes, wide_keys, preferred_element_type=jnp.float32
            )
            key_part = jnp.einsum(
                "hqk,qhe->khe", slopes, queries, preferred_element_type=jnp.float32
            )
            value_part = jnp.einsum(
                "hqk,qhe->khe",
                probs.astype(jnp.bfloat16),
                grad_heads,
                preferred_element_type=jnp.float32,
            )
            return (
                acc_next,
                jnp.stack(
                    [
                        fold_group(key_part, kv_count, group),
                        fold_group(value_part, kv_count, group),
                    ],
                    0,
                ),
            )

        def skipped(acc_now):
            return (acc_now, jnp.zeros((2, row_count, kv_count, HD), jnp.float32))

        return lax.cond(jnp.any(visible), backward, skipped, query_acc)

    query_acc, pieces = lax.scan(
        second_pass, jnp.zeros((row_count, head_count, HD), jnp.float32), (window, offsets)
    )
    key_value = return_grads(pieces, reach_count)
    query_grads = query_acc.reshape(row_count, head_count * HD).astype(jnp.bfloat16)
    key_grads = key_value[0].reshape(row_count, kv_count * HD).astype(jnp.bfloat16)
    value_grads = key_value[1].reshape(row_count, kv_count * HD).astype(jnp.bfloat16)
    return (query_grads, key_grads, value_grads)


def solution(mesh):
    in_specs = (
        P("ctx", "tp"),
        P("ctx", "tp"),
        P("ctx", "tp"),
        P("ctx", "tp"),
        P("tp", None),
        P(),
        P(),
    )
    out_specs = (P("ctx", "tp"), P("ctx", "tp"), P("ctx", "tp"))
    return jax.shard_map(
        on_device, mesh=mesh, in_specs=in_specs, out_specs=out_specs, check_vma=False
    )
```

profile of v0, /device:TPU:230, one launch (start us, length us, event | category | flops | bytes accessed | tf_op | source)
XLA Modules:
  0.0 291.8 jit_solution(16937075390460398981)
XLA Ops:
  8.9 5.0 %collective-permute-start = (bf16[2,384,1,128]{3,1,0,2:T(8,128)(2,1)S(1)}, bf16[2,384,1,128]{3,1,0,2:T(8,128)(2,1)S(1)}, u32[]{:S(2)}, u32[]{:S(2)}) collective-permute-start(bf16[2,384,1,128]{3,1,0,2:T(8,128)(2,1)S(1)} %pad_maximum_fusion), channel_id=1, source_target_pairs={{0,8},{8,16},{16,24},{24,32},{32,40},{40,48},{48,56},{56,64},{64,7... | collective-permute-start | bytes 589832 | tf_op jit(solution)/shard_map/ppermute | solution.py:16
  16.5 1.6 collective-permute-done
  18.0 7.7 %collective-permute-start.1 = (bf16[2,384,1,128]{3,1,0,2:T(8,128)(2,1)S(1)}, bf16[2,384,1,128]{3,1,0,2:T(8,128)(2,1)S(1)}, u32[]{:S(2)}, u32[]{:S(2)}) collective-permute-start(bf16[2,384,1,128]{3,1,0,2:T(8,128)(2,1)S(1)} %collective-permute-done), channel_id=1, source_target_pairs={{0,8},{8,16},{16,24},{24,32},{32,40},{40,48},{48,56},{56,64},{64,7... | collective-permute-start | bytes 589832 | tf_op jit(solution)/shard_map/ppermute | solution.py:16
  25.8 3.2 %collective-permute-done.1 = bf16[2,384,1,128]{3,1,0,2:T(8,128)(2,1)S(1)} collective-permute-done((bf16[2,384,1,128]{3,1,0,2:T(8,128)(2,1)S(1)}, bf16[2,384,1,128]{3,1,0,2:T(8,128)(2,1)S(1)}, u32[]{:S(2)}, u32[]{:S(2)}) %collective-permute-start.1) | collective-permute-done | bytes 196640 | tf_op jit(solution)/shard_map/ppermute | solution.py:16
  29.0 7.7 %collective-permute-start.2 = (bf16[2,384,1,128]{3,1,0,2:T(8,128)(2,1)S(1)}, bf16[2,384,1,128]{3,1,0,2:T(8,128)(2,1)S(1)}, u32[]{:S(2)}, u32[]{:S(2)}) collective-permute-start(bf16[2,384,1,128]{3,1,0,2:T(8,128)(2,1)S(1)} %collective-permute-done.1), channel_id=1, source_target_pairs={{0,8},{8,16},{16,24},{24,32},{32,40},{40,48},{48,56},{56,64},{64,7... | collective-permute-start | bytes 589832 | tf_op jit(solution)/shard_map/ppermute | solution.py:16
  36.7 3.1 %collective-permute-done.2 = bf16[2,384,1,128]{3,1,0,2:T(8,128)(2,1)S(1)} collective-permute-done((bf16[2,384,1,128]{3,1,0,2:T(8,128)(2,1)S(1)}, bf16[2,384,1,128]{3,1,0,2:T(8,128)(2,1)S(1)}, u32[]{:S(2)}, u32[]{:S(2)}) %collective-permute-start.2) | collective-permute-done | bytes 196640 | tf_op jit(solution)/shard_map/ppermute | solution.py:16
  39.9 7.7 %collective-permute-start.3 = (bf16[2,384,1,128]{3,1,0,2:T(8,128)(2,1)S(1)}, bf16[2,384,1,128]{3,1,0,2:T(8,128)(2,1)S(1)}, u32[]{:S(2)}, u32[]{:S(2)}) collective-permute-start(bf16[2,384,1,128]{3,1,0,2:T(8,128)(2,1)S(1)} %collective-permute-done.2), channel_id=1, source_target_pairs={{0,8},{8,16},{16,24},{24,32},{32,40},{40,48},{48,56},{56,64},{64,7... | collective-permute-start | bytes 589832 | tf_op jit(solution)/shard_map/ppermute | solution.py:16
  47.6 3.1 %collective-permute-done.3 = bf16[2,384,1,128]{3,1,0,2:T(8,128)(2,1)S(1)} collective-permute-done((bf16[2,384,1,128]{3,1,0,2:T(8,128)(2,1)S(1)}, bf16[2,384,1,128]{3,1,0,2:T(8,128)(2,1)S(1)}, u32[]{:S(2)}, u32[]{:S(2)}) %collective-permute-start.3) | collective-permute-done | bytes 196640 | tf_op jit(solution)/shard_map/ppermute | solution.py:16
  50.8 7.7 %collective-permute-start.4 = (bf16[2,384,1,128]{3,1,0,2:T(8,128)(2,1)S(1)}, bf16[2,384,1,128]{3,1,0,2:T(8,128)(2,1)S(1)}, u32[]{:S(2)}, u32[]{:S(2)}) collective-permute-start(bf16[2,384,1,128]{3,1,0,2:T(8,128)(2,1)S(1)} %collective-permute-done.3), channel_id=1, source_target_pairs={{0,8},{8,16},{16,24},{24,32},{32,40},{40,48},{48,56},{56,64},{64,7... | collective-permute-start | bytes 589832 | tf_op jit(solution)/shard_map/ppermute | solution.py:16
  58.5 3.1 %collective-permute-done.4 = bf16[2,384,1,128]{3,1,0,2:T(8,128)(2,1)S(1)} collective-permute-done((bf16[2,384,1,128]{3,1,0,2:T(8,128)(2,1)S(1)}, bf16[2,384,1,128]{3,1,0,2:T(8,128)(2,1)S(1)}, u32[]{:S(2)}, u32[]{:S(2)}) %collective-permute-start.4) | collective-permute-done | bytes 196640 | tf_op jit(solution)/shard_map/ppermute | solution.py:16
  61.6 7.7 %collective-permute-start.5 = (bf16[2,384,1,128]{3,1,0,2:T(8,128)(2,1)S(1)}, bf16[2,384,1,128]{3,1,0,2:T(8,128)(2,1)S(1)}, u32[]{:S(2)}, u32[]{:S(2)}) collective-permute-start(bf16[2,384,1,128]{3,1,0,2:T(8,128)(2,1)S(1)} %collective-permute-done.4), channel_id=1, source_target_pairs={{0,8},{8,16},{16,24},{24,32},{32,40},{40,48},{48,56},{56,64},{64,7... | collective-permute-start | bytes 589832 | tf_op jit(solution)/shard_map/ppermute | solution.py:16
  69.4 3.1 %collective-permute-done.5 = bf16[2,384,1,128]{3,1,0,2:T(8,128)(2,1)S(1)} collective-permute-done((bf16[2,384,1,128]{3,1,0,2:T(8,128)(2,1)S(1)}, bf16[2,384,1,128]{3,1,0,2:T(8,128)(2,1)S(1)}, u32[]{:S(2)}, u32[]{:S(2)}) %collective-permute-start.5) | collective-permute-done | bytes 196640 | tf_op jit(solution)/shard_map/ppermute | solution.py:16
  72.5 7.7 %collective-permute-start.6 = (bf16[2,384,1,128]{3,1,0,2:T(8,128)(2,1)S(1)}, bf16[2,384,1,128]{3,1,0,2:T(8,128)(2,1)S(1)}, u32[]{:S(2)}, u32[]{:S(2)}) collective-permute-start(bf16[2,384,1,128]{3,1,0,2:T(8,128)(2,1)S(1)} %collective-permute-done.5), channel_id=1, source_target_pairs={{0,8},{8,16},{16,24},{24,32},{32,40},{40,48},{48,56},{56,64},{64,7... | collective-permute-start | bytes 589832 | tf_op jit(solution)/shard_map/ppermute | solution.py:16
  80.2 3.1 %collective-permute-done.6 = bf16[2,384,1,128]{3,1,0,2:T(8,128)(2,1)S(1)} collective-permute-done((bf16[2,384,1,128]{3,1,0,2:T(8,128)(2,1)S(1)}, bf16[2,384,1,128]{3,1,0,2:T(8,128)(2,1)S(1)}, u32[]{:S(2)}, u32[]{:S(2)}) %collective-permute-start.6) | collective-permute-done | bytes 196640 | tf_op jit(solution)/shard_map/ppermute | solution.py:16
  84.5 39.8 %while.29 = (s32[]{:T(128)}, f32[2,384]{1,0:T(2,128)S(1)}, f32[384,2,128]{2,0,1:T(8,128)S(1)}, s32[384]{0:T(512)S(1)}, s32[8]{0:T(128)S(1)}, /*index=5*/s32[18]{...) while((s32[]{:T(128)}, f32[2,384]{1,0:T(2,128)S(1)}, ...), condition=%wide.region_11.12_spmd.clone, body=%wide.region_3.11_spmd.clone.sunk | while | flops 153328624 | bytes 3073783 | solution.py:121
  88.0 2.0 conditional.6
  93.5 2.0 conditional.6
  99.0 2.0 conditional.6
  104.4 2.0 conditional.6
  109.9 2.0 conditional.6
  115.4 2.0 conditional.6
  124.4 3.4 %convolution_convert_fusion = bf16[384,256]{0,1:T(8,128)(2,1)S(1)} fusion(bf16[256,4608]{1,0:T(8,128)(2,1)S(1)} %copy-done, bf16[384,4608]{0,1:T(8,128)(2,1)} %all-gather.2.cloned.1.call-done), kind=kOutput, calls=%fused_computation.56 | convolution fusion | flops 906067968 | bytes 6094848 | tf_op jit(solution)/shard_map/dot_general | solution.py:75
  128.9 60.7 %while.30 = (s32[]{:T(128)}, f32[384,2,128]{2,0,1:T(8,128)S(1)}, f32[8,2,384,1,128]{4,2,1,3,0:T(8,128)}, s32[384]{0:T(512)S(1)}, s32[8]{0:T(128)}, /*index=5*/s3...) while((s32[]{:T(128)}, f32[384,2,128]{2,0,1:T(8,128)S(1)}, ...), condition=%wide.region_20.21_spmd.clone, body=%wide.region_13.20_spmd.clone.sunk | while | flops 382868448 | bytes 10001671 | solution.py:172
  128.9 1.2 dynamic_slice.25
  133.3 3.1 %conditional.7 = (f32[384,2,128]{2,0,1:T(8,128)S(1)}, f32[1,2,384,1,128]{4,2,1,3,0:T(8,128)S(1)}) conditional(s32[]{:T(128)} %convert_element_type.158, f32[384,2,128]{2,0,1:T(8,128)S(1)} %get-tuple-element.621, (pred[384,384]{0,1:T(8,128)(4,1)S(1)}, bf16[8,2,384,1,128]{4,2,3,1,0:T(8,128)(2,1)}, s32[]{:T(128)}, ...), branch_computations={%region_18.18_spmd, %region_19.19_spmd} | conditional | flops 382107648 | bytes 9053220 | solution.py:170
  137.2 1.2 dynamic_slice.25
  141.7 3.1 %conditional.7 = (f32[384,2,128]{2,0,1:T(8,128)S(1)}, f32[1,2,384,1,128]{4,2,1,3,0:T(8,128)S(1)}) conditional(s32[]{:T(128)} %convert_element_type.158, f32[384,2,128]{2,0,1:T(8,128)S(1)} %get-tuple-element.621, (pred[384,384]{0,1:T(8,128)(4,1)S(1)}, bf16[8,2,384,1,128]{4,2,3,1,0:T(8,128)(2,1)}, s32[]{:T(128)}, ...), branch_computations={%region_18.18_spmd, %region_19.19_spmd} | conditional | flops 382107648 | bytes 9053220 | solution.py:170
  145.6 1.2 dynamic_slice.25
  150.0 3.1 %conditional.7 = (f32[384,2,128]{2,0,1:T(8,128)S(1)}, f32[1,2,384,1,128]{4,2,1,3,0:T(8,128)S(1)}) conditional(s32[]{:T(128)} %convert_element_type.158, f32[384,2,128]{2,0,1:T(8,128)S(1)} %get-tuple-element.621, (pred[384,384]{0,1:T(8,128)(4,1)S(1)}, bf16[8,2,384,1,128]{4,2,3,1,0:T(8,128)(2,1)}, s32[]{:T(128)}, ...), branch_computations={%region_18.18_spmd, %region_19.19_spmd} | conditional | flops 382107648 | bytes 9053220 | solution.py:170
  153.9 1.2 dynamic_slice.25
  158.4 3.1 %conditional.7 = (f32[384,2,128]{2,0,1:T(8,128)S(1)}, f32[1,2,384,1,128]{4,2,1,3,0:T(8,128)S(1)}) conditional(s32[]{:T(128)} %convert_element_type.158, f32[384,2,128]{2,0,1:T(8,128)S(1)} %get-tuple-element.621, (pred[384,384]{0,1:T(8,128)(4,1)S(1)}, bf16[8,2,384,1,128]{4,2,3,1,0:T(8,128)(2,1)}, s32[]{:T(128)}, ...), branch_computations={%region_18.18_spmd, %region_19.19_spmd} | conditional | flops 382107648 | bytes 9053220 | solution.py:170
  162.3 1.2 dynamic_slice.25
  166.7 3.1 %conditional.7 = (f32[384,2,128]{2,0,1:T(8,128)S(1)}, f32[1,2,384,1,128]{4,2,1,3,0:T(8,128)S(1)}) conditional(s32[]{:T(128)} %convert_element_type.158, f32[384,2,128]{2,0,1:T(8,128)S(1)} %get-tuple-element.621, (pred[384,384]{0,1:T(8,128)(4,1)S(1)}, bf16[8,2,384,1,128]{4,2,3,1,0:T(8,128)(2,1)}, s32[]{:T(128)}, ...), branch_computations={%region_18.18_spmd, %region_19.19_spmd} | conditional | flops 382107648 | bytes 9053220 | solution.py:170
  175.1 3.1 %conditional.7 = (f32[384,2,128]{2,0,1:T(8,128)S(1)}, f32[1,2,384,1,128]{4,2,1,3,0:T(8,128)S(1)}) conditional(s32[]{:T(128)} %convert_element_type.158, f32[384,2,128]{2,0,1:T(8,128)S(1)} %get-tuple-element.621, (pred[384,384]{0,1:T(8,128)(4,1)S(1)}, bf16[8,2,384,1,128]{4,2,3,1,0:T(8,128)(2,1)}, s32[]{:T(128)}, ...), branch_computations={%region_18.18_spmd, %region_19.19_spmd} | conditional | flops 382107648 | bytes 9053220 | solution.py:170
  190.6 1.9 collective-permute-start.7
  192.6 14.5 %collective-permute-done.7 = bf16[2,384,1,128]{3,1,2,0:T(8,128)(2,1)S(1)} collective-permute-done((bf16[2,384,1,128]{3,1,2,0:T(8,128)(2,1)S(1)}, bf16[2,384,1,128]{3,1,2,0:T(8,128)(2,1)S(1)}, u32[]{:S(2)}, u32[]{:S(2)}) %collective-permute-start.7) | collective-permute-done | bytes 196640 | tf_op jit(solution)/shard_map/ppermute | solution.py:16
  208.1 1.9 collective-permute-start.8
  210.0 9.8 %collective-permute-done.8 = bf16[2,384,1,128]{3,1,2,0:T(8,128)(2,1)S(1)} collective-permute-done((bf16[2,384,1,128]{3,1,2,0:T(8,128)(2,1)S(1)}, bf16[2,384,1,128]{3,1,2,0:T(8,128)(2,1)S(1)}, u32[]{:S(2)}, u32[]{:S(2)}) %collective-permute-start.8) | collective-permute-done | bytes 196640 | tf_op jit(solution)/shard_map/ppermute | solution.py:16
  220.9 1.9 collective-permute-start.9
  222.8 11.0 %collective-permute-done.9 = bf16[2,384,1,128]{3,1,2,0:T(8,128)(2,1)S(1)} collective-permute-done((bf16[2,384,1,128]{3,1,2,0:T(8,128)(2,1)S(1)}, bf16[2,384,1,128]{3,1,2,0:T(8,128)(2,1)S(1)}, u32[]{:S(2)}, u32[]{:S(2)}) %collective-permute-start.9) | collective-permute-done | bytes 196640 | tf_op jit(solution)/shard_map/ppermute | solution.py:16
  234.8 1.9 collective-permute-start.10
  236.8 10.2 %collective-permute-done.10 = bf16[2,384,1,128]{3,1,2,0:T(8,128)(2,1)S(1)} collective-permute-done((bf16[2,384,1,128]{3,1,2,0:T(8,128)(2,1)S(1)}, bf16[2,384,1,128]{3,1,2,0:T(8,128)(2,1)S(1)}, u32[]{:S(2)}, u32[]{:S(2)}) %collective-permute-start.10) | collective-permute-done | bytes 196640 | tf_op jit(solution)/shard_map/ppermute | solution.py:16
  248.0 1.9 collective-permute-start.11
  249.9 9.4 %collective-permute-done.11 = bf16[2,384,1,128]{3,1,2,0:T(8,128)(2,1)S(1)} collective-permute-done((bf16[2,384,1,128]{3,1,2,0:T(8,128)(2,1)S(1)}, bf16[2,384,1,128]{3,1,2,0:T(8,128)(2,1)S(1)}, u32[]{:S(2)}, u32[]{:S(2)}) %collective-permute-start.11) | collective-permute-done | bytes 196640 | tf_op jit(solution)/shard_map/ppermute | solution.py:16
  260.4 1.9 collective-permute-start.12
  262.3 9.0 %collective-permute-done.12 = bf16[2,384,1,128]{3,1,2,0:T(8,128)(2,1)S(1)} collective-permute-done((bf16[2,384,1,128]{3,1,2,0:T(8,128)(2,1)S(1)}, bf16[2,384,1,128]{3,1,2,0:T(8,128)(2,1)S(1)}, u32[]{:S(2)}, u32[]{:S(2)}) %collective-permute-start.12) | collective-permute-done | bytes 196640 | tf_op jit(solution)/shard_map/ppermute | solution.py:16
  272.3 1.9 collective-permute-start.13
  274.9 8.3 %collective-permute-done.13 = bf16[2,384,1,128]{3,1,2,0:T(8,128)(2,1)S(1)} collective-permute-done((bf16[2,384,1,128]{3,1,2,0:T(8,128)(2,1)S(1)}, bf16[2,384,1,128]{3,1,2,0:T(8,128)(2,1)S(1)}, u32[]{:S(2)}, u32[]{:S(2)}) %collective-permute-start.13) | collective-permute-done | bytes 196640 | tf_op jit(solution)/shard_map/ppermute | solution.py:16
  (270 shorter events, 90.1 us)
Async XLA Ops:
  7.2 117.3 %copy-start = (bf16[256,4608]{1,0:T(8,128)(2,1)S(1)}, bf16[256,4608]{1,0:T(8,128)(2,1)}, u32[]{:S(2)}) copy-start(bf16[256,4608]{1,0:T(8,128)(2,1)} %param.19) | copy-start | bytes 7077892
  7.2 9.2 %copy-start.2 = (bf16[384,128]{1,0:T(8,128)(2,1)S(1)}, bf16[384,128]{1,0:T(8,128)(2,1)}, u32[]{:S(2)}) copy-start(bf16[384,128]{1,0:T(8,128)(2,1)} %param.17) | copy-start | bytes 294916
  7.2 9.2 %copy-start.3 = (bf16[384,128]{1,0:T(8,128)(2,1)S(1)}, bf16[384,128]{1,0:T(8,128)(2,1)}, u32[]{:S(2)}) copy-start(bf16[384,128]{1,0:T(8,128)(2,1)} %param.16) | copy-start | bytes 294916
  7.2 117.2 %all-gather.2.cloned.1.call-start = ((), (), s32[]{:S(2)}) async-start(), calls=%async_computation | async-start | bytes 3981312 | tf_op jit(solution)/shard_map/all_gather | solution.py:76
  8.9 9.1 %collective-permute-start = (bf16[2,384,1,128]{3,1,0,2:T(8,128)(2,1)S(1)}, bf16[2,384,1,128]{3,1,0,2:T(8,128)(2,1)S(1)}, u32[]{:S(2)}, u32[]{:S(2)}) collective-permute-start(bf16[2,384,1,128]{3,1,0,2:T(8,128)(2,1)S(1)} %pad_maximum_fusion), channel_id=1, source_target_pairs={{0,8},{8,16},{16,24},{24,32},{32,40},{40,48},{48,56},{56,64},{64,7... | collective-permute-start | bytes 589832 | tf_op jit(solution)/shard_map/ppermute | solution.py:16
  16.5 68.1 %copy-start.4 = (s32[18]{0:T(128)S(1)}, s32[18]{0:T(128)}, u32[]{:S(2)}) copy-start(s32[18]{0:T(128)} %param.20) | copy-start | bytes 220
  16.5 68.1 %copy-start.5 = (s32[18]{0:T(128)S(1)}, s32[18]{0:T(128)}, u32[]{:S(2)}) copy-start(s32[18]{0:T(128)} %param.21) | copy-start | bytes 220
  18.0 11.0 %collective-permute-start.1 = (bf16[2,384,1,128]{3,1,0,2:T(8,128)(2,1)S(1)}, bf16[2,384,1,128]{3,1,0,2:T(8,128)(2,1)S(1)}, u32[]{:S(2)}, u32[]{:S(2)}) collective-permute-start(bf16[2,384,1,128]{3,1,0,2:T(8,128)(2,1)S(1)} %collective-permute-done), channel_id=1, source_target_pairs={{0,8},{8,16},{16,24},{24,32},{32,40},{40,48},{48,56},{56,64},{64,7... | collective-permute-start | bytes 589832 | tf_op jit(solution)/shard_map/ppermute | solution.py:16
  29.0 10.9 %collective-permute-start.2 = (bf16[2,384,1,128]{3,1,0,2:T(8,128)(2,1)S(1)}, bf16[2,384,1,128]{3,1,0,2:T(8,128)(2,1)S(1)}, u32[]{:S(2)}, u32[]{:S(2)}) collective-permute-start(bf16[2,384,1,128]{3,1,0,2:T(8,128)(2,1)S(1)} %collective-permute-done.1), channel_id=1, source_target_pairs={{0,8},{8,16},{16,24},{24,32},{32,40},{40,48},{48,56},{56,64},{64,7... | collective-permute-start | bytes 589832 | tf_op jit(solution)/shard_map/ppermute | solution.py:16
  39.9 10.9 %collective-permute-start.3 = (bf16[2,384,1,128]{3,1,0,2:T(8,128)(2,1)S(1)}, bf16[2,384,1,128]{3,1,0,2:T(8,128)(2,1)S(1)}, u32[]{:S(2)}, u32[]{:S(2)}) collective-permute-start(bf16[2,384,1,128]{3,1,0,2:T(8,128)(2,1)S(1)} %collective-permute-done.2), channel_id=1, source_target_pairs={{0,8},{8,16},{16,24},{24,32},{32,40},{40,48},{48,56},{56,64},{64,7... | collective-permute-start | bytes 589832 | tf_op jit(solution)/shard_map/ppermute | solution.py:16
  50.8 10.9 %collective-permute-start.4 = (bf16[2,384,1,128]{3,1,0,2:T(8,128)(2,1)S(1)}, bf16[2,384,1,128]{3,1,0,2:T(8,128)(2,1)S(1)}, u32[]{:S(2)}, u32[]{:S(2)}) collective-permute-start(bf16[2,384,1,128]{3,1,0,2:T(8,128)(2,1)S(1)} %collective-permute-done.3), channel_id=1, source_target_pairs={{0,8},{8,16},{16,24},{24,32},{32,40},{40,48},{48,56},{56,64},{64,7... | collective-permute-start | bytes 589832 | tf_op jit(solution)/shard_map/ppermute | solution.py:16
  61.6 10.9 %collective-permute-start.5 = (bf16[2,384,1,128]{3,1,0,2:T(8,128)(2,1)S(1)}, bf16[2,384,1,128]{3,1,0,2:T(8,128)(2,1)S(1)}, u32[]{:S(2)}, u32[]{:S(2)}) collective-permute-start(bf16[2,384,1,128]{3,1,0,2:T(8,128)(2,1)S(1)} %collective-permute-done.4), channel_id=1, source_target_pairs={{0,8},{8,16},{16,24},{24,32},{32,40},{40,48},{48,56},{56,64},{64,7... | collective-permute-start | bytes 589832 | tf_op jit(solution)/shard_map/ppermute | solution.py:16
  72.5 10.9 %collective-permute-start.6 = (bf16[2,384,1,128]{3,1,0,2:T(8,128)(2,1)S(1)}, bf16[2,384,1,128]{3,1,0,2:T(8,128)(2,1)S(1)}, u32[]{:S(2)}, u32[]{:S(2)}) collective-permute-start(bf16[2,384,1,128]{3,1,0,2:T(8,128)(2,1)S(1)} %collective-permute-done.5), channel_id=1, source_target_pairs={{0,8},{8,16},{16,24},{24,32},{32,40},{40,48},{48,56},{56,64},{64,7... | collective-permute-start | bytes 589832 | tf_op jit(solution)/shard_map/ppermute | solution.py:16
  83.4 1.1 copy-start.1
  190.6 16.4 %collective-permute-start.7 = (bf16[2,384,1,128]{3,1,2,0:T(8,128)(2,1)S(1)}, bf16[2,384,1,128]{3,1,2,0:T(8,128)(2,1)S(1)}, u32[]{:S(2)}, u32[]{:S(2)}) collective-permute-start(bf16[2,384,1,128]{3,1,2,0:T(8,128)(2,1)S(1)} %fusion.38), channel_id=1, source_target_pairs={{8,0},{16,8},{24,16},{32,24},{40,32},{48,40},{56,48},{64,56},{72,6... | collective-permute-start | bytes 589832 | tf_op jit(solution)/shard_map/ppermute | solution.py:16
  208.1 11.8 %collective-permute-start.8 = (bf16[2,384,1,128]{3,1,2,0:T(8,128)(2,1)S(1)}, bf16[2,384,1,128]{3,1,2,0:T(8,128)(2,1)S(1)}, u32[]{:S(2)}, u32[]{:S(2)}) collective-permute-start(bf16[2,384,1,128]{3,1,2,0:T(8,128)(2,1)S(1)} %fusion.37), channel_id=1, source_target_pairs={{8,0},{16,8},{24,16},{32,24},{40,32},{48,40},{56,48},{64,56},{72,6... | collective-permute-start | bytes 589832 | tf_op jit(solution)/shard_map/ppermute | solution.py:16
  220.9 12.9 %collective-permute-start.9 = (bf16[2,384,1,128]{3,1,2,0:T(8,128)(2,1)S(1)}, bf16[2,384,1,128]{3,1,2,0:T(8,128)(2,1)S(1)}, u32[]{:S(2)}, u32[]{:S(2)}) collective-permute-start(bf16[2,384,1,128]{3,1,2,0:T(8,128)(2,1)S(1)} %fusion.36), channel_id=1, source_target_pairs={{8,0},{16,8},{24,16},{32,24},{40,32},{48,40},{56,48},{64,56},{72,6... | collective-permute-start | bytes 589832 | tf_op jit(solution)/shard_map/ppermute | solution.py:16
  234.8 12.1 %collective-permute-start.10 = (bf16[2,384,1,128]{3,1,2,0:T(8,128)(2,1)S(1)}, bf16[2,384,1,128]{3,1,2,0:T(8,128)(2,1)S(1)}, u32[]{:S(2)}, u32[]{:S(2)}) collective-permute-start(bf16[2,384,1,128]{3,1,2,0:T(8,128)(2,1)S(1)} %fusion.35), channel_id=1, source_target_pairs={{8,0},{16,8},{24,16},{32,24},{40,32},{48,40},{56,48},{64,56},{72,6... | collective-permute-start | bytes 589832 | tf_op jit(solution)/shard_map/ppermute | solution.py:16
  248.0 11.3 %collective-permute-start.11 = (bf16[2,384,1,128]{3,1,2,0:T(8,128)(2,1)S(1)}, bf16[2,384,1,128]{3,1,2,0:T(8,128)(2,1)S(1)}, u32[]{:S(2)}, u32[]{:S(2)}) collective-permute-start(bf16[2,384,1,128]{3,1,2,0:T(8,128)(2,1)S(1)} %fusion.34), channel_id=1, source_target_pairs={{8,0},{16,8},{24,16},{32,24},{40,32},{48,40},{56,48},{64,56},{72,6... | collective-permute-start | bytes 589832 | tf_op jit(solution)/shard_map/ppermute | solution.py:16
  260.4 10.9 %collective-permute-start.12 = (bf16[2,384,1,128]{3,1,2,0:T(8,128)(2,1)S(1)}, bf16[2,384,1,128]{3,1,2,0:T(8,128)(2,1)S(1)}, u32[]{:S(2)}, u32[]{:S(2)}) collective-permute-start(bf16[2,384,1,128]{3,1,2,0:T(8,128)(2,1)S(1)} %fusion.33), channel_id=1, source_target_pairs={{8,0},{16,8},{24,16},{32,24},{40,32},{48,40},{56,48},{64,56},{72,6... | collective-permute-start | bytes 589832 | tf_op jit(solution)/shard_map/ppermute | solution.py:16
  272.3 10.9 %collective-permute-start.13 = (bf16[2,384,1,128]{3,1,2,0:T(8,128)(2,1)S(1)}, bf16[2,384,1,128]{3,1,2,0:T(8,128)(2,1)S(1)}, u32[]{:S(2)}, u32[]{:S(2)}) collective-permute-start(bf16[2,384,1,128]{3,1,2,0:T(8,128)(2,1)S(1)} %fusion.32), channel_id=1, source_target_pairs={{8,0},{16,8},{24,16},{32,24},{40,32},{48,40},{56,48},{64,56},{72,6... | collective-permute-start | bytes 589832 | tf_op jit(solution)/shard_map/ppermute | solution.py:16
Sparse Core Ops, SparseCore 0:
  10.2 38.9 all-gather.1
where the time goes:
time: 290 us; the launch traced here: 292 us
  waiting for transfers between devices  93.2 us (32%)
  starting transfers between devices  64.6 us (22%)
  local copies, waits for them, and re-layouts  39.8 us (14%)
  other arithmetic  37.3 us (13%)
  matrix products  21.8 us (8%)
  loops' own time  20.8 us (7%)
  between operations  14.4 us (5%)
    ppermute x14, waiting for transfers between devices, passed_along(): return lax.ppermute(block, axis, route)  92.5 us
    ppermute x14, starting transfers between devices, passed_along(): return lax.ppermute(block, axis, route)  64.6 us
    dynamic_slice x16, local copies, waits for them, and re-layouts, on_device(): lax.scan(first_pass, start_pair, (window, offsets))  15.2 us
    another operation x1, loops' own time, on_device(): lax.scan(first_pass, start_pair, (window, offsets))  10.9 us
    another operation x1, loops' own time, on_device(): lax.scan(second_pass, jnp.zeros((row_count, head_count, HD), jnp.float32)...  9.24 us
    reduce_sum x17, other arithmetic, doc_index(): ordered = jnp.sum(picked * doc_lengths[None, :], axis=1, dtype=jnp.int32)  8.99 us
    reduce_or x8, other arithmetic, first_pass(): return (lax.cond(jnp.any(visible), attend, unchanged, state_pair), None)  7.36 us
    reduce_or x8, other arithmetic, second_pass(): return lax.cond(jnp.any(visible), backward, skipped, query_acc)  6.85 us
  transfers between devices with their start and end apart: 15, of which 14 were waited for; matrix products, arithmetic and copies ran while one was open for 11% of the time, Pallas kernels for 0%

commit v1 on v0

v1 whole, which is shorter than its diff:
```python
import functools

import jax
import jax.numpy as jnp
from jax import lax
from jax.experimental import pallas as pl
from jax.experimental.pallas import tpu as pltpu
from jax.sharding import PartitionSpec as P

HD = 128
SOFT_CAP = 50.0
SCORE_SCALE = 1.0 / 12.0
GROUP = 8
LANES = 256
LOG2E = 1.4426950408889634
TANH_SCALE = SCORE_SCALE / SOFT_CAP
EXP_SCALE = SOFT_CAP * LOG2E


def shifted(block, distance):
    count = lax.axis_size("ctx")
    route = [(i, i + distance) for i in range(count) if 0 <= i + distance < count]
    return lax.ppermute(block, "ctx", route)


def document_starts(base, lengths_ref, order_ref, rows, width):
    lane = lax.broadcasted_iota(jnp.int32, (1, width), 1)
    places = base + jnp.where(lane >= rows, lane - rows, lane)
    starts = jnp.zeros((1, width), jnp.int32)
    first = jnp.int32(0)
    bound = jnp.int32(0)
    for i in range(lengths_ref.shape[0]):
        bound = bound + lengths_ref[order_ref[i]]
        starts = jnp.where(bound <= places, bound, starts)
        first = jnp.where(bound <= base, bound, first)
    return starts, first


def transposed_heads(rows_ref, out_ref):
    rows = rows_ref.shape[0]
    for head in range(2):
        out_ref[:, head * rows : (head + 1) * rows] = rows_ref[:, head * HD : (head + 1) * HD].T


def kept(shape, offset, starts, base, rows, diagonal):
    key_row = lax.broadcasted_iota(jnp.int32, shape, 0)
    keep = key_row >= starts - base
    if diagonal:
        lane = lax.broadcasted_iota(jnp.int32, shape, 1) + offset
        keep &= key_row <= jnp.where(lane >= rows, lane - rows, lane)
    return keep


def key_place(base, spot, i, rows):
    return base + (i - spot) * rows - jnp.where(i > spot, GROUP * rows, 0)


def grouped_exchange(blocks):
    count = lax.axis_size("ctx")
    groups = [list(range(g, g + GROUP)) for g in range(0, count, GROUP)]
    return lax.all_to_all(
        blocks, "ctx", split_axis=0, concat_axis=0, axis_index_groups=groups, tiled=True
    )


def dot(a, b):
    return jnp.dot(a, b, preferred_element_type=jnp.float32)


def stats_kernel(
    place_ref, lengths_ref, order_ref, query_ref, window, log_ref, attended_ref, query_t, value_t, starts_ref
):
    rows = query_ref.shape[0]
    width = 2 * rows
    base, spot = place_ref[0], place_ref[1]
    starts, first = document_starts(base, lengths_ref, order_ref, rows, width)
    starts_ref[...] = starts
    transposed_heads(query_ref, query_t)
    log_ref[...] = jnp.zeros_like(log_ref)
    attended_ref[...] = jnp.zeros_like(attended_ref)

    def block(i, diagonal):
        key_base = key_place(base, spot, i, rows)
        value_t[...] = window[i, :, HD:].T
        for c in range(0, width, LANES):
            part = slice(c, c + LANES)
            score = dot(window[i, :, :HD], query_t[:, part])
            expo = jnp.exp2(jnp.tanh(score * TANH_SCALE) * EXP_SCALE)
            keep = kept(expo.shape, c, starts_ref[:, part], key_base, rows, diagonal)
            expo = jnp.where(keep, expo, 0.0)
            log_ref[:, part] += jnp.sum(expo, axis=0, keepdims=True)
            attended_ref[:, part] += dot(value_t[...], expo.astype(jnp.bfloat16))

    block(spot, True)

    def step(j, carry):
        i = lax.rem(spot + j, GROUP)

        @pl.when(key_place(base, spot, i, rows) + rows > first)
        def _():
            block(i, False)

        return carry

    lax.fori_loop(1, GROUP, step, 0)
    attended_ref[...] = attended_ref[...] / log_ref[...]
    log_ref[...] = jnp.log2(log_ref[...])


def grads_kernel(
    place_ref, lengths_ref, order_ref, query_ref, grad_ref, log_ref, attended_ref, window,
    query_grad_ref, own_ref, pieces, query_t, grad_t, query_s, grad_s, key_t, starts_ref, delta_ref, prob_s,
    slope_s, acc,
):
    rows = query_ref.shape[0]
    width = 2 * rows
    base, spot = place_ref[0], place_ref[1]
    starts, first = document_starts(base, lengths_ref, order_ref, rows, width)
    starts_ref[...] = starts
    transposed_heads(query_ref, query_t)
    transposed_heads(grad_ref, grad_t)
    for head in range(2):
        query_s[head * rows : (head + 1) * rows, :] = query_ref[:, head * HD : (head + 1) * HD]
        grad_s[head * rows : (head + 1) * rows, :] = grad_ref[:, head * HD : (head + 1) * HD]
    delta_ref[...] = jnp.sum(
        grad_t[...].astype(jnp.float32) * attended_ref[...], axis=0, keepdims=True
    )
    acc[...] = jnp.zeros_like(acc)

    def block(i, diagonal):
        key_base = key_place(base, spot, i, rows)
        key_t[...] = window[i, :, :HD].T
        for c in range(0, width, LANES):
            part = slice(c, c + LANES)
            score = dot(window[i, :, :HD], query_t[:, part])
            ratio = jnp.tanh(score * TANH_SCALE)
            prob = jnp.exp2(ratio * EXP_SCALE - log_ref[:, part])
            keep = kept(prob.shape, c, starts_ref[:, part], key_base, rows, diagonal)
            prob = jnp.where(keep, prob, 0.0)
            dprob = dot(window[i, :, HD:], grad_t[:, part])
            slope = prob * (dprob - delta_ref[:, part]) * (1.0 - ratio * ratio)
            prob_s[:, part] = prob.astype(jnp.bfloat16)
            slope_s[:, part] = slope.astype(jnp.bfloat16)
        acc[...] += dot(key_t[...], slope_s[...])
        return dot(slope_s[...], query_s[...]) * SCORE_SCALE, dot(prob_s[...], grad_s[...])

    def step(j, carry):
        i = lax.rem(spot + j, GROUP)
        visible = key_place(base, spot, i, rows) + rows > first

        @pl.when(visible)
        def _():
            key_part, value_part = block(i, False)
            pieces[i, :, :HD] = key_part.astype(jnp.bfloat16)
            pieces[i, :, HD:] = value_part.astype(jnp.bfloat16)

        @pl.when(jnp.logical_not(visible))
        def _():
            pieces[i] = jnp.zeros(pieces.shape[1:], jnp.bfloat16)

        return carry

    lax.fori_loop(1, GROUP, step, 0)
    pieces[spot] = jnp.zeros(pieces.shape[1:], jnp.bfloat16)
    key_part, value_part = block(spot, True)
    own_ref[:, :HD] = key_part
    own_ref[:, HD:] = value_part
    for head in range(2):
        query_grad_ref[:, head * HD : (head + 1) * HD] = (
            (acc[:, head * rows : (head + 1) * rows] * SCORE_SCALE).T.astype(jnp.bfloat16)
        )


def smem():
    return pl.BlockSpec(memory_space=pltpu.SMEM)


def vmem():
    return pl.BlockSpec(memory_space=pltpu.VMEM)


def forward_stats(place, doc_lengths, doc_order, query_rows, window):
    rows = query_rows.shape[0]
    width = 2 * rows
    pairs = width * rows * GROUP
    return pl.pallas_call(
        stats_kernel,
        out_shape=(
            jax.ShapeDtypeStruct((1, width), jnp.float32),
            jax.ShapeDtypeStruct((HD, width), jnp.float32),
        ),
        in_specs=[smem()] * 3 + [vmem()] * 2,
        out_specs=(vmem(), vmem()),
        scratch_shapes=[
            pltpu.VMEM((HD, width), jnp.bfloat16),
            pltpu.VMEM((HD, rows), jnp.bfloat16),
            pltpu.VMEM((1, width), jnp.int32),
        ],
        compiler_params=pltpu.CompilerParams(vmem_limit_bytes=32 * 1024 * 1024),
        cost_estimate=pl.CostEstimate(
            flops=4 * pairs * HD, bytes_accessed=4 * 1024 * 1024, transcendentals=2 * pairs
        ),
        name="attention_stats",
    )(place, doc_lengths, doc_order, query_rows, window)


def backward_grads(place, doc_lengths, doc_order, query_rows, head_grads, log_sums, attended, window):
    rows = query_rows.shape[0]
    width = 2 * rows
    pairs = width * rows * GROUP
    return pl.pallas_call(
        grads_kernel,
        out_shape=(
            jax.ShapeDtypeStruct((rows, 2 * HD), jnp.bfloat16),
            jax.ShapeDtypeStruct((rows, 2 * HD), jnp.float32),
            jax.ShapeDtypeStruct((GROUP, rows, 2 * HD), jnp.bfloat16),
        ),
        in_specs=[smem()] * 3 + [vmem()] * 5,
        out_specs=(vmem(),) * 3,
        scratch_shapes=[
            pltpu.VMEM((HD, width), jnp.bfloat16),
            pltpu.VMEM((HD, width), jnp.bfloat16),
            pltpu.VMEM((width, HD), jnp.bfloat16),
            pltpu.VMEM((width, HD), jnp.bfloat16),
            pltpu.VMEM((HD, rows), jnp.bfloat16),
            pltpu.VMEM((1, width), jnp.int32),
            pltpu.VMEM((1, width), jnp.float32),
            pltpu.VMEM((rows, width), jnp.bfloat16),
            pltpu.VMEM((rows, width), jnp.bfloat16),
            pltpu.VMEM((HD, width), jnp.float32),
        ],
        compiler_params=pltpu.CompilerParams(vmem_limit_bytes=32 * 1024 * 1024),
        cost_estimate=pl.CostEstimate(
            flops=10 * pairs * HD, bytes_accessed=8 * 1024 * 1024, transcendentals=2 * pairs
        ),
        name="attention_grads",
    )(place, doc_lengths, doc_order, query_rows, head_grads, log_sums, attended, window)


def on_device(query_rows, key_rows, value_rows, grad_out, out_weight, doc_lengths, doc_order):
    rows = query_rows.shape[0]
    at = lax.axis_index("ctx").astype(jnp.int32)
    spot = lax.rem(at, GROUP)
    place = jnp.stack([at * rows, spot])
    gathered = lax.all_gather(grad_out, "tp", axis=1, tiled=True)
    own_pair = jnp.concatenate([key_rows, value_rows], axis=1)
    before = shifted(own_pair, GROUP)
    slots = jnp.arange(GROUP, dtype=jnp.int32)[:, None, None]
    window = grouped_exchange(jnp.where(slots >= spot, own_pair, before))
    log_sums, attended = forward_stats(place, doc_lengths, doc_order, query_rows, window)
    head_grads = lax.dot_general(
        gathered, out_weight, (((1,), (1,)), ((), ())), preferred_element_type=jnp.float32
    ).astype(jnp.bfloat16)
    query_grads, own, pieces = backward_grads(
        place, doc_lengths, doc_order, query_rows, head_grads, log_sums, attended, window
    )
    returned = grouped_exchange(pieces).astype(jnp.float32)
    for_before = jnp.sum(jnp.where(slots < spot, returned, 0.0), axis=0).astype(jnp.bfloat16)
    own = own + jnp.sum(jnp.where(slots > spot, returned, 0.0), axis=0)
    total = (own + shifted(for_before, -GROUP).astype(jnp.float32)).astype(jnp.bfloat16)
    return query_grads, total[:, :HD], total[:, HD:]


def solution(mesh):
    in_specs = (
        P("ctx", "tp"),
        P("ctx", "tp"),
        P("ctx", "tp"),
        P("ctx", "tp"),
        P("tp", None),
        P(),
        P(),
    )
    out_specs = (P("ctx", "tp"), P("ctx", "tp"), P("ctx", "tp"))
    return jax.shard_map(
        on_device, mesh=mesh, in_specs=in_specs, out_specs=out_specs, check_vma=False
    )
```

time: 290 us -> 125 us (0.43)
  the two profiles are of different devices: /device:TPU:230 before, /device:TPU:64 now
where the time goes in v1:
time: 125 us
  waiting for transfers between devices  63.7 us (51%)
  starting transfers between devices  24 us (19%)
  between operations  14.2 us (11%)
  Pallas kernels  12.7 us (10%)
  local copies, waits for them, and re-layouts  3.69 us (3%)
  other arithmetic  3.63 us (3%)
  matrix products  3.13 us (3%)
    all_to_all x2, waiting for transfers between devices, grouped_exchange(): lax.all_to_all(blocks, 'ctx', split_axis=0, concat_axis=0, axis_index_gro...  41.8 us
    ppermute x2, waiting for transfers between devices, shifted(): return lax.ppermute(block, 'ctx', route)  21.1 us
    all_to_all x2, starting transfers between devices, grouped_exchange(): lax.all_to_all(blocks, 'ctx', split_axis=0, concat_axis=0, axis_index_gro...  15.7 us
    ppermute x2, starting transfers between devices, shifted(): return lax.ppermute(block, 'ctx', route)  8.31 us
    pallas_call x1, Pallas kernels, backward_grads(): pl.pallas_call(grads_kernel, out_shape=(jax.ShapeDtypeStruct((rows, 2 * H...  7.34 us
    pallas_call x1, Pallas kernels, forward_stats(): pl.pallas_call(stats_kernel, out_shape=(jax.ShapeDtypeStruct((1, width),...  5.34 us
    dot_general x1, matrix products, on_device(): lax.dot_general(gathered, out_weight, (((1,), (1,)), ((), ())), preferred...  3.13 us
  transfers between devices with their start and end apart: 5, of which 4 were waited for; matrix products, arithmetic and copies ran while one was open for 3% of the time, Pallas kernels for 4%

profile of v1, /device:TPU:64, one launch (start us, length us, event | category | flops | bytes accessed | tf_op | source)
XLA Modules:
  0.0 125.0 jit_solution(10924016924035351242)
XLA Ops:
  7.2 0.0 copy-start
  7.2 0.0 all-gather.2.cloned.1.call-start
  7.2 0.7 all-gather.2.cloned.1.call-update
  7.9 0.9 constant_dynamic-update-slice_fusion.1
  8.8 0.9 constant_dynamic-update-slice_fusion
  9.8 6.4 %collective-permute-start = (bf16[384,256]{1,0:T(8,128)(2,1)S(1)}, bf16[384,256]{1,0:T(8,128)(2,1)S(1)}, u32[]{:S(2)}, u32[]{:S(2)}) collective-permute-start(bf16[384,256]{1,0:T(8,128)(2,1)S(1)} %constant_dynamic-update-slice_fusion), channel_id=1, source_target_pairs={{0,64},{8,72},{16,80},{24,88},{32,96},{40,104},{48,112},{56,120},{... | collective-permute-start | bytes 589832 | tf_op jit(solution)/shard_map/ppermute | solution.py:23
  16.2 0.0 copy-start.2
  16.2 0.0 copy-start.3
  16.2 0.0 copy-start.4
  16.2 8.3 %collective-permute-done = bf16[384,256]{1,0:T(8,128)(2,1)S(1)} collective-permute-done((bf16[384,256]{1,0:T(8,128)(2,1)S(1)}, bf16[384,256]{1,0:T(8,128)(2,1)S(1)}, u32[]{:S(2)}, u32[]{:S(2)}) %collective-permute-start) | collective-permute-done | bytes 196640 | tf_op jit(solution)/shard_map/ppermute | solution.py:23
  24.5 1.4 %broadcast_select_fusion = bf16[8,384,256]{2,1,0:T(8,128)(2,1)} fusion(pred[8]{0:T(512)(128)(4,1)S(1)} %iota_compare_fusion.2, bf16[384,256]{1,0:T(8,128)(2,1)S(1)} %collective-permute-done, bf16[384,256]{1,0:T(8,128)(2,1)S(1)} %constant_dynamic-update-slice_fusion), kind=kLoop, calls=%fused_computation.4 | loop fusion | flops 786432 | bytes 1966088 | tf_op jit(solution)/shard_map/jit(_where)/select_n | solution.py:249
  25.9 4.3 %all-to-all-start = ((bf16[8,384,256]{2,1,0:T(8,128)(2,1)}), bf16[8,384,256]{2,1,0:T(8,128)(2,1)}, u32[]{:S(2)}, u32[]{:S(2)}) async-start(bf16[8,384,256]{2,1,0:T(8,128)(2,1)} %broadcast_select_fusion), calls=%async_computation | async-start | bytes 3145728 | tf_op jit(solution)/shard_map/all_to_all | solution.py:61
  30.2 0.1 pad_add_fusion.place_ref
  30.3 20.5 %all-to-all-done.window = bf16[8,384,256]{2,1,0:T(8,128)(2,1)} async-done(((bf16[8,384,256]{2,1,0:T(8,128)(2,1)}), bf16[8,384,256]{2,1,0:T(8,128)(2,1)}, u32[]{:S(2)}, u32[]{:S(2)}) %all-to-all-start) | async-done | bytes 1572896 | tf_op jit(solution)/shard_map/all_to_all | solution.py:61
  50.8 0.0 copy-done.2
  50.8 0.0 copy-done.3
  50.8 0.0 copy-done.4
  50.8 5.3 %attention_stats.1 = (f32[1,768]{1,0:T(1,128)S(1)}, f32[128,768]{1,0:T(8,128)S(1)}) custom-call(s32[2]{0:T(128)S(1)} %pad_add_fusion.place_ref, s32[18]{0:T(128)S(1)} %copy-done.3, s32[18]{0:T(128)S(1)} %copy-done.4, bf16[384,256]{1,0:T(8,128)(2,1)S(1)} %copy-done.2, bf16[8,384,256]{2,1,0:T(8,128)(2,1)} %all-to-all-done.window), custom_call_target="tpu_custom_call" | custom-call | flops 1207959552 | bytes 4194304 | tf_op jit(solution)/shard_map/attention_stats/pallas_call | solution.py:186
  56.1 0.0 all-gather.2.cloned.1.call-done
  56.1 0.0 copy-done
  56.1 3.1 %convolution_convert_fusion.grad_ref = bf16[384,256]{1,0:T(8,128)(2,1)S(1)} fusion(bf16[384,4608]{0,1:T(8,128)(2,1)} %all-gather.2.cloned.1.call-done, bf16[256,4608]{1,0:T(8,128)(2,1)S(1)} %copy-done), kind=kOutput, calls=%fused_computation.5 | convolution fusion | flops 906067968 | bytes 6094848 | tf_op jit(solution)/shard_map/dot_general | solution.py:251
  59.3 7.3 %attention_grads.1 = (bf16[384,256]{1,0:T(8,128)(2,1)}, f32[384,256]{1,0:T(8,128)S(1)}, bf16[8,384,256]{2,1,0:T(8,128)(2,1)S(1)}) custom-call(s32[2]{0:T(128)S(1)} %pad_add_fusion.place_ref, s32[18]{0:T(128)S(1)} %copy-done.3, s32[18]{0:T(128)S(1)} %copy-done.4, bf16[384,256]{1,0:T(8,128)(2,1)S(1)} %copy-done.2, ...), custom_call_target="tpu_custom_call" | custom-call | flops 3019898880 | bytes 8388608 | tf_op jit(solution)/shard_map/attention_grads/pallas_call | solution.py:211
  66.6 0.0 copy-start.1
  66.6 1.1 copy-done.1
  67.8 11.4 %all-to-all-start.1 = ((bf16[8,384,256]{2,1,0:T(8,128)(2,1)}), bf16[8,384,256]{2,1,0:T(8,128)(2,1)}, u32[]{:S(2)}, u32[]{:S(2)}) async-start(bf16[8,384,256]{2,1,0:T(8,128)(2,1)} %copy-done.1), calls=%async_computation.1 | async-start | bytes 3145728 | tf_op jit(solution)/shard_map/all_to_all | solution.py:61
  79.2 21.3 %all-to-all-done.1 = bf16[8,384,256]{2,1,0:T(8,128)(2,1)} async-done(((bf16[8,384,256]{2,1,0:T(8,128)(2,1)}), bf16[8,384,256]{2,1,0:T(8,128)(2,1)}, u32[]{:S(2)}, u32[]{:S(2)}) %all-to-all-start.1) | async-done | bytes 1572896 | tf_op jit(solution)/shard_map/all_to_all | solution.py:61
  100.5 2.1 %fusion = (f32[384,256]{1,0:T(8,128)S(1)}, bf16[384,256]{1,0:T(8,128)(2,1)S(1)}) fusion(bf16[8,384,256]{2,1,0:T(8,128)(2,1)} %all-to-all-done.1, pred[8]{0:T(512)(128)(4,1)S(1)} %get-tuple-element.18, pred[8]{0:T(512)(128)(4,1)S(1)} %get-tuple-element.17), kind=kLoop, calls=%fused_computation.2 | loop fusion | flops 3735552 | bytes 2162704 | tf_op jit(solution)/shard_map/reduce_sum | solution.py:259
  102.6 1.9 %collective-permute-start.1 = (bf16[384,256]{1,0:T(8,128)(2,1)S(1)}, bf16[384,256]{1,0:T(8,128)(2,1)S(1)}, u32[]{:S(2)}, u32[]{:S(2)}) collective-permute-start(bf16[384,256]{1,0:T(8,128)(2,1)S(1)} %get-tuple-element.14), channel_id=1, source_target_pairs={{64,0},{72,8},{80,16},{88,24},{96,32},{104,40},{112,48},{120,56},{... | collective-permute-start | bytes 589832 | tf_op jit(solution)/shard_map/ppermute | solution.py:23
  104.5 12.9 %collective-permute-done.1 = bf16[384,256]{1,0:T(8,128)(2,1)S(1)} collective-permute-done((bf16[384,256]{1,0:T(8,128)(2,1)S(1)}, bf16[384,256]{1,0:T(8,128)(2,1)S(1)}, u32[]{:S(2)}, u32[]{:S(2)}) %collective-permute-start.1) | collective-permute-done | bytes 196640 | tf_op jit(solution)/shard_map/ppermute | solution.py:23
  117.4 0.1 add_convert_fusion
  117.4 0.7 fusion.2
  (2 shorter events, 0.0 us)
Async XLA Ops:
  7.2 49.0 %copy-start = (bf16[256,4608]{1,0:T(8,128)(2,1)S(1)}, bf16[256,4608]{1,0:T(8,128)(2,1)}, u32[]{:S(2)}) copy-start(bf16[256,4608]{1,0:T(8,128)(2,1)} %param.11) | copy-start | bytes 7077892
  7.2 48.9 %all-gather.2.cloned.1.call-start = ((), (), s32[]{:S(2)}) async-start(), calls=%async_computation.2 | async-start | bytes 3981312 | tf_op jit(solution)/shard_map/all_gather | solution.py:245
  9.8 14.7 %collective-permute-start = (bf16[384,256]{1,0:T(8,128)(2,1)S(1)}, bf16[384,256]{1,0:T(8,128)(2,1)S(1)}, u32[]{:S(2)}, u32[]{:S(2)}) collective-permute-start(bf16[384,256]{1,0:T(8,128)(2,1)S(1)} %constant_dynamic-update-slice_fusion), channel_id=1, source_target_pairs={{0,64},{8,72},{16,80},{24,88},{32,96},{40,104},{48,112},{56,120},{... | collective-permute-start | bytes 589832 | tf_op jit(solution)/shard_map/ppermute | solution.py:23
  16.2 34.6 %copy-start.2 = (bf16[384,256]{1,0:T(8,128)(2,1)S(1)}, bf16[384,256]{1,0:T(8,128)(2,1)}, u32[]{:S(2)}) copy-start(bf16[384,256]{1,0:T(8,128)(2,1)} %query_ref.3) | copy-start | bytes 589828
  16.2 34.6 %copy-start.3 = (s32[18]{0:T(128)S(1)}, s32[18]{0:T(128)}, u32[]{:S(2)}) copy-start(s32[18]{0:T(128)} %lengths_ref.3) | copy-start | bytes 220
  16.2 34.6 %copy-start.4 = (s32[18]{0:T(128)S(1)}, s32[18]{0:T(128)}, u32[]{:S(2)}) copy-start(s32[18]{0:T(128)} %order_ref.3) | copy-start | bytes 220
  25.9 24.8 %all-to-all-start = ((bf16[8,384,256]{2,1,0:T(8,128)(2,1)}), bf16[8,384,256]{2,1,0:T(8,128)(2,1)}, u32[]{:S(2)}, u32[]{:S(2)}) async-start(bf16[8,384,256]{2,1,0:T(8,128)(2,1)} %broadcast_select_fusion), calls=%async_computation | async-start | bytes 3145728 | tf_op jit(solution)/shard_map/all_to_all | solution.py:61
  66.6 1.1 copy-start.1
  67.8 32.7 %all-to-all-start.1 = ((bf16[8,384,256]{2,1,0:T(8,128)(2,1)}), bf16[8,384,256]{2,1,0:T(8,128)(2,1)}, u32[]{:S(2)}, u32[]{:S(2)}) async-start(bf16[8,384,256]{2,1,0:T(8,128)(2,1)} %copy-done.1), calls=%async_computation.1 | async-start | bytes 3145728 | tf_op jit(solution)/shard_map/all_to_all | solution.py:61
  102.6 14.8 %collective-permute-start.1 = (bf16[384,256]{1,0:T(8,128)(2,1)S(1)}, bf16[384,256]{1,0:T(8,128)(2,1)S(1)}, u32[]{:S(2)}, u32[]{:S(2)}) collective-permute-start(bf16[384,256]{1,0:T(8,128)(2,1)S(1)} %get-tuple-element.14), channel_id=1, source_target_pairs={{64,0},{72,8},{80,16},{88,24},{96,32},{104,40},{112,48},{120,56},{... | collective-permute-start | bytes 589832 | tf_op jit(solution)/shard_map/ppermute | solution.py:23
Sparse Core Ops, SparseCore 0:
  10.1 40.8 all-gather.1

commit v2 on v1

v2 whole, which is shorter than its diff:
```python
import functools

import jax
import jax.numpy as jnp
from jax import lax
from jax.experimental import pallas as pl
from jax.experimental.pallas import tpu as pltpu
from jax.sharding import PartitionSpec as P

HD = 128
SOFT_CAP = 50.0
SCORE_SCALE = 1.0 / 12.0
LANES = 256
LOG2E = 1.4426950408889634
TANH_SCALE = SCORE_SCALE / SOFT_CAP
EXP_SCALE = SOFT_CAP * LOG2E
XS = 4
YS = 4
TASKS = 8
ROW_STEP = 128
VMEM_LIMIT = 48 * 1024 * 1024
HERE, BACK, BACK2, FAR_BACK, FAR = range(5)
SECOND = 5


def permuted(block, axis, target):
    count = lax.axis_size(axis)
    route = [(i, target(i)) for i in range(count) if 0 <= target(i) < count]
    return lax.ppermute(block, axis, route)


def planes_on(block, planes):
    return permuted(block, "ctx", lambda i: i + planes * XS)


def to_query_partner(block):
    return permuted(block, "ctx", lambda i: i ^ 1)


def to_key_partner(block):
    return permuted(block, "ctx", lambda i: i ^ 3)


def to_other_core(block):
    return permuted(block, "tp", lambda i: i ^ 1)


def turned(block, steps):
    return permuted(block, "tp", lambda i: (i + 2 * steps) % (2 * YS))


def dot(a, b):
    return jnp.dot(a, b, preferred_element_type=jnp.float32)


def kept(shape, first_row, offset, starts, key_base, rows, diagonal):
    key_row = lax.broadcasted_iota(jnp.int32, shape, 0) + first_row
    keep = key_row >= starts - key_base
    if diagonal:
        lane = lax.broadcasted_iota(jnp.int32, shape, 1) + offset
        keep &= key_row <= jnp.where(lane >= rows, lane - rows, lane)
    return keep


def load_keys(refs, buffer, semaphores):
    here, back, back2, far = refs
    sources = [here, back, back2, far.at[0], far.at[1]]
    copies = [
        pltpu.make_async_copy(source, buffer.at[i], semaphores.at[i]) for i, source in enumerate(sources)
    ]
    for copy in copies:
        copy.start()
    return copies


def set_queries(base, x, lengths_ref, order_ref, rows, starts_ref):
    width = 2 * rows
    other_base = base + jnp.where(x % 2 == 0, rows, -rows)
    lane = lax.broadcasted_iota(jnp.int32, (1, width), 1)
    lane = jnp.where(lane >= rows, lane - rows, lane)
    bound = jnp.int32(0)
    starts = [jnp.zeros((1, width), jnp.int32)] * 2
    for i in range(lengths_ref.shape[0]):
        bound = bound + lengths_ref[order_ref[i]]
        starts = [
            jnp.where(bound <= place + lane, bound, start) for place, start in zip((base, other_base), starts)
        ]
    starts_ref[:, :width], starts_ref[:, width:] = starts


def task_of(t, base, x, rows):
    even, low = x % 2 == 0, x < 2
    far_base = base + (3 - 2 * x) * rows
    plane = XS * rows
    if t == 0:
        return HERE, base
    if t == 1:
        return jnp.where(even, HERE, BACK2), jnp.where(even, base, base - 2 * plane)
    if t < 4:
        return BACK, base - plane
    if t < 6:
        return FAR_BACK, far_base - plane
    return FAR, jnp.where(low, far_base - 2 * plane, far_base)


def on_lanes(rows_ref, out_ref, at):
    rows = rows_ref.shape[0]
    for head in range(2):
        out_ref[:, at + head * rows : at + (head + 1) * rows] = rows_ref[:, head * HD : (head + 1) * HD].T


def stats_kernel(
    place_ref, lengths_ref, order_ref, query_ref, other_query_ref, here, back, back2, far,
    sums_ref, attended_ref, buffer, query_t, value_t, starts_ref, semaphores,
):
    rows = query_ref.shape[0]
    width = 2 * rows
    copies = load_keys((here, back, back2, far), buffer, semaphores)
    base, x = place_ref[0], place_ref[1]
    set_queries(base, x, lengths_ref, order_ref, rows, starts_ref)
    on_lanes(query_ref, query_t, 0)
    on_lanes(other_query_ref, query_t, width)
    sums_ref[...] = jnp.zeros_like(sums_ref)
    attended_ref[...] = jnp.zeros_like(attended_ref)

    def task(block, key_base, half, diagonal):
        value_t[...] = buffer[block, 1].T
        for c in range(0, width, LANES):
            part = slice(half * width + c, half * width + c + LANES)
            for r in range(0, rows, ROW_STEP):
                score = dot(buffer[block, 0, r : r + ROW_STEP], query_t[:, part])
                expo = jnp.exp2(jnp.tanh(score * TANH_SCALE) * EXP_SCALE)
                keep = kept(expo.shape, r, c, starts_ref[:, part], key_base, rows, diagonal)
                expo = jnp.where(keep, expo, 0.0)
                sums_ref[:, part] += jnp.sum(expo, axis=0, keepdims=True)
                attended_ref[:, part] += dot(value_t[:, r : r + ROW_STEP], expo.astype(jnp.bfloat16))

    for copy in copies:
        copy.wait()
    for t in range(TASKS):
        block, key_base = task_of(t, base, x, rows)
        task(block, key_base, t % 2, t == 0)


def project_kernel(
    place_ref, here, before, after, across_low, across_high, own_weight, other_weight, own_ref, other_ref, across
):
    features = here.shape[0]
    y, core = place_ref[2], place_ref[3]
    across[: features // 2] = across_low[...]
    across[features // 2 :] = across_high[...]
    own = jnp.zeros(own_ref.shape, jnp.float32)
    other = jnp.zeros(own_ref.shape, jnp.float32)
    for steps, block in ((0, here), (YS - 1, before), (1, after), (2, across)):
        at = pl.multiple_of(lax.rem(y + steps, YS) * 2 * features, HD)
        columns = pl.ds(at, 2 * features)

        def of_core(ref):
            return jnp.where(core == 0, ref[:, columns][:, :features], ref[:, columns][:, features:])

        own += dot(of_core(own_weight), block[...])
        other += dot(of_core(other_weight), block[...])
    own_ref[...] = own
    other_ref[...] = other


def delta_kernel(sums_ref, attended_ref, grad_ref, other_grad_ref, out_ref):
    width = attended_ref.shape[1] // 2
    rows = width // 2
    out_ref[0:1, :] = sums_ref[...]
    for i, grads in enumerate((grad_ref, other_grad_ref)):
        for head in range(2):
            at = i * width + head * rows
            lanes = slice(at, at + rows)
            grad = grads[head * HD : (head + 1) * HD, :].astype(jnp.float32)
            out_ref[1:2, lanes] = jnp.sum(grad * attended_ref[:, lanes], axis=0, keepdims=True)
    out_ref[2:, :] = jnp.zeros((6, 2 * width), jnp.float32)


def grads_kernel(
    tasks, slots, place_ref, lengths_ref, order_ref, query_ref, other_query_ref, grad_ref, other_grad_ref,
    stats_ref, other_stats_ref, here, back, back2, far, *refs,
):
    first = FAR in slots
    if first:
        acc, far_ref, refs = refs[0], refs[1], refs[2:]
    else:
        acc_in, query_grad_ref, other_query_grad_ref, here_ref, back_ref, back2_ref, acc, refs = *refs[:7], refs[7:]
    (buffer, query_t, grad_t, query_s, grad_s, key_t, starts_ref, log_ref, delta_ref, prob_s, slope_s, kv_acc,
     semaphores) = refs
    rows = query_ref.shape[0]
    width = 2 * rows
    copies = load_keys((here, back, back2, far), buffer, semaphores)
    base, x = place_ref[0], place_ref[1]
    set_queries(base, x, lengths_ref, order_ref, rows, starts_ref)
    on_lanes(query_ref, query_t, 0)
    on_lanes(other_query_ref, query_t, width)
    for i, (queries, grads) in enumerate(((query_ref, grad_ref), (other_query_ref, other_grad_ref))):
        for head in range(2):
            at = i * width + head * rows
            grad = grads[head * HD : (head + 1) * HD, :]
            grad_t[:, at : at + rows] = grad
            grad_s[at : at + rows, :] = grad.T
            query_s[at : at + rows, :] = queries[:, head * HD : (head + 1) * HD]
        lanes, mirrored = slice(i * width, (i + 1) * width), slice((1 - i) * width, (2 - i) * width)
        total = stats_ref[0:2, lanes] + other_stats_ref[0:2, mirrored]
        log_ref[:, lanes] = jnp.log2(total[0:1])
        delta_ref[:, lanes] = total[1:2] / total[0:1]
    acc[...] = jnp.zeros_like(acc) if first else acc_in[...]
    kv_acc[...] = jnp.zeros_like(kv_acc)

    def pairwise(t):
        block, key_base = task_of(t, base, x, rows)
        half, store = t % 2, t % 2
        key_t[store] = buffer[block, 0].T
        for c in range(0, width, LANES):
            part = slice(half * width + c, half * width + c + LANES)
            score = dot(buffer[block, 0], query_t[:, part])
            ratio = jnp.tanh(score * TANH_SCALE)
            prob = jnp.exp2(ratio * EXP_SCALE - log_ref[:, part])
            keep = kept(prob.shape, 0, c, starts_ref[:, part], key_base, rows, t == 0)
            prob = jnp.where(keep, prob, 0.0)
            dprob = dot(buffer[block, 1], grad_t[:, part])
            slope = prob * (dprob - delta_ref[:, part]) * (1.0 - ratio * ratio)
            prob_s[store, :, c : c + LANES] = prob.astype(jnp.bfloat16)
            slope_s[store, :, c : c + LANES] = slope.astype(jnp.bfloat16)

    def collect(t):
        half, store = t % 2, t % 2
        lanes = slice(half * width, (half + 1) * width)
        out = slots.index((HERE, SECOND, BACK, BACK, FAR_BACK, FAR_BACK, FAR, FAR)[t])
        acc[:, lanes] += dot(key_t[store], slope_s[store])
        kv_acc[out, :, :HD] += dot(slope_s[store], query_s[lanes, :])
        kv_acc[out, :, HD:] += dot(prob_s[store], grad_s[lanes, :])

    for copy in copies:
        copy.wait()
    for t in tasks:
        pairwise(t)
        if t > tasks[0]:
            collect(t - 1)
    collect(tasks[-1])

    def scaled(i):
        return kv_acc[i, :, :HD] * SCORE_SCALE, kv_acc[i, :, HD:]

    if first:
        for i in range(2):
            key_part, value_part = scaled(i)
            far_ref[i, :, :HD] = key_part.astype(jnp.bfloat16)
            far_ref[i, :, HD:] = value_part.astype(jnp.bfloat16)
        return
    even = x % 2 == 0
    back_ref[:, :HD], back_ref[:, HD:] = scaled(slots.index(BACK))
    for i, (own, second) in enumerate(zip(scaled(slots.index(HERE)), scaled(slots.index(SECOND)))):
        here_ref[:, i * HD : (i + 1) * HD] = own + jnp.where(even, second, 0.0)
        back2_ref[:, i * HD : (i + 1) * HD] = jnp.where(even, 0.0, second)
    for head in range(2):
        at = head * rows
        query_grad_ref[:, head * HD : (head + 1) * HD] = (acc[:, at : at + rows] * SCORE_SCALE).T
        at += width
        other_query_grad_ref[:, head * HD : (head + 1) * HD] = (
            (acc[:, at : at + rows] * SCORE_SCALE).T.astype(jnp.bfloat16)
        )


def smem():
    return pl.BlockSpec(memory_space=pltpu.SMEM)


def vmem():
    return pl.BlockSpec(memory_space=pltpu.VMEM)


def hbm():
    return pl.BlockSpec(memory_space=pl.ANY)


def like(shape, dtype):
    return jax.ShapeDtypeStruct(shape, dtype)


def cost(flops, nbytes, transcendentals=0):
    return pl.CostEstimate(flops=flops, bytes_accessed=nbytes, transcendentals=transcendentals)


def params():
    return pltpu.CompilerParams(vmem_limit_bytes=VMEM_LIMIT)


def forward_stats(place, lengths, order, queries, other_queries, keys):
    rows = queries.shape[0]
    width = 2 * rows
    pairs = TASKS * width * rows
    return pl.pallas_call(
        stats_kernel,
        out_shape=(like((1, 2 * width), jnp.float32), like((HD, 2 * width), jnp.float32)),
        in_specs=[smem()] * 3 + [vmem()] * 2 + [hbm()] * 4,
        out_specs=(vmem(),) * 2,
        scratch_shapes=[
            pltpu.VMEM((5, 2, rows, HD), jnp.bfloat16),
            pltpu.VMEM((HD, 2 * width), jnp.bfloat16),
            pltpu.VMEM((HD, rows), jnp.bfloat16),
            pltpu.VMEM((1, 2 * width), jnp.int32),
            pltpu.SemaphoreType.DMA((5,)),
        ],
        compiler_params=params(),
        cost_estimate=cost(4 * pairs * HD, 3_000_000, 2 * pairs),
        name="attention_stats",
    )(place, lengths, order, queries, other_queries, *keys)


def project(place, blocks, own_weight, other_weight):
    heads = own_weight.shape[0]
    features, rows = blocks[0].shape
    return pl.pallas_call(
        project_kernel,
        out_shape=(like((heads, rows), jnp.float32),) * 2,
        in_specs=[smem()] + [vmem()] * 7,
        out_specs=(vmem(),) * 2,
        scratch_shapes=[pltpu.VMEM((features, rows), jnp.bfloat16)],
        compiler_params=params(),
        cost_estimate=cost(4 * YS * heads * rows * features, 5_000_000),
        name="head_projection",
    )(place, *blocks, own_weight, other_weight)


def partial_deltas(sums, attended, grads, other_grads):
    width = attended.shape[1]
    return pl.pallas_call(
        delta_kernel,
        out_shape=like((8, width), jnp.float32),
        in_specs=[vmem()] * 4,
        out_specs=vmem(),
        compiler_params=params(),
        cost_estimate=cost(2 * HD * width, 1_500_000),
        name="partial_deltas",
    )(sums, attended, grads, other_grads)


def backward_grads(place, lengths, order, queries, other_queries, grads, other_grads, stats, other_stats, keys, acc):
    rows = queries.shape[0]
    width = 2 * rows
    first = acc is None
    tasks, slots = ((4, 5, 6, 7), (FAR_BACK, FAR)) if first else ((0, 1, 2, 3), (HERE, SECOND, BACK))
    pairs = len(tasks) * width * rows
    acc_shape = like((HD, 2 * width), jnp.float32)
    block = like((rows, 2 * HD), jnp.float32)
    if first:
        out_shape = (acc_shape, like((2, rows, 2 * HD), jnp.bfloat16))
    else:
        out_shape = (block, like((rows, 2 * HD), jnp.bfloat16), block, block, block)
    return pl.pallas_call(
        functools.partial(grads_kernel, tasks, slots),
        out_shape=out_shape,
        in_specs=[smem()] * 3 + [vmem()] * 6 + [hbm()] * 4 + ([] if first else [vmem()]),
        out_specs=(vmem(),) * len(out_shape),
        scratch_shapes=([] if first else [pltpu.VMEM((HD, 2 * width), jnp.float32)]) + [
            pltpu.VMEM((5, 2, rows, HD), jnp.bfloat16),
            pltpu.VMEM((HD, 2 * width), jnp.bfloat16),
            pltpu.VMEM((HD, 2 * width), jnp.bfloat16),
            pltpu.VMEM((2 * width, HD), jnp.bfloat16),
            pltpu.VMEM((2 * width, HD), jnp.bfloat16),
            pltpu.VMEM((2, HD, rows), jnp.bfloat16),
            pltpu.VMEM((1, 2 * width), jnp.int32),
            pltpu.VMEM((1, 2 * width), jnp.float32),
            pltpu.VMEM((1, 2 * width), jnp.float32),
            pltpu.VMEM((2, rows, width), jnp.bfloat16),
            pltpu.VMEM((2, rows, width), jnp.bfloat16),
            pltpu.VMEM((len(slots), rows, 2 * HD), jnp.float32),
            pltpu.SemaphoreType.DMA((5,)),
        ],
        compiler_params=params(),
        cost_estimate=cost(10 * pairs * HD, 4_000_000, 2 * pairs),
        name="far_grads" if first else "near_grads",
    )(
        place, lengths, order, queries, other_queries, grads, other_grads, stats, other_stats, *keys,
        *(() if first else (acc,)),
    )


def on_device(query_rows, key_rows, value_rows, grad_out, out_weight, doc_lengths, doc_order):
    rows = query_rows.shape[0]
    at = lax.axis_index("ctx").astype(jnp.int32)
    x = lax.rem(at, XS)
    lane = lax.axis_index("tp").astype(jnp.int32)
    core = lax.rem(lane, 2)
    place = jnp.stack([at * rows, x, lane // 2, core])
    features = grad_out.shape[1]

    own = grad_out.T
    before, after = turned(own, 1), turned(own, -1)
    here = jnp.stack([key_rows, value_rows], axis=0)
    back, back2 = planes_on(here, 1), planes_on(here, 2)
    other_queries, other_weight = to_query_partner(query_rows), to_other_core(out_weight)
    before, after, back = lax.optimization_barrier((before, after, back))
    across_low = turned(before[: features // 2], 1)
    across_high = turned(after[features // 2 :], -1)
    far_send = jnp.stack([back, jnp.where(x < 2, here, back2)], axis=0)
    far_send, across_low, across_high = lax.optimization_barrier((far_send, across_low, across_high))
    far = to_key_partner(far_send)
    keys = (here, back, back2, far)

    own_part, other_part = project(
        place, (own, before, after, across_low, across_high), out_weight, other_weight
    )
    grads = (own_part + to_other_core(other_part)).astype(jnp.bfloat16)
    other_grads = to_query_partner(grads)
    sums, attended = forward_stats(place, doc_lengths, doc_order, query_rows, other_queries, keys)
    stats = partial_deltas(sums, attended, grads, other_grads)
    other_stats = to_query_partner(stats)

    common = (
        place, doc_lengths, doc_order, query_rows, other_queries, grads, other_grads, stats, other_stats, keys
    )
    acc, far_grads = backward_grads(*common, None)
    far_grads = to_key_partner(far_grads).astype(jnp.float32)
    query_grads, other_query_grads, here_grads, back_grads, back2_grads = backward_grads(*common, acc)
    other_query_grads = to_query_partner(other_query_grads)
    back2_grads = planes_on(
        (back2_grads + jnp.where(x < 2, 0.0, far_grads[1])).astype(jnp.bfloat16), -2
    )
    back_grads = planes_on((back_grads + far_grads[0]).astype(jnp.bfloat16), -1)
    query_grads = (query_grads + other_query_grads.astype(jnp.float32)).astype(jnp.bfloat16)
    total = here_grads + jnp.where(x < 2, far_grads[1], 0.0)
    total = total + back_grads.astype(jnp.float32) + back2_grads.astype(jnp.float32)
    total = total.astype(jnp.bfloat16)
    return query_grads, total[:, :HD], total[:, HD:]


def solution(mesh):
    in_specs = (
        P("ctx", "tp"),
        P("ctx", "tp"),
        P("ctx", "tp"),
        P("ctx", "tp"),
        P("tp", None),
        P(),
        P(),
    )
    out_specs = (P("ctx", "tp"), P("ctx", "tp"), P("ctx", "tp"))
    return jax.shard_map(
        on_device, mesh=mesh, in_specs=in_specs, out_specs=out_specs, check_vma=False
    )
```

time: 125 us -> 107 us (0.86)
  the two profiles are of different devices: /device:TPU:64 before, /device:TPU:248 now
where the time goes in v2:
time: 107 us; the launch traced here: 106 us
  starting transfers between devices  43.8 us (41%)
  waiting for transfers between devices  34.5 us (32%)
  Pallas kernels  20.9 us (20%)
  other arithmetic  4.07 us (4%)
  local copies, waits for them, and re-layouts  1.77 us (2%)
    ppermute x16, starting transfers between devices, permuted(): return lax.ppermute(block, axis, route)  43.8 us
    ppermute x16, waiting for transfers between devices, permuted(): return lax.ppermute(block, axis, route)  34.5 us
    pallas_call x2, Pallas kernels, backward_grads(): pl.pallas_call(functools.partial(grads_kernel, tasks, slots), out_shape=o...  11.8 us
    pallas_call x1, Pallas kernels, forward_stats(): pl.pallas_call(stats_kernel, out_shape=(like((1, 2 * width), jnp.float32)...  5.45 us
    pallas_call x1, Pallas kernels, project(): pl.pallas_call(project_kernel, out_shape=(like((heads, rows), jnp.float32...  3.52 us
  transfers between devices with their start and end apart: 16, of which 8 were waited for; matrix products, arithmetic and copies ran while one was open for 4% of the time, Pallas kernels for 11%

profile of v2, /device:TPU:248, one launch (start us, length us, event | category | flops | bytes accessed | tf_op | source)
XLA Modules:
  0.0 106.0 jit_solution(14668976759119542516)
XLA Ops:
  0.6 2.1 %collective-permute-start.7 = (bf16[256,4608]{1,0:T(8,128)(2,1)}, bf16[256,4608]{1,0:T(8,128)(2,1)}, u32[]{:S(2)}, u32[]{:S(2)}) collective-permute-start(bf16[256,4608]{1,0:T(8,128)(2,1)} %own_weight.1), channel_id=1, source_target_pairs={{0,1},{1,0},{2,3},{3,2},{4,5},{5,4},{6,7},{7,6},{8,9},{9,8},{10,11... | collective-permute-start | bytes 7077896 | tf_op jit(solution)/shard_map/ppermute | solution.py:29
  2.7 2.1 %collective-permute-start.1 = (bf16[576,384]{1,0:T(8,128)(2,1)}, bf16[576,384]{1,0:T(8,128)(2,1)S(1)}, u32[]{:S(2)}, u32[]{:S(2)}) collective-permute-start(bf16[576,384]{1,0:T(8,128)(2,1)} %bitcast.28), channel_id=1, source_target_pairs={{0,2},{1,3},{2,4},{3,5},{4,6},{5,7},{6,0},{7,1},{8,10},{9,11},{10,... | collective-permute-start | bytes 1327112 | tf_op jit(solution)/shard_map/ppermute | solution.py:29
  4.8 3.7 %collective-permute-start.2 = (bf16[576,384]{1,0:T(8,128)(2,1)}, bf16[576,384]{1,0:T(8,128)(2,1)S(1)}, u32[]{:S(2)}, u32[]{:S(2)}) collective-permute-start(bf16[576,384]{1,0:T(8,128)(2,1)} %bitcast.29), channel_id=1, source_target_pairs={{0,6},{1,7},{2,0},{3,1},{4,2},{5,3},{6,4},{7,5},{8,14},{9,15},{10,... | collective-permute-start | bytes 1327112 | tf_op jit(solution)/shard_map/ppermute | solution.py:29
  8.6 1.0 pad_maximum_fusion.1.here
  9.5 5.0 %collective-permute-start.3 = (bf16[2,384,128]{2,1,0:T(8,128)(2,1)S(1)}, bf16[2,384,128]{2,1,0:T(8,128)(2,1)}, u32[]{:S(2)}, u32[]{:S(2)}) collective-permute-start(bf16[2,384,128]{2,1,0:T(8,128)(2,1)S(1)} %pad_maximum_fusion.1.here), channel_id=1, source_target_pairs={{0,32},{8,40},{16,48},{24,56},{32,64},{40,72},{48,80},{56,88},{64,... | collective-permute-start | bytes 589832 | tf_op jit(solution)/shard_map/ppermute | solution.py:29
  14.6 3.4 %collective-permute-start.4 = (bf16[2,384,128]{2,1,0:T(8,128)(2,1)S(1)}, bf16[2,384,128]{2,1,0:T(8,128)(2,1)}, u32[]{:S(2)}, u32[]{:S(2)}) collective-permute-start(bf16[2,384,128]{2,1,0:T(8,128)(2,1)S(1)} %pad_maximum_fusion.1.here), channel_id=1, source_target_pairs={{0,64},{8,72},{16,80},{24,88},{32,96},{40,104},{48,112},{56,120},{... | collective-permute-start | bytes 589832 | tf_op jit(solution)/shard_map/ppermute | solution.py:29
  18.0 0.1 pad_add_fusion.place_ref
  18.1 4.3 %collective-permute-done.3.back = bf16[2,384,128]{2,1,0:T(8,128)(2,1)} collective-permute-done((bf16[2,384,128]{2,1,0:T(8,128)(2,1)S(1)}, bf16[2,384,128]{2,1,0:T(8,128)(2,1)}, u32[]{:S(2)}, u32[]{:S(2)}) %collective-permute-start.3) | collective-permute-done | bytes 196640 | tf_op jit(solution)/shard_map/ppermute | solution.py:29
  22.3 0.0 collective-permute-done.1.before
  22.3 0.0 collective-permute-done.2.after
  22.4 4.3 %collective-permute-start.5 = (bf16[288,384]{1,0:T(8,128)(2,1)S(1)}, bf16[288,384]{1,0:T(8,128)(2,1)S(1)}, u32[]{:S(2)}, u32[]{:S(2)}) collective-permute-start(bf16[288,384]{1,0:T(8,128)(2,1)S(1)} %slice.19), channel_id=1, source_target_pairs={{0,2},{1,3},{2,4},{3,5},{4,6},{5,7},{6,0},{7,1},{8,10},{9,11},{10,... | collective-permute-start | bytes 663560 | tf_op jit(solution)/shard_map/ppermute | solution.py:29
  26.7 1.9 %collective-permute-start.6 = (bf16[288,384]{1,0:T(8,128)(2,1)S(1)}, bf16[288,384]{1,0:T(8,128)(2,1)S(1)}, u32[]{:S(2)}, u32[]{:S(2)}) collective-permute-start(bf16[288,384]{1,0:T(8,128)(2,1)S(1)} %slice.20), channel_id=1, source_target_pairs={{0,6},{1,7},{2,0},{3,1},{4,2},{5,3},{6,4},{7,5},{8,14},{9,15},{10,... | collective-permute-start | bytes 663560 | tf_op jit(solution)/shard_map/ppermute | solution.py:29
  28.6 0.0 collective-permute-done.4.back2
  28.6 1.0 select_bitcast_fusion
  29.6 0.0 copy-start.2
  29.6 0.0 copy-start.3
  29.6 0.0 copy-start.4
  29.7 1.0 pad_maximum_fusion
  30.7 5.1 %collective-permute-done.6.across_high = bf16[288,384]{1,0:T(8,128)(2,1)S(1)} collective-permute-done((bf16[288,384]{1,0:T(8,128)(2,1)S(1)}, bf16[288,384]{1,0:T(8,128)(2,1)S(1)}, u32[]{:S(2)}, u32[]{:S(2)}) %collective-permute-start.6) | collective-permute-done | bytes 221216 | tf_op jit(solution)/shard_map/ppermute | solution.py:29
  35.7 0.0 collective-permute-done.7.other_weight
  35.7 1.0 copy-done.1
  36.8 3.5 %head_projection.1 = (f32[256,384]{1,0:T(8,128)S(1)}, f32[256,384]{1,0:T(8,128)S(1)}) custom-call(s32[4]{0:T(128)S(1)} %pad_add_fusion.place_ref, bf16[576,384]{1,0:T(8,128)(2,1)S(1)} %bitcast.30, bf16[576,384]{1,0:T(8,128)(2,1)S(1)} %collective-permute-done.1.before, bf16[576,384]{1,0:T(8,128)(2,1)S(1)} %collective-permute-done.2.after, ...), custom_call_target="tpu_custom_call" | custom-call | flops 905969664 | bytes 5000000 | tf_op jit(solution)/shard_map/head_projection/pallas_call | solution.py:316
  40.3 1.9 %collective-permute-start.8 = (f32[256,384]{1,0:T(8,128)S(1)}, f32[256,384]{1,0:T(8,128)S(1)}, u32[]{:S(2)}, u32[]{:S(2)}) collective-permute-start(f32[256,384]{1,0:T(8,128)S(1)} %get-tuple-element.26), channel_id=1, source_target_pairs={{0,1},{1,0},{2,3},{3,2},{4,5},{5,4},{6,7},{7,6},{8,9},{9,8},{10,11... | collective-permute-start | bytes 1179656 | tf_op jit(solution)/shard_map/ppermute | solution.py:29
  42.2 2.8 %collective-permute-start.10 = (bf16[2,2,384,128]{3,2,1,0:T(8,128)(2,1)S(1)}, bf16[2,2,384,128]{3,2,1,0:T(8,128)(2,1)S(1)}, u32[]{:S(2)}, u32[]{:S(2)}) collective-permute-start(bf16[2,2,384,128]{3,2,1,0:T(8,128)(2,1)S(1)} %pad_maximum_fusion), channel_id=1, source_target_pairs={{0,24},{8,16},{16,8},{24,0},{32,56},{40,48},{48,40},{56,32},{64,88... | collective-permute-start | bytes 1179656 | tf_op jit(solution)/shard_map/ppermute | solution.py:29
  45.1 2.1 %collective-permute-start = (bf16[384,256]{1,0:T(8,128)(2,1)S(1)}, bf16[384,256]{1,0:T(8,128)(2,1)S(1)}, u32[]{:S(2)}, u32[]{:S(2)}) collective-permute-start(bf16[384,256]{1,0:T(8,128)(2,1)S(1)} %copy-done.2), channel_id=1, source_target_pairs={{0,8},{8,0},{16,24},{24,16},{32,40},{40,32},{48,56},{56,48},{64,72... | collective-permute-start | bytes 589832 | tf_op jit(solution)/shard_map/ppermute | solution.py:29
  47.2 0.0 collective-permute-done.8
  47.3 3.7 %collective-permute-start.9 = (bf16[256,384]{1,0:T(8,128)(2,1)S(1)}, bf16[256,384]{1,0:T(8,128)(2,1)S(1)}, u32[]{:S(2)}, u32[]{:S(2)}) collective-permute-start(bf16[256,384]{1,0:T(8,128)(2,1)S(1)} %add_convert_fusion.1.grad_ref), channel_id=1, source_target_pairs={{0,8},{8,0},{16,24},{24,16},{32,40},{40,32},{48,56},{56,48},{64,72... | collective-permute-start | bytes 589832 | tf_op jit(solution)/shard_map/ppermute | solution.py:29
  51.0 3.7 %collective-permute-done.other_query_ref = bf16[384,256]{1,0:T(8,128)(2,1)S(1)} collective-permute-done((bf16[384,256]{1,0:T(8,128)(2,1)S(1)}, bf16[384,256]{1,0:T(8,128)(2,1)S(1)}, u32[]{:S(2)}, u32[]{:S(2)}) %collective-permute-start) | collective-permute-done | bytes 196640 | tf_op jit(solution)/shard_map/ppermute | solution.py:29
  54.7 2.1 %collective-permute-done.10.far = bf16[2,2,384,128]{3,2,1,0:T(8,128)(2,1)S(1)} collective-permute-done((bf16[2,2,384,128]{3,2,1,0:T(8,128)(2,1)S(1)}, bf16[2,2,384,128]{3,2,1,0:T(8,128)(2,1)S(1)}, u32[]{:S(2)}, u32[]{:S(2)}) %collective-permute-start.10) | collective-permute-done | bytes 393248 | tf_op jit(solution)/shard_map/ppermute | solution.py:29
  56.8 5.4 %attention_stats.1 = (f32[1,1536]{1,0:T(1,128)S(1)}, f32[128,1536]{1,0:T(8,128)S(1)}) custom-call(s32[4]{0:T(128)S(1)} %pad_add_fusion.place_ref, s32[18]{0:T(128)S(1)} %copy-done.3, s32[18]{0:T(128)S(1)} %copy-done.4, bf16[384,256]{1,0:T(8,128)(2,1)S(1)} %copy-done.2, bf16[384,256]{1,0:T(8,128)(2,1)S(1)} %collective-permute-done.other_query_ref, ...), custom_call_target="tpu_custom_call" | custom-call | flops 1207959552 | bytes 3000000 | tf_op jit(solution)/shard_map/attention_stats/pallas_call | solution.py:295
  62.3 0.0 collective-permute-done.9.other_grad_ref
  62.3 0.1 partial_deltas.1.stats_ref
  62.4 1.9 %collective-permute-start.11 = (f32[8,1536]{1,0:T(8,128)S(1)}, f32[8,1536]{1,0:T(8,128)S(1)}, u32[]{:S(2)}, u32[]{:S(2)}) collective-permute-start(f32[8,1536]{1,0:T(8,128)S(1)} %partial_deltas.1.stats_ref), channel_id=1, source_target_pairs={{0,8},{8,0},{16,24},{24,16},{32,40},{40,32},{48,56},{56,48},{64,72... | collective-permute-start | bytes 147464 | tf_op jit(solution)/shard_map/ppermute | solution.py:29
  64.4 4.1 %collective-permute-done.11.other_stats_ref = f32[8,1536]{1,0:T(8,128)S(1)} collective-permute-done((f32[8,1536]{1,0:T(8,128)S(1)}, f32[8,1536]{1,0:T(8,128)S(1)}, u32[]{:S(2)}, u32[]{:S(2)}) %collective-permute-start.11) | collective-permute-done | bytes 49184 | tf_op jit(solution)/shard_map/ppermute | solution.py:29
  68.4 5.9 %far_grads.1 = (f32[128,1536]{1,0:T(8,128)S(1)}, bf16[2,384,256]{2,1,0:T(8,128)(2,1)S(1)}) custom-call(s32[4]{0:T(128)S(1)} %pad_add_fusion.place_ref, s32[18]{0:T(128)S(1)} %copy-done.3, s32[18]{0:T(128)S(1)} %copy-done.4, bf16[384,256]{1,0:T(8,128)(2,1)S(1)} %copy-done.2, bf16[384,256]{1,0:T(8,128)(2,1)S(1)} %collective-permute-done.other_query_ref, ...), custom_call_target="tpu_custom_call" | custom-call | flops 1509949440 | bytes 4000000 | tf_op jit(solution)/shard_map/far_grads/pallas_call | solution.py:353
  74.3 3.0 %collective-permute-start.13 = (bf16[2,384,256]{2,1,0:T(8,128)(2,1)S(1)}, bf16[2,384,256]{2,1,0:T(8,128)(2,1)S(1)}, u32[]{:S(2)}, u32[]{:S(2)}) collective-permute-start(bf16[2,384,256]{2,1,0:T(8,128)(2,1)S(1)} %get-tuple-element.34), channel_id=1, source_target_pairs={{0,24},{8,16},{16,8},{24,0},{32,56},{40,48},{48,40},{56,32},{64,88... | collective-permute-start | bytes 1179656 | tf_op jit(solution)/shard_map/ppermute | solution.py:29
  77.4 5.9 %near_grads.1 = (f32[384,256]{1,0:T(8,128)S(1)}, bf16[384,256]{1,0:T(8,128)(2,1)S(1)}, f32[384,256]{1,0:T(8,128)S(1)}, f32[384,256]{1,0:T(8,128)S(1)}, f32[384,256]{1,0:T(8,128)S(1)}) custom-call(s32[4]{0:T(128)S(1)} %pad_add_fusion.place_ref, s32[18]{0:T(128)S(1)} %copy-done.3, s32[18]{0:T(128)S(1)} %copy-done.4, bf16[384,256]{1,0:T(8,128)(2,1)S(1)} %copy-done.2, ...), custom_call_target="tpu_custom_call" | custom-call | flops 1509949440 | bytes 4000000 | tf_op jit(solution)/shard_map/near_grads/pallas_call | solution.py:353
  83.3 1.9 %collective-permute-start.12 = (bf16[384,256]{1,0:T(8,128)(2,1)S(1)}, bf16[384,256]{1,0:T(8,128)(2,1)S(1)}, u32[]{:S(2)}, u32[]{:S(2)}) collective-permute-start(bf16[384,256]{1,0:T(8,128)(2,1)S(1)} %get-tuple-element.32), channel_id=1, source_target_pairs={{0,8},{8,0},{16,24},{24,16},{32,40},{40,32},{48,56},{56,48},{64,72... | collective-permute-start | bytes 589832 | tf_op jit(solution)/shard_map/ppermute | solution.py:29
  85.2 1.8 %collective-permute-done.13 = bf16[2,384,256]{2,1,0:T(8,128)(2,1)S(1)} collective-permute-done((bf16[2,384,256]{2,1,0:T(8,128)(2,1)S(1)}, bf16[2,384,256]{2,1,0:T(8,128)(2,1)S(1)}, u32[]{:S(2)}, u32[]{:S(2)}) %collective-permute-start.13) | collective-permute-done | bytes 393248 | tf_op jit(solution)/shard_map/ppermute | solution.py:29
  87.0 0.1 convert_element_type.30
  87.1 0.1 fusion.1
  87.2 1.9 %collective-permute-start.14 = (bf16[384,256]{1,0:T(8,128)(2,1)S(1)}, bf16[384,256]{1,0:T(8,128)(2,1)S(1)}, u32[]{:S(2)}, u32[]{:S(2)}) collective-permute-start(bf16[384,256]{1,0:T(8,128)(2,1)S(1)} %get-tuple-element.37), channel_id=1, source_target_pairs={{32,0},{40,8},{48,16},{56,24},{64,32},{72,40},{80,48},{88,56},{96,... | collective-permute-start | bytes 589832 | tf_op jit(solution)/shard_map/ppermute | solution.py:29
  89.1 1.9 %collective-permute-start.15 = (bf16[384,256]{1,0:T(8,128)(2,1)S(1)}, bf16[384,256]{1,0:T(8,128)(2,1)S(1)}, u32[]{:S(2)}, u32[]{:S(2)}) collective-permute-start(bf16[384,256]{1,0:T(8,128)(2,1)S(1)} %get-tuple-element.38), channel_id=1, source_target_pairs={{64,0},{72,8},{80,16},{88,24},{96,32},{104,40},{112,48},{120,56},{... | collective-permute-start | bytes 589832 | tf_op jit(solution)/shard_map/ppermute | solution.py:29
  91.1 0.7 add_convert_fusion
  91.8 8.0 %collective-permute-done.14 = bf16[384,256]{1,0:T(8,128)(2,1)S(1)} collective-permute-done((bf16[384,256]{1,0:T(8,128)(2,1)S(1)}, bf16[384,256]{1,0:T(8,128)(2,1)S(1)}, u32[]{:S(2)}, u32[]{:S(2)}) %collective-permute-start.14) | collective-permute-done | bytes 196640 | tf_op jit(solution)/shard_map/ppermute | solution.py:29
  99.8 5.4 %collective-permute-done.15 = bf16[384,256]{1,0:T(8,128)(2,1)S(1)} collective-permute-done((bf16[384,256]{1,0:T(8,128)(2,1)S(1)}, bf16[384,256]{1,0:T(8,128)(2,1)S(1)}, u32[]{:S(2)}, u32[]{:S(2)}) %collective-permute-start.15) | collective-permute-done | bytes 196640 | tf_op jit(solution)/shard_map/ppermute | solution.py:29
  105.2 0.1 fusion.5
  105.3 0.7 fusion.6
  (11 shorter events, 0.1 us)
Async XLA Ops:
  0.6 35.1 %copy-start = (bf16[256,4608]{1,0:T(8,128)(2,1)S(1)}, bf16[256,4608]{1,0:T(8,128)(2,1)}, u32[]{:S(2)}) copy-start(bf16[256,4608]{1,0:T(8,128)(2,1)} %own_weight.1) | copy-start | bytes 7077892
  0.6 35.1 %collective-permute-start.7 = (bf16[256,4608]{1,0:T(8,128)(2,1)}, bf16[256,4608]{1,0:T(8,128)(2,1)}, u32[]{:S(2)}, u32[]{:S(2)}) collective-permute-start(bf16[256,4608]{1,0:T(8,128)(2,1)} %own_weight.1), channel_id=1, source_target_pairs={{0,1},{1,0},{2,3},{3,2},{4,5},{5,4},{6,7},{7,6},{8,9},{9,8},{10,11... | collective-permute-start | bytes 7077896 | tf_op jit(solution)/shard_map/ppermute | solution.py:29
  2.7 19.6 %collective-permute-start.1 = (bf16[576,384]{1,0:T(8,128)(2,1)}, bf16[576,384]{1,0:T(8,128)(2,1)S(1)}, u32[]{:S(2)}, u32[]{:S(2)}) collective-permute-start(bf16[576,384]{1,0:T(8,128)(2,1)} %bitcast.28), channel_id=1, source_target_pairs={{0,2},{1,3},{2,4},{3,5},{4,6},{5,7},{6,0},{7,1},{8,10},{9,11},{10,... | collective-permute-start | bytes 1327112 | tf_op jit(solution)/shard_map/ppermute | solution.py:29
  4.8 17.5 %collective-permute-start.2 = (bf16[576,384]{1,0:T(8,128)(2,1)}, bf16[576,384]{1,0:T(8,128)(2,1)S(1)}, u32[]{:S(2)}, u32[]{:S(2)}) collective-permute-start(bf16[576,384]{1,0:T(8,128)(2,1)} %bitcast.29), channel_id=1, source_target_pairs={{0,6},{1,7},{2,0},{3,1},{4,2},{5,3},{6,4},{7,5},{8,14},{9,15},{10,... | collective-permute-start | bytes 1327112 | tf_op jit(solution)/shard_map/ppermute | solution.py:29
  9.5 12.8 %collective-permute-start.3 = (bf16[2,384,128]{2,1,0:T(8,128)(2,1)S(1)}, bf16[2,384,128]{2,1,0:T(8,128)(2,1)}, u32[]{:S(2)}, u32[]{:S(2)}) collective-permute-start(bf16[2,384,128]{2,1,0:T(8,128)(2,1)S(1)} %pad_maximum_fusion.1.here), channel_id=1, source_target_pairs={{0,32},{8,40},{16,48},{24,56},{32,64},{40,72},{48,80},{56,88},{64,... | collective-permute-start | bytes 589832 | tf_op jit(solution)/shard_map/ppermute | solution.py:29
  14.6 14.1 %collective-permute-start.4 = (bf16[2,384,128]{2,1,0:T(8,128)(2,1)S(1)}, bf16[2,384,128]{2,1,0:T(8,128)(2,1)}, u32[]{:S(2)}, u32[]{:S(2)}) collective-permute-start(bf16[2,384,128]{2,1,0:T(8,128)(2,1)S(1)} %pad_maximum_fusion.1.here), channel_id=1, source_target_pairs={{0,64},{8,72},{16,80},{24,88},{32,96},{40,104},{48,112},{56,120},{... | collective-permute-start | bytes 589832 | tf_op jit(solution)/shard_map/ppermute | solution.py:29
  22.4 8.3 %collective-permute-start.5 = (bf16[288,384]{1,0:T(8,128)(2,1)S(1)}, bf16[288,384]{1,0:T(8,128)(2,1)S(1)}, u32[]{:S(2)}, u32[]{:S(2)}) collective-permute-start(bf16[288,384]{1,0:T(8,128)(2,1)S(1)} %slice.19), channel_id=1, source_target_pairs={{0,2},{1,3},{2,4},{3,5},{4,6},{5,7},{6,0},{7,1},{8,10},{9,11},{10,... | collective-permute-start | bytes 663560 | tf_op jit(solution)/shard_map/ppermute | solution.py:29
  26.7 9.0 %collective-permute-start.6 = (bf16[288,384]{1,0:T(8,128)(2,1)S(1)}, bf16[288,384]{1,0:T(8,128)(2,1)S(1)}, u32[]{:S(2)}, u32[]{:S(2)}) collective-permute-start(bf16[288,384]{1,0:T(8,128)(2,1)S(1)} %slice.20), channel_id=1, source_target_pairs={{0,6},{1,7},{2,0},{3,1},{4,2},{5,3},{6,4},{7,5},{8,14},{9,15},{10,... | collective-permute-start | bytes 663560 | tf_op jit(solution)/shard_map/ppermute | solution.py:29
  29.6 15.4 %copy-start.2 = (bf16[384,256]{1,0:T(8,128)(2,1)S(1)}, bf16[384,256]{1,0:T(8,128)(2,1)}, u32[]{:S(2)}) copy-start(bf16[384,256]{1,0:T(8,128)(2,1)} %query_ref.5) | copy-start | bytes 589828
  29.6 27.2 %copy-start.3 = (s32[18]{0:T(128)S(1)}, s32[18]{0:T(128)}, u32[]{:S(2)}) copy-start(s32[18]{0:T(128)} %lengths_ref.5) | copy-start | bytes 220
  29.6 27.2 %copy-start.4 = (s32[18]{0:T(128)S(1)}, s32[18]{0:T(128)}, u32[]{:S(2)}) copy-start(s32[18]{0:T(128)} %order_ref.5) | copy-start | bytes 220
  35.7 1.0 copy-start.1
  40.3 6.9 %collective-permute-start.8 = (f32[256,384]{1,0:T(8,128)S(1)}, f32[256,384]{1,0:T(8,128)S(1)}, u32[]{:S(2)}, u32[]{:S(2)}) collective-permute-start(f32[256,384]{1,0:T(8,128)S(1)} %get-tuple-element.26), channel_id=1, source_target_pairs={{0,1},{1,0},{2,3},{3,2},{4,5},{5,4},{6,7},{7,6},{8,9},{9,8},{10,11... | collective-permute-start | bytes 1179656 | tf_op jit(solution)/shard_map/ppermute | solution.py:29
  42.2 14.6 %collective-permute-start.10 = (bf16[2,2,384,128]{3,2,1,0:T(8,128)(2,1)S(1)}, bf16[2,2,384,128]{3,2,1,0:T(8,128)(2,1)S(1)}, u32[]{:S(2)}, u32[]{:S(2)}) collective-permute-start(bf16[2,2,384,128]{3,2,1,0:T(8,128)(2,1)S(1)} %pad_maximum_fusion), channel_id=1, source_target_pairs={{0,24},{8,16},{16,8},{24,0},{32,56},{40,48},{48,40},{56,32},{64,88... | collective-permute-start | bytes 1179656 | tf_op jit(solution)/shard_map/ppermute | solution.py:29
  45.1 9.6 %collective-permute-start = (bf16[384,256]{1,0:T(8,128)(2,1)S(1)}, bf16[384,256]{1,0:T(8,128)(2,1)S(1)}, u32[]{:S(2)}, u32[]{:S(2)}) collective-permute-start(bf16[384,256]{1,0:T(8,128)(2,1)S(1)} %copy-done.2), channel_id=1, source_target_pairs={{0,8},{8,0},{16,24},{24,16},{32,40},{40,32},{48,56},{56,48},{64,72... | collective-permute-start | bytes 589832 | tf_op jit(solution)/shard_map/ppermute | solution.py:29
  47.3 15.0 %collective-permute-start.9 = (bf16[256,384]{1,0:T(8,128)(2,1)S(1)}, bf16[256,384]{1,0:T(8,128)(2,1)S(1)}, u32[]{:S(2)}, u32[]{:S(2)}) collective-permute-start(bf16[256,384]{1,0:T(8,128)(2,1)S(1)} %add_convert_fusion.1.grad_ref), channel_id=1, source_target_pairs={{0,8},{8,0},{16,24},{24,16},{32,40},{40,32},{48,56},{56,48},{64,72... | collective-permute-start | bytes 589832 | tf_op jit(solution)/shard_map/ppermute | solution.py:29
  62.4 6.0 %collective-permute-start.11 = (f32[8,1536]{1,0:T(8,128)S(1)}, f32[8,1536]{1,0:T(8,128)S(1)}, u32[]{:S(2)}, u32[]{:S(2)}) collective-permute-start(f32[8,1536]{1,0:T(8,128)S(1)} %partial_deltas.1.stats_ref), channel_id=1, source_target_pairs={{0,8},{8,0},{16,24},{24,16},{32,40},{40,32},{48,56},{56,48},{64,72... | collective-permute-start | bytes 147464 | tf_op jit(solution)/shard_map/ppermute | solution.py:29
  74.3 12.7 %collective-permute-start.13 = (bf16[2,384,256]{2,1,0:T(8,128)(2,1)S(1)}, bf16[2,384,256]{2,1,0:T(8,128)(2,1)S(1)}, u32[]{:S(2)}, u32[]{:S(2)}) collective-permute-start(bf16[2,384,256]{2,1,0:T(8,128)(2,1)S(1)} %get-tuple-element.34), channel_id=1, source_target_pairs={{0,24},{8,16},{16,8},{24,0},{32,56},{40,48},{48,40},{56,32},{64,88... | collective-permute-start | bytes 1179656 | tf_op jit(solution)/shard_map/ppermute | solution.py:29
  83.3 7.8 %collective-permute-start.12 = (bf16[384,256]{1,0:T(8,128)(2,1)S(1)}, bf16[384,256]{1,0:T(8,128)(2,1)S(1)}, u32[]{:S(2)}, u32[]{:S(2)}) collective-permute-start(bf16[384,256]{1,0:T(8,128)(2,1)S(1)} %get-tuple-element.32), channel_id=1, source_target_pairs={{0,8},{8,0},{16,24},{24,16},{32,40},{40,32},{48,56},{56,48},{64,72... | collective-permute-start | bytes 589832 | tf_op jit(solution)/shard_map/ppermute | solution.py:29
  87.2 12.6 %collective-permute-start.14 = (bf16[384,256]{1,0:T(8,128)(2,1)S(1)}, bf16[384,256]{1,0:T(8,128)(2,1)S(1)}, u32[]{:S(2)}, u32[]{:S(2)}) collective-permute-start(bf16[384,256]{1,0:T(8,128)(2,1)S(1)} %get-tuple-element.37), channel_id=1, source_target_pairs={{32,0},{40,8},{48,16},{56,24},{64,32},{72,40},{80,48},{88,56},{96,... | collective-permute-start | bytes 589832 | tf_op jit(solution)/shard_map/ppermute | solution.py:29
  89.1 16.1 %collective-permute-start.15 = (bf16[384,256]{1,0:T(8,128)(2,1)S(1)}, bf16[384,256]{1,0:T(8,128)(2,1)S(1)}, u32[]{:S(2)}, u32[]{:S(2)}) collective-permute-start(bf16[384,256]{1,0:T(8,128)(2,1)S(1)} %get-tuple-element.38), channel_id=1, source_target_pairs={{64,0},{72,8},{80,16},{88,24},{96,32},{104,40},{112,48},{120,56},{... | collective-permute-start | bytes 589832 | tf_op jit(solution)/shard_map/ppermute | solution.py:29

commit v3 on v2

--- a/solution.py
+++ b/solution.py
@@ -33,6 +33,10 @@
     return permuted(block, "ctx", lambda i: i + planes * XS)
 
 
+def two_planes_on(block, sign):
+    return permuted(block, "ctx", lambda i: i + sign * 2 * XS if i % XS else -1)
+
+
 def to_query_partner(block):
     return permuted(block, "ctx", lambda i: i ^ 1)
 
@@ -143,25 +147,31 @@
 
 
 def project_kernel(
-    place_ref, here, before, after, across_low, across_high, own_weight, other_weight, own_ref, other_ref, across
+    place_ref, here, before, after, across_low, across_high, own_weight, other_weight,
+    own_ref, other_ref, here_s, across, other_s, semaphores,
 ):
-    features = here.shape[0]
+    here_copy = pltpu.make_async_copy(here, here_s, semaphores.at[0])
+    other_copy = pltpu.make_async_copy(other_weight, other_s, semaphores.at[1])
+    here_copy.start()
+    other_copy.start()
+    features = here_s.shape[0]
     y, core = place_ref[2], place_ref[3]
     across[: features // 2] = across_low[...]
     across[features // 2 :] = across_high[...]
-    own = jnp.zeros(own_ref.shape, jnp.float32)
-    other = jnp.zeros(own_ref.shape, jnp.float32)
-    for steps, block in ((0, here), (YS - 1, before), (1, after), (2, across)):
-        at = pl.multiple_of(lax.rem(y + steps, YS) * 2 * features, HD)
-        columns = pl.ds(at, 2 * features)
-
-        def of_core(ref):
-            return jnp.where(core == 0, ref[:, columns][:, :features], ref[:, columns][:, features:])
-
-        own += dot(of_core(own_weight), block[...])
-        other += dot(of_core(other_weight), block[...])
-    own_ref[...] = own
-    other_ref[...] = other
+    blocks = ((1, after), (2, across), (3, before), (0, here_s))
+
+    def product(weight):
+        total = jnp.zeros(own_ref.shape, jnp.float32)
+        for steps, block in blocks:
+            at = pl.multiple_of(lax.rem(y + steps, YS) * 2 * features, HD)
+            both = weight[:, pl.ds(at, 2 * features)]
+            total += dot(jnp.where(core == 0, both[:, :features], both[:, features:]), block[...])
+        return total
+
+    here_copy.wait()
+    own_ref[...] = product(own_weight)
+    other_copy.wait()
+    other_ref[...] = product(other_s)
 
 
 def delta_kernel(sums_ref, attended_ref, grad_ref, other_grad_ref, out_ref):
@@ -316,9 +326,14 @@
     return pl.pallas_call(
         project_kernel,
         out_shape=(like((heads, rows), jnp.float32),) * 2,
-        in_specs=[smem()] + [vmem()] * 7,
+        in_specs=[smem(), hbm()] + [vmem()] * 5 + [hbm()],
         out_specs=(vmem(),) * 2,
-        scratch_shapes=[pltpu.VMEM((features, rows), jnp.bfloat16)],
+        scratch_shapes=[
+            pltpu.VMEM((features, rows), jnp.bfloat16),
+            pltpu.VMEM((features, rows), jnp.bfloat16),
+            pltpu.VMEM(own_weight.shape, jnp.bfloat16),
+            pltpu.SemaphoreType.DMA((2,)),
+        ],
         compiler_params=params(),
         cost_estimate=cost(4 * YS * heads * rows * features, 5_000_000),
         name="head_projection",
@@ -391,8 +406,9 @@
     own = grad_out.T
     before, after = turned(own, 1), turned(own, -1)
     here = jnp.stack([key_rows, value_rows], axis=0)
-    back, back2 = planes_on(here, 1), planes_on(here, 2)
-    other_queries, other_weight = to_query_partner(query_rows), to_other_core(out_weight)
+    back, back2 = planes_on(here, 1), two_planes_on(here, 1)
+    other_queries = to_query_partner(query_rows)
+    other_weight = to_other_core(out_weight)
     before, after, back = lax.optimization_barrier((before, after, back))
     across_low = turned(before[: features // 2], 1)
     across_high = turned(after[features // 2 :], -1)
@@ -417,8 +433,8 @@
     far_grads = to_key_partner(far_grads).astype(jnp.float32)
     query_grads, other_query_grads, here_grads, back_grads, back2_grads = backward_grads(*common, acc)
     other_query_grads = to_query_partner(other_query_grads)
-    back2_grads = planes_on(
-        (back2_grads + jnp.where(x < 2, 0.0, far_grads[1])).astype(jnp.bfloat16), -2
+    back2_grads = two_planes_on(
+        (back2_grads + jnp.where(x < 2, 0.0, far_grads[1])).astype(jnp.bfloat16), -1
     )
     back_grads = planes_on((back_grads + far_grads[0]).astype(jnp.bfloat16), -1)
     query_grads = (query_grads + other_query_grads.astype(jnp.float32)).astype(jnp.bfloat16)

time: 107 us -> 106 us (level)
  the two profiles are of different devices: /device:TPU:248 before, /device:TPU:250 now
where the time goes in v3:
time: 106 us; the launch traced here: 105 us
  starting transfers between devices  49.1 us (46%)
  waiting for transfers between devices  28.2 us (27%)
  Pallas kernels  21 us (20%)
  other arithmetic  4.07 us (4%)
  local copies, waits for them, and re-layouts  1.77 us (2%)
    ppermute x16, starting transfers between devices, permuted(): return lax.ppermute(block, axis, route)  49.1 us
    ppermute x16, waiting for transfers between devices, permuted(): return lax.ppermute(block, axis, route)  28.2 us
    pallas_call x2, Pallas kernels, backward_grads(): pl.pallas_call(functools.partial(grads_kernel, tasks, slots), out_shape=o...  11.8 us
    pallas_call x1, Pallas kernels, forward_stats(): pl.pallas_call(stats_kernel, out_shape=(like((1, 2 * width), jnp.float32)...  5.45 us
    pallas_call x1, Pallas kernels, project(): pl.pallas_call(project_kernel, out_shape=(like((heads, rows), jnp.float32...  3.66 us
  transfers between devices with their start and end apart: 16, of which 7 were waited for; matrix products, arithmetic and copies ran while one was open for 4% of the time, Pallas kernels for 11%

profile of v3, /device:TPU:250, one launch (start us, length us, event | category | flops | bytes accessed | tf_op | source)
XLA Modules:
  0.0 105.2 jit_solution(4289243176325071174)
XLA Ops:
  0.6 2.1 %collective-permute-start.7 = (bf16[256,4608]{1,0:T(8,128)(2,1)}, bf16[256,4608]{1,0:T(8,128)(2,1)}, u32[]{:S(2)}, u32[]{:S(2)}) collective-permute-start(bf16[256,4608]{1,0:T(8,128)(2,1)} %own_weight.1), channel_id=1, source_target_pairs={{0,1},{1,0},{2,3},{3,2},{4,5},{5,4},{6,7},{7,6},{8,9},{9,8},{10,11... | collective-permute-start | bytes 7077896 | tf_op jit(solution)/shard_map/ppermute | solution.py:29
  2.7 2.1 %collective-permute-start.1 = (bf16[576,384]{1,0:T(8,128)(2,1)}, bf16[576,384]{1,0:T(8,128)(2,1)S(1)}, u32[]{:S(2)}, u32[]{:S(2)}) collective-permute-start(bf16[576,384]{1,0:T(8,128)(2,1)} %bitcast.28), channel_id=1, source_target_pairs={{0,2},{1,3},{2,4},{3,5},{4,6},{5,7},{6,0},{7,1},{8,10},{9,11},{10,... | collective-permute-start | bytes 1327112 | tf_op jit(solution)/shard_map/ppermute | solution.py:29
  4.8 3.7 %collective-permute-start.2 = (bf16[576,384]{1,0:T(8,128)(2,1)}, bf16[576,384]{1,0:T(8,128)(2,1)S(1)}, u32[]{:S(2)}, u32[]{:S(2)}) collective-permute-start(bf16[576,384]{1,0:T(8,128)(2,1)} %bitcast.29), channel_id=1, source_target_pairs={{0,6},{1,7},{2,0},{3,1},{4,2},{5,3},{6,4},{7,5},{8,14},{9,15},{10,... | collective-permute-start | bytes 1327112 | tf_op jit(solution)/shard_map/ppermute | solution.py:29
  8.6 1.0 pad_maximum_fusion.1.here
  9.5 5.0 %collective-permute-start.3 = (bf16[2,384,128]{2,1,0:T(8,128)(2,1)S(1)}, bf16[2,384,128]{2,1,0:T(8,128)(2,1)}, u32[]{:S(2)}, u32[]{:S(2)}) collective-permute-start(bf16[2,384,128]{2,1,0:T(8,128)(2,1)S(1)} %pad_maximum_fusion.1.here), channel_id=1, source_target_pairs={{0,32},{8,40},{16,48},{24,56},{32,64},{40,72},{48,80},{56,88},{64,... | collective-permute-start | bytes 589832 | tf_op jit(solution)/shard_map/ppermute | solution.py:29
  14.6 3.4 %collective-permute-start.4 = (bf16[2,384,128]{2,1,0:T(8,128)(2,1)S(1)}, bf16[2,384,128]{2,1,0:T(8,128)(2,1)}, u32[]{:S(2)}, u32[]{:S(2)}) collective-permute-start(bf16[2,384,128]{2,1,0:T(8,128)(2,1)S(1)} %pad_maximum_fusion.1.here), channel_id=1, source_target_pairs={{8,72},{16,80},{24,88},{40,104},{48,112},{56,120},{72,136},{80,144... | collective-permute-start | bytes 589832 | tf_op jit(solution)/shard_map/ppermute | solution.py:29
  18.0 0.1 pad_add_fusion.place_ref
  18.1 3.4 %collective-permute-done.3.back = bf16[2,384,128]{2,1,0:T(8,128)(2,1)} collective-permute-done((bf16[2,384,128]{2,1,0:T(8,128)(2,1)S(1)}, bf16[2,384,128]{2,1,0:T(8,128)(2,1)}, u32[]{:S(2)}, u32[]{:S(2)}) %collective-permute-start.3) | collective-permute-done | bytes 196640 | tf_op jit(solution)/shard_map/ppermute | solution.py:29
  21.5 0.0 collective-permute-done.1.before
  21.5 0.0 collective-permute-done.2.after
  21.5 3.3 %collective-permute-start.5 = (bf16[288,384]{1,0:T(8,128)(2,1)S(1)}, bf16[288,384]{1,0:T(8,128)(2,1)S(1)}, u32[]{:S(2)}, u32[]{:S(2)}) collective-permute-start(bf16[288,384]{1,0:T(8,128)(2,1)S(1)} %slice.19), channel_id=1, source_target_pairs={{0,2},{1,3},{2,4},{3,5},{4,6},{5,7},{6,0},{7,1},{8,10},{9,11},{10,... | collective-permute-start | bytes 663560 | tf_op jit(solution)/shard_map/ppermute | solution.py:29
  24.9 2.5 %collective-permute-start.6 = (bf16[288,384]{1,0:T(8,128)(2,1)S(1)}, bf16[288,384]{1,0:T(8,128)(2,1)S(1)}, u32[]{:S(2)}, u32[]{:S(2)}) collective-permute-start(bf16[288,384]{1,0:T(8,128)(2,1)S(1)} %slice.20), channel_id=1, source_target_pairs={{0,6},{1,7},{2,0},{3,1},{4,2},{5,3},{6,4},{7,5},{8,14},{9,15},{10,... | collective-permute-start | bytes 663560 | tf_op jit(solution)/shard_map/ppermute | solution.py:29
  27.4 0.0 collective-permute-done.4.back2
  27.4 1.0 select_bitcast_fusion
  28.4 0.0 copy-start.2
  28.4 0.0 copy-start.3
  28.4 0.0 copy-start.4
  28.4 1.0 pad_maximum_fusion
  29.4 0.0 collective-permute-done.5.across_low
  29.4 4.5 %collective-permute-done.6.across_high = bf16[288,384]{1,0:T(8,128)(2,1)S(1)} collective-permute-done((bf16[288,384]{1,0:T(8,128)(2,1)S(1)}, bf16[288,384]{1,0:T(8,128)(2,1)S(1)}, u32[]{:S(2)}, u32[]{:S(2)}) %collective-permute-start.6) | collective-permute-done | bytes 221216 | tf_op jit(solution)/shard_map/ppermute | solution.py:29
  33.9 0.0 collective-permute-done.7.other_weight
  33.9 1.0 copy-done.1
  34.9 3.7 %head_projection.1 = (f32[256,384]{1,0:T(8,128)S(1)}, f32[256,384]{1,0:T(8,128)S(1)}) custom-call(s32[4]{0:T(128)S(1)} %pad_add_fusion.place_ref, bf16[576,384]{1,0:T(8,128)(2,1)S(1)} %bitcast.30, bf16[576,384]{1,0:T(8,128)(2,1)S(1)} %collective-permute-done.1.before, bf16[576,384]{1,0:T(8,128)(2,1)S(1)} %collective-permute-done.2.after, ...), custom_call_target="tpu_custom_call" | custom-call | flops 905969664 | bytes 5000000 | tf_op jit(solution)/shard_map/head_projection/pallas_call | solution.py:326
  38.6 1.9 %collective-permute-start.8 = (f32[256,384]{1,0:T(8,128)S(1)}, f32[256,384]{1,0:T(8,128)S(1)}, u32[]{:S(2)}, u32[]{:S(2)}) collective-permute-start(f32[256,384]{1,0:T(8,128)S(1)} %get-tuple-element.26), channel_id=1, source_target_pairs={{0,1},{1,0},{2,3},{3,2},{4,5},{5,4},{6,7},{7,6},{8,9},{9,8},{10,11... | collective-permute-start | bytes 1179656 | tf_op jit(solution)/shard_map/ppermute | solution.py:29
  40.5 3.4 %collective-permute-start.10 = (bf16[2,2,384,128]{3,2,1,0:T(8,128)(2,1)S(1)}, bf16[2,2,384,128]{3,2,1,0:T(8,128)(2,1)S(1)}, u32[]{:S(2)}, u32[]{:S(2)}) collective-permute-start(bf16[2,2,384,128]{3,2,1,0:T(8,128)(2,1)S(1)} %pad_maximum_fusion), channel_id=1, source_target_pairs={{0,24},{8,16},{16,8},{24,0},{32,56},{40,48},{48,40},{56,32},{64,88... | collective-permute-start | bytes 1179656 | tf_op jit(solution)/shard_map/ppermute | solution.py:29
  43.9 3.7 %collective-permute-start = (bf16[384,256]{1,0:T(8,128)(2,1)S(1)}, bf16[384,256]{1,0:T(8,128)(2,1)S(1)}, u32[]{:S(2)}, u32[]{:S(2)}) collective-permute-start(bf16[384,256]{1,0:T(8,128)(2,1)S(1)} %copy-done.2), channel_id=1, source_target_pairs={{0,8},{8,0},{16,24},{24,16},{32,40},{40,32},{48,56},{56,48},{64,72... | collective-permute-start | bytes 589832 | tf_op jit(solution)/shard_map/ppermute | solution.py:29
  47.7 0.0 collective-permute-done.8
  47.7 2.1 %collective-permute-start.9 = (bf16[256,384]{1,0:T(8,128)(2,1)S(1)}, bf16[256,384]{1,0:T(8,128)(2,1)S(1)}, u32[]{:S(2)}, u32[]{:S(2)}) collective-permute-start(bf16[256,384]{1,0:T(8,128)(2,1)S(1)} %add_convert_fusion.1.grad_ref), channel_id=1, source_target_pairs={{0,8},{8,0},{16,24},{24,16},{32,40},{40,32},{48,56},{56,48},{64,72... | collective-permute-start | bytes 589832 | tf_op jit(solution)/shard_map/ppermute | solution.py:29
  49.9 3.7 %collective-permute-done.other_query_ref = bf16[384,256]{1,0:T(8,128)(2,1)S(1)} collective-permute-done((bf16[384,256]{1,0:T(8,128)(2,1)S(1)}, bf16[384,256]{1,0:T(8,128)(2,1)S(1)}, u32[]{:S(2)}, u32[]{:S(2)}) %collective-permute-start) | collective-permute-done | bytes 196640 | tf_op jit(solution)/shard_map/ppermute | solution.py:29
  53.6 0.4 collective-permute-done.10.far
  53.9 5.4 %attention_stats.1 = (f32[1,1536]{1,0:T(1,128)S(1)}, f32[128,1536]{1,0:T(8,128)S(1)}) custom-call(s32[4]{0:T(128)S(1)} %pad_add_fusion.place_ref, s32[18]{0:T(128)S(1)} %copy-done.3, s32[18]{0:T(128)S(1)} %copy-done.4, bf16[384,256]{1,0:T(8,128)(2,1)S(1)} %copy-done.2, bf16[384,256]{1,0:T(8,128)(2,1)S(1)} %collective-permute-done.other_query_ref, ...), custom_call_target="tpu_custom_call" | custom-call | flops 1207959552 | bytes 3000000 | tf_op jit(solution)/shard_map/attention_stats/pallas_call | solution.py:305
  59.4 0.1 partial_deltas.1.stats_ref
  59.5 3.5 %collective-permute-start.11 = (f32[8,1536]{1,0:T(8,128)S(1)}, f32[8,1536]{1,0:T(8,128)S(1)}, u32[]{:S(2)}, u32[]{:S(2)}) collective-permute-start(f32[8,1536]{1,0:T(8,128)S(1)} %partial_deltas.1.stats_ref), channel_id=1, source_target_pairs={{0,8},{8,0},{16,24},{24,16},{32,40},{40,32},{48,56},{56,48},{64,72... | collective-permute-start | bytes 147464 | tf_op jit(solution)/shard_map/ppermute | solution.py:29
  63.0 2.5 %collective-permute-done.11.other_stats_ref = f32[8,1536]{1,0:T(8,128)S(1)} collective-permute-done((f32[8,1536]{1,0:T(8,128)S(1)}, f32[8,1536]{1,0:T(8,128)S(1)}, u32[]{:S(2)}, u32[]{:S(2)}) %collective-permute-start.11) | collective-permute-done | bytes 49184 | tf_op jit(solution)/shard_map/ppermute | solution.py:29
  65.5 5.9 %far_grads.1 = (f32[128,1536]{1,0:T(8,128)S(1)}, bf16[2,384,256]{2,1,0:T(8,128)(2,1)S(1)}) custom-call(s32[4]{0:T(128)S(1)} %pad_add_fusion.place_ref, s32[18]{0:T(128)S(1)} %copy-done.3, s32[18]{0:T(128)S(1)} %copy-done.4, bf16[384,256]{1,0:T(8,128)(2,1)S(1)} %copy-done.2, bf16[384,256]{1,0:T(8,128)(2,1)S(1)} %collective-permute-done.other_query_ref, ...), custom_call_target="tpu_custom_call" | custom-call | flops 1509949440 | bytes 4000000 | tf_op jit(solution)/shard_map/far_grads/pallas_call | solution.py:368
  71.4 4.0 %collective-permute-start.13 = (bf16[2,384,256]{2,1,0:T(8,128)(2,1)S(1)}, bf16[2,384,256]{2,1,0:T(8,128)(2,1)S(1)}, u32[]{:S(2)}, u32[]{:S(2)}) collective-permute-start(bf16[2,384,256]{2,1,0:T(8,128)(2,1)S(1)} %get-tuple-element.34), channel_id=1, source_target_pairs={{0,24},{8,16},{16,8},{24,0},{32,56},{40,48},{48,40},{56,32},{64,88... | collective-permute-start | bytes 1179656 | tf_op jit(solution)/shard_map/ppermute | solution.py:29
  75.4 5.9 %near_grads.1 = (f32[384,256]{1,0:T(8,128)S(1)}, bf16[384,256]{1,0:T(8,128)(2,1)S(1)}, f32[384,256]{1,0:T(8,128)S(1)}, f32[384,256]{1,0:T(8,128)S(1)}, f32[384,256]{1,0:T(8,128)S(1)}) custom-call(s32[4]{0:T(128)S(1)} %pad_add_fusion.place_ref, s32[18]{0:T(128)S(1)} %copy-done.3, s32[18]{0:T(128)S(1)} %copy-done.4, bf16[384,256]{1,0:T(8,128)(2,1)S(1)} %copy-done.2, ...), custom_call_target="tpu_custom_call" | custom-call | flops 1509949440 | bytes 4000000 | tf_op jit(solution)/shard_map/near_grads/pallas_call | solution.py:368
  81.3 4.5 %collective-permute-start.12 = (bf16[384,256]{1,0:T(8,128)(2,1)S(1)}, bf16[384,256]{1,0:T(8,128)(2,1)S(1)}, u32[]{:S(2)}, u32[]{:S(2)}) collective-permute-start(bf16[384,256]{1,0:T(8,128)(2,1)S(1)} %get-tuple-element.32), channel_id=1, source_target_pairs={{0,8},{8,0},{16,24},{24,16},{32,40},{40,32},{48,56},{56,48},{64,72... | collective-permute-start | bytes 589832 | tf_op jit(solution)/shard_map/ppermute | solution.py:29
  85.9 0.1 convert_element_type.30
  85.9 0.1 fusion.1
  86.1 1.9 %collective-permute-start.14 = (bf16[384,256]{1,0:T(8,128)(2,1)S(1)}, bf16[384,256]{1,0:T(8,128)(2,1)S(1)}, u32[]{:S(2)}, u32[]{:S(2)}) collective-permute-start(bf16[384,256]{1,0:T(8,128)(2,1)S(1)} %get-tuple-element.37), channel_id=1, source_target_pairs={{32,0},{40,8},{48,16},{56,24},{64,32},{72,40},{80,48},{88,56},{96,... | collective-permute-start | bytes 589832 | tf_op jit(solution)/shard_map/ppermute | solution.py:29
  88.0 1.9 %collective-permute-start.15 = (bf16[384,256]{1,0:T(8,128)(2,1)S(1)}, bf16[384,256]{1,0:T(8,128)(2,1)S(1)}, u32[]{:S(2)}, u32[]{:S(2)}) collective-permute-start(bf16[384,256]{1,0:T(8,128)(2,1)S(1)} %get-tuple-element.38), channel_id=1, source_target_pairs={{72,8},{80,16},{88,24},{104,40},{112,48},{120,56},{136,72},{144,80... | collective-permute-start | bytes 589832 | tf_op jit(solution)/shard_map/ppermute | solution.py:29
  89.9 0.0 collective-permute-done.12
  89.9 0.7 add_convert_fusion
  90.7 8.4 %collective-permute-done.14 = bf16[384,256]{1,0:T(8,128)(2,1)S(1)} collective-permute-done((bf16[384,256]{1,0:T(8,128)(2,1)S(1)}, bf16[384,256]{1,0:T(8,128)(2,1)S(1)}, u32[]{:S(2)}, u32[]{:S(2)}) %collective-permute-start.14) | collective-permute-done | bytes 196640 | tf_op jit(solution)/shard_map/ppermute | solution.py:29
  99.0 5.4 %collective-permute-done.15 = bf16[384,256]{1,0:T(8,128)(2,1)S(1)} collective-permute-done((bf16[384,256]{1,0:T(8,128)(2,1)S(1)}, bf16[384,256]{1,0:T(8,128)(2,1)S(1)}, u32[]{:S(2)}, u32[]{:S(2)}) %collective-permute-start.15) | collective-permute-done | bytes 196640 | tf_op jit(solution)/shard_map/ppermute | solution.py:29
  104.4 0.1 fusion.5
  104.5 0.7 fusion.6
  (11 shorter events, 0.1 us)
Async XLA Ops:
  0.6 33.3 %copy-start = (bf16[256,4608]{1,0:T(8,128)(2,1)S(1)}, bf16[256,4608]{1,0:T(8,128)(2,1)}, u32[]{:S(2)}) copy-start(bf16[256,4608]{1,0:T(8,128)(2,1)} %own_weight.1) | copy-start | bytes 7077892
  0.6 33.3 %collective-permute-start.7 = (bf16[256,4608]{1,0:T(8,128)(2,1)}, bf16[256,4608]{1,0:T(8,128)(2,1)}, u32[]{:S(2)}, u32[]{:S(2)}) collective-permute-start(bf16[256,4608]{1,0:T(8,128)(2,1)} %own_weight.1), channel_id=1, source_target_pairs={{0,1},{1,0},{2,3},{3,2},{4,5},{5,4},{6,7},{7,6},{8,9},{9,8},{10,11... | collective-permute-start | bytes 7077896 | tf_op jit(solution)/shard_map/ppermute | solution.py:29
  2.7 18.8 %collective-permute-start.1 = (bf16[576,384]{1,0:T(8,128)(2,1)}, bf16[576,384]{1,0:T(8,128)(2,1)S(1)}, u32[]{:S(2)}, u32[]{:S(2)}) collective-permute-start(bf16[576,384]{1,0:T(8,128)(2,1)} %bitcast.28), channel_id=1, source_target_pairs={{0,2},{1,3},{2,4},{3,5},{4,6},{5,7},{6,0},{7,1},{8,10},{9,11},{10,... | collective-permute-start | bytes 1327112 | tf_op jit(solution)/shard_map/ppermute | solution.py:29
  4.8 16.6 %collective-permute-start.2 = (bf16[576,384]{1,0:T(8,128)(2,1)}, bf16[576,384]{1,0:T(8,128)(2,1)S(1)}, u32[]{:S(2)}, u32[]{:S(2)}) collective-permute-start(bf16[576,384]{1,0:T(8,128)(2,1)} %bitcast.29), channel_id=1, source_target_pairs={{0,6},{1,7},{2,0},{3,1},{4,2},{5,3},{6,4},{7,5},{8,14},{9,15},{10,... | collective-permute-start | bytes 1327112 | tf_op jit(solution)/shard_map/ppermute | solution.py:29
  9.5 11.9 %collective-permute-start.3 = (bf16[2,384,128]{2,1,0:T(8,128)(2,1)S(1)}, bf16[2,384,128]{2,1,0:T(8,128)(2,1)}, u32[]{:S(2)}, u32[]{:S(2)}) collective-permute-start(bf16[2,384,128]{2,1,0:T(8,128)(2,1)S(1)} %pad_maximum_fusion.1.here), channel_id=1, source_target_pairs={{0,32},{8,40},{16,48},{24,56},{32,64},{40,72},{48,80},{56,88},{64,... | collective-permute-start | bytes 589832 | tf_op jit(solution)/shard_map/ppermute | solution.py:29
  14.6 12.8 %collective-permute-start.4 = (bf16[2,384,128]{2,1,0:T(8,128)(2,1)S(1)}, bf16[2,384,128]{2,1,0:T(8,128)(2,1)}, u32[]{:S(2)}, u32[]{:S(2)}) collective-permute-start(bf16[2,384,128]{2,1,0:T(8,128)(2,1)S(1)} %pad_maximum_fusion.1.here), channel_id=1, source_target_pairs={{8,72},{16,80},{24,88},{40,104},{48,112},{56,120},{72,136},{80,144... | collective-permute-start | bytes 589832 | tf_op jit(solution)/shard_map/ppermute | solution.py:29
  21.5 7.9 %collective-permute-start.5 = (bf16[288,384]{1,0:T(8,128)(2,1)S(1)}, bf16[288,384]{1,0:T(8,128)(2,1)S(1)}, u32[]{:S(2)}, u32[]{:S(2)}) collective-permute-start(bf16[288,384]{1,0:T(8,128)(2,1)S(1)} %slice.19), channel_id=1, source_target_pairs={{0,2},{1,3},{2,4},{3,5},{4,6},{5,7},{6,0},{7,1},{8,10},{9,11},{10,... | collective-permute-start | bytes 663560 | tf_op jit(solution)/shard_map/ppermute | solution.py:29
  24.9 9.0 %collective-permute-start.6 = (bf16[288,384]{1,0:T(8,128)(2,1)S(1)}, bf16[288,384]{1,0:T(8,128)(2,1)S(1)}, u32[]{:S(2)}, u32[]{:S(2)}) collective-permute-start(bf16[288,384]{1,0:T(8,128)(2,1)S(1)} %slice.20), channel_id=1, source_target_pairs={{0,6},{1,7},{2,0},{3,1},{4,2},{5,3},{6,4},{7,5},{8,14},{9,15},{10,... | collective-permute-start | bytes 663560 | tf_op jit(solution)/shard_map/ppermute | solution.py:29
  28.4 15.6 %copy-start.2 = (bf16[384,256]{1,0:T(8,128)(2,1)S(1)}, bf16[384,256]{1,0:T(8,128)(2,1)}, u32[]{:S(2)}) copy-start(bf16[384,256]{1,0:T(8,128)(2,1)} %query_ref.5) | copy-start | bytes 589828
  28.4 25.5 %copy-start.3 = (s32[18]{0:T(128)S(1)}, s32[18]{0:T(128)}, u32[]{:S(2)}) copy-start(s32[18]{0:T(128)} %lengths_ref.5) | copy-start | bytes 220
  28.4 25.5 %copy-start.4 = (s32[18]{0:T(128)S(1)}, s32[18]{0:T(128)}, u32[]{:S(2)}) copy-start(s32[18]{0:T(128)} %order_ref.5) | copy-start | bytes 220
  33.9 1.0 copy-start.1
  38.6 9.1 %collective-permute-start.8 = (f32[256,384]{1,0:T(8,128)S(1)}, f32[256,384]{1,0:T(8,128)S(1)}, u32[]{:S(2)}, u32[]{:S(2)}) collective-permute-start(f32[256,384]{1,0:T(8,128)S(1)} %get-tuple-element.26), channel_id=1, source_target_pairs={{0,1},{1,0},{2,3},{3,2},{4,5},{5,4},{6,7},{7,6},{8,9},{9,8},{10,11... | collective-permute-start | bytes 1179656 | tf_op jit(solution)/shard_map/ppermute | solution.py:29
  40.5 13.4 %collective-permute-start.10 = (bf16[2,2,384,128]{3,2,1,0:T(8,128)(2,1)S(1)}, bf16[2,2,384,128]{3,2,1,0:T(8,128)(2,1)S(1)}, u32[]{:S(2)}, u32[]{:S(2)}) collective-permute-start(bf16[2,2,384,128]{3,2,1,0:T(8,128)(2,1)S(1)} %pad_maximum_fusion), channel_id=1, source_target_pairs={{0,24},{8,16},{16,8},{24,0},{32,56},{40,48},{48,40},{56,32},{64,88... | collective-permute-start | bytes 1179656 | tf_op jit(solution)/shard_map/ppermute | solution.py:29
  43.9 9.6 %collective-permute-start = (bf16[384,256]{1,0:T(8,128)(2,1)S(1)}, bf16[384,256]{1,0:T(8,128)(2,1)S(1)}, u32[]{:S(2)}, u32[]{:S(2)}) collective-permute-start(bf16[384,256]{1,0:T(8,128)(2,1)S(1)} %copy-done.2), channel_id=1, source_target_pairs={{0,8},{8,0},{16,24},{24,16},{32,40},{40,32},{48,56},{56,48},{64,72... | collective-permute-start | bytes 589832 | tf_op jit(solution)/shard_map/ppermute | solution.py:29
  47.7 11.7 %collective-permute-start.9 = (bf16[256,384]{1,0:T(8,128)(2,1)S(1)}, bf16[256,384]{1,0:T(8,128)(2,1)S(1)}, u32[]{:S(2)}, u32[]{:S(2)}) collective-permute-start(bf16[256,384]{1,0:T(8,128)(2,1)S(1)} %add_convert_fusion.1.grad_ref), channel_id=1, source_target_pairs={{0,8},{8,0},{16,24},{24,16},{32,40},{40,32},{48,56},{56,48},{64,72... | collective-permute-start | bytes 589832 | tf_op jit(solution)/shard_map/ppermute | solution.py:29
  59.5 6.0 %collective-permute-start.11 = (f32[8,1536]{1,0:T(8,128)S(1)}, f32[8,1536]{1,0:T(8,128)S(1)}, u32[]{:S(2)}, u32[]{:S(2)}) collective-permute-start(f32[8,1536]{1,0:T(8,128)S(1)} %partial_deltas.1.stats_ref), channel_id=1, source_target_pairs={{0,8},{8,0},{16,24},{24,16},{32,40},{40,32},{48,56},{56,48},{64,72... | collective-permute-start | bytes 147464 | tf_op jit(solution)/shard_map/ppermute | solution.py:29
  71.4 14.4 %collective-permute-start.13 = (bf16[2,384,256]{2,1,0:T(8,128)(2,1)S(1)}, bf16[2,384,256]{2,1,0:T(8,128)(2,1)S(1)}, u32[]{:S(2)}, u32[]{:S(2)}) collective-permute-start(bf16[2,384,256]{2,1,0:T(8,128)(2,1)S(1)} %get-tuple-element.34), channel_id=1, source_target_pairs={{0,24},{8,16},{16,8},{24,0},{32,56},{40,48},{48,40},{56,32},{64,88... | collective-permute-start | bytes 1179656 | tf_op jit(solution)/shard_map/ppermute | solution.py:29
  81.3 8.6 %collective-permute-start.12 = (bf16[384,256]{1,0:T(8,128)(2,1)S(1)}, bf16[384,256]{1,0:T(8,128)(2,1)S(1)}, u32[]{:S(2)}, u32[]{:S(2)}) collective-permute-start(bf16[384,256]{1,0:T(8,128)(2,1)S(1)} %get-tuple-element.32), channel_id=1, source_target_pairs={{0,8},{8,0},{16,24},{24,16},{32,40},{40,32},{48,56},{56,48},{64,72... | collective-permute-start | bytes 589832 | tf_op jit(solution)/shard_map/ppermute | solution.py:29
  86.1 13.0 %collective-permute-start.14 = (bf16[384,256]{1,0:T(8,128)(2,1)S(1)}, bf16[384,256]{1,0:T(8,128)(2,1)S(1)}, u32[]{:S(2)}, u32[]{:S(2)}) collective-permute-start(bf16[384,256]{1,0:T(8,128)(2,1)S(1)} %get-tuple-element.37), channel_id=1, source_target_pairs={{32,0},{40,8},{48,16},{56,24},{64,32},{72,40},{80,48},{88,56},{96,... | collective-permute-start | bytes 589832 | tf_op jit(solution)/shard_map/ppermute | solution.py:29
  88.0 16.4 %collective-permute-start.15 = (bf16[384,256]{1,0:T(8,128)(2,1)S(1)}, bf16[384,256]{1,0:T(8,128)(2,1)S(1)}, u32[]{:S(2)}, u32[]{:S(2)}) collective-permute-start(bf16[384,256]{1,0:T(8,128)(2,1)S(1)} %get-tuple-element.38), channel_id=1, source_target_pairs={{72,8},{80,16},{88,24},{104,40},{112,48},{120,56},{136,72},{144,80... | collective-permute-start | bytes 589832 | tf_op jit(solution)/shard_map/ppermute | solution.py:29

commit v4 on v3

--- a/solution.py
+++ b/solution.py
@@ -33,8 +33,16 @@
     return permuted(block, "ctx", lambda i: i + planes * XS)
 
 
-def two_planes_on(block, sign):
-    return permuted(block, "ctx", lambda i: i + sign * 2 * XS if i % XS else -1)
+def two_planes_on(block):
+    return permuted(block, "ctx", lambda i: i + 2 * XS if i % XS else -1)
+
+
+def from_odd_home(block):
+    return permuted(block, "ctx", lambda i: i - 2 * XS if i % 2 else -1)
+
+
+def far_home(block):
+    return permuted(block, "ctx", lambda i: (i ^ 3) - (2 * XS if i % XS < 2 else 0))
 
 
 def to_query_partner(block):
@@ -193,9 +201,9 @@
 ):
     first = FAR in slots
     if first:
-        acc, far_ref, refs = refs[0], refs[1], refs[2:]
+        acc, far_back_ref, far_ref, second_low_ref, second_ref, refs = *refs[:5], refs[5:]
     else:
-        acc_in, query_grad_ref, other_query_grad_ref, here_ref, back_ref, back2_ref, acc, refs = *refs[:7], refs[7:]
+        acc_in, query_grad_ref, other_query_grad_ref, here_ref, back_ref, acc, refs = *refs[:6], refs[6:]
     (buffer, query_t, grad_t, query_s, grad_s, key_t, starts_ref, log_ref, delta_ref, prob_s, slope_s, kv_acc,
      semaphores) = refs
     rows = query_ref.shape[0]
@@ -245,26 +253,22 @@
 
     for copy in copies:
         copy.wait()
-    for t in tasks:
+    for last, t in zip((None,) + tasks, tasks):
         pairwise(t)
-        if t > tasks[0]:
-            collect(t - 1)
+        if last is not None:
+            collect(last)
     collect(tasks[-1])
 
     def scaled(i):
         return kv_acc[i, :, :HD] * SCORE_SCALE, kv_acc[i, :, HD:]
 
     if first:
-        for i in range(2):
-            key_part, value_part = scaled(i)
-            far_ref[i, :, :HD] = key_part.astype(jnp.bfloat16)
-            far_ref[i, :, HD:] = value_part.astype(jnp.bfloat16)
+        for ref, i in ((far_back_ref, FAR_BACK), (far_ref, FAR), (second_low_ref, SECOND), (second_ref, SECOND)):
+            key_part, value_part = scaled(slots.index(i))
+            ref[:, :HD], ref[:, HD:] = key_part.astype(ref.dtype), value_part.astype(ref.dtype)
         return
-    even = x % 2 == 0
-    back_ref[:, :HD], back_ref[:, HD:] = scaled(slots.index(BACK))
-    for i, (own, second) in enumerate(zip(scaled(slots.index(HERE)), scaled(slots.index(SECOND)))):
-        here_ref[:, i * HD : (i + 1) * HD] = own + jnp.where(even, second, 0.0)
-        back2_ref[:, i * HD : (i + 1) * HD] = jnp.where(even, 0.0, second)
+    for ref, i in ((here_ref, HERE), (back_ref, BACK)):
+        ref[:, :HD], ref[:, HD:] = scaled(slots.index(i))
     for head in range(2):
         at = head * rows
         query_grad_ref[:, head * HD : (head + 1) * HD] = (acc[:, at : at + rows] * SCORE_SCALE).T
@@ -357,14 +361,11 @@
     rows = queries.shape[0]
     width = 2 * rows
     first = acc is None
-    tasks, slots = ((4, 5, 6, 7), (FAR_BACK, FAR)) if first else ((0, 1, 2, 3), (HERE, SECOND, BACK))
+    tasks, slots = ((1, 4, 5, 6, 7), (FAR_BACK, FAR, SECOND)) if first else ((2, 3, 0), (HERE, BACK))
     pairs = len(tasks) * width * rows
     acc_shape = like((HD, 2 * width), jnp.float32)
-    block = like((rows, 2 * HD), jnp.float32)
-    if first:
-        out_shape = (acc_shape, like((2, rows, 2 * HD), jnp.bfloat16))
-    else:
-        out_shape = (block, like((rows, 2 * HD), jnp.bfloat16), block, block, block)
+    wide, block = like((rows, 2 * HD), jnp.float32), like((rows, 2 * HD), jnp.bfloat16)
+    out_shape = (acc_shape, block, block, block, wide) if first else (wide, block, wide, wide)
     return pl.pallas_call(
         functools.partial(grads_kernel, tasks, slots),
         out_shape=out_shape,
@@ -406,7 +407,7 @@
     own = grad_out.T
     before, after = turned(own, 1), turned(own, -1)
     here = jnp.stack([key_rows, value_rows], axis=0)
-    back, back2 = planes_on(here, 1), two_planes_on(here, 1)
+    back, back2 = planes_on(here, 1), two_planes_on(here)
     other_queries = to_query_partner(query_rows)
     other_weight = to_other_core(out_weight)
     before, after, back = lax.optimization_barrier((before, after, back))
@@ -429,17 +430,17 @@
     common = (
         place, doc_lengths, doc_order, query_rows, other_queries, grads, other_grads, stats, other_stats, keys
     )
-    acc, far_grads = backward_grads(*common, None)
-    far_grads = to_key_partner(far_grads).astype(jnp.float32)
-    query_grads, other_query_grads, here_grads, back_grads, back2_grads = backward_grads(*common, acc)
+    acc, far_back_grads, far_grads, second_low, second = backward_grads(*common, None)
+    far_grads, second_low = far_home(far_grads), from_odd_home(second_low)
+    far_back_grads = to_key_partner(far_back_grads)
+    query_grads, other_query_grads, here_grads, back_grads = backward_grads(*common, acc)
+    far_back_grads, far_grads, second_low = lax.optimization_barrier((far_back_grads, far_grads, second_low))
+    back_grads = planes_on((back_grads + far_back_grads.astype(jnp.float32)).astype(jnp.bfloat16), -1)
     other_query_grads = to_query_partner(other_query_grads)
-    back2_grads = two_planes_on(
-        (back2_grads + jnp.where(x < 2, 0.0, far_grads[1])).astype(jnp.bfloat16), -1
-    )
-    back_grads = planes_on((back_grads + far_grads[0]).astype(jnp.bfloat16), -1)
     query_grads = (query_grads + other_query_grads.astype(jnp.float32)).astype(jnp.bfloat16)
-    total = here_grads + jnp.where(x < 2, far_grads[1], 0.0)
-    total = total + back_grads.astype(jnp.float32) + back2_grads.astype(jnp.float32)
+    total = here_grads + jnp.where(x % 2 == 0, second, 0.0)
+    for part in (far_grads, second_low, back_grads):
+        total = total + part.astype(jnp.float32)
     total = total.astype(jnp.bfloat16)
     return query_grads, total[:, :HD], total[:, HD:]
 

time: 106 us -> 111 us (1.047)
  the two profiles are of different devices: /device:TPU:250 before, /device:TPU:186 now
where the time goes in v4:
time: 111 us; the launch traced here: 110 us
  starting transfers between devices  59.1 us (53%)
  waiting for transfers between devices  22.4 us (20%)
  Pallas kernels  21.1 us (19%)
  other arithmetic  4.99 us (4%)
  local copies, waits for them, and re-layouts  1.78 us (2%)
    ppermute x17, starting transfers between devices, permuted(): return lax.ppermute(block, axis, route)  59.1 us
    ppermute x17, waiting for transfers between devices, permuted(): return lax.ppermute(block, axis, route)  22.4 us
    pallas_call x2, Pallas kernels, backward_grads(): pl.pallas_call(functools.partial(grads_kernel, tasks, slots), out_shape=o...  11.9 us
    pallas_call x1, Pallas kernels, forward_stats(): pl.pallas_call(stats_kernel, out_shape=(like((1, 2 * width), jnp.float32)...  5.45 us
    pallas_call x1, Pallas kernels, project(): pl.pallas_call(project_kernel, out_shape=(like((heads, rows), jnp.float32...  3.66 us
  transfers between devices with their start and end apart: 17, of which 8 were waited for; matrix products, arithmetic and copies ran while one was open for 4% of the time, Pallas kernels for 9%

profile of v4, /device:TPU:186, one launch (start us, length us, event | category | flops | bytes accessed | tf_op | source)
XLA Modules:
  0.0 110.4 jit_solution(5233670068359274070)
XLA Ops:
  0.6 2.1 %collective-permute-start.7 = (bf16[256,4608]{1,0:T(8,128)(2,1)}, bf16[256,4608]{1,0:T(8,128)(2,1)}, u32[]{:S(2)}, u32[]{:S(2)}) collective-permute-start(bf16[256,4608]{1,0:T(8,128)(2,1)} %own_weight.1), channel_id=1, source_target_pairs={{0,1},{1,0},{2,3},{3,2},{4,5},{5,4},{6,7},{7,6},{8,9},{9,8},{10,11... | collective-permute-start | bytes 7077896 | tf_op jit(solution)/shard_map/ppermute | solution.py:29
  2.7 2.1 %collective-permute-start.1 = (bf16[576,384]{1,0:T(8,128)(2,1)}, bf16[576,384]{1,0:T(8,128)(2,1)S(1)}, u32[]{:S(2)}, u32[]{:S(2)}) collective-permute-start(bf16[576,384]{1,0:T(8,128)(2,1)} %bitcast.10), channel_id=1, source_target_pairs={{0,2},{1,3},{2,4},{3,5},{4,6},{5,7},{6,0},{7,1},{8,10},{9,11},{10,... | collective-permute-start | bytes 1327112 | tf_op jit(solution)/shard_map/ppermute | solution.py:29
  4.8 3.7 %collective-permute-start.2 = (bf16[576,384]{1,0:T(8,128)(2,1)}, bf16[576,384]{1,0:T(8,128)(2,1)S(1)}, u32[]{:S(2)}, u32[]{:S(2)}) collective-permute-start(bf16[576,384]{1,0:T(8,128)(2,1)} %bitcast.11), channel_id=1, source_target_pairs={{0,6},{1,7},{2,0},{3,1},{4,2},{5,3},{6,4},{7,5},{8,14},{9,15},{10,... | collective-permute-start | bytes 1327112 | tf_op jit(solution)/shard_map/ppermute | solution.py:29
  8.6 1.0 pad_maximum_fusion.1.here
  9.5 3.8 %collective-permute-start.3 = (bf16[2,384,128]{2,1,0:T(8,128)(2,1)S(1)}, bf16[2,384,128]{2,1,0:T(8,128)(2,1)}, u32[]{:S(2)}, u32[]{:S(2)}) collective-permute-start(bf16[2,384,128]{2,1,0:T(8,128)(2,1)S(1)} %pad_maximum_fusion.1.here), channel_id=1, source_target_pairs={{0,32},{8,40},{16,48},{24,56},{32,64},{40,72},{48,80},{56,88},{64,... | collective-permute-start | bytes 589832 | tf_op jit(solution)/shard_map/ppermute | solution.py:29
  13.4 6.4 %collective-permute-start.4 = (bf16[2,384,128]{2,1,0:T(8,128)(2,1)S(1)}, bf16[2,384,128]{2,1,0:T(8,128)(2,1)}, u32[]{:S(2)}, u32[]{:S(2)}) collective-permute-start(bf16[2,384,128]{2,1,0:T(8,128)(2,1)S(1)} %pad_maximum_fusion.1.here), channel_id=1, source_target_pairs={{8,72},{16,80},{24,88},{40,104},{48,112},{56,120},{72,136},{80,144... | collective-permute-start | bytes 589832 | tf_op jit(solution)/shard_map/ppermute | solution.py:29
  19.8 0.1 pad_add_fusion.place_ref
  19.9 0.0 collective-permute-done.3.back
  19.9 0.7 collective-permute-done.2.after
  20.5 2.7 %collective-permute-start.5 = (bf16[288,384]{1,0:T(8,128)(2,1)S(1)}, bf16[288,384]{1,0:T(8,128)(2,1)S(1)}, u32[]{:S(2)}, u32[]{:S(2)}) collective-permute-start(bf16[288,384]{1,0:T(8,128)(2,1)S(1)} %slice.12), channel_id=1, source_target_pairs={{0,2},{1,3},{2,4},{3,5},{4,6},{5,7},{6,0},{7,1},{8,10},{9,11},{10,... | collective-permute-start | bytes 663560 | tf_op jit(solution)/shard_map/ppermute | solution.py:29
  23.3 3.1 %collective-permute-start.6 = (bf16[288,384]{1,0:T(8,128)(2,1)S(1)}, bf16[288,384]{1,0:T(8,128)(2,1)S(1)}, u32[]{:S(2)}, u32[]{:S(2)}) collective-permute-start(bf16[288,384]{1,0:T(8,128)(2,1)S(1)} %slice.13), channel_id=1, source_target_pairs={{0,6},{1,7},{2,0},{3,1},{4,2},{5,3},{6,4},{7,5},{8,14},{9,15},{10,... | collective-permute-start | bytes 663560 | tf_op jit(solution)/shard_map/ppermute | solution.py:29
  26.4 1.3 %collective-permute-done.4.back2 = bf16[2,384,128]{2,1,0:T(8,128)(2,1)} collective-permute-done((bf16[2,384,128]{2,1,0:T(8,128)(2,1)S(1)}, bf16[2,384,128]{2,1,0:T(8,128)(2,1)}, u32[]{:S(2)}, u32[]{:S(2)}) %collective-permute-start.4) | collective-permute-done | bytes 196640 | tf_op jit(solution)/shard_map/ppermute | solution.py:29
  27.8 1.0 select_bitcast_fusion
  28.8 0.0 copy-start.2
  28.8 0.0 copy-start.4
  28.8 0.0 copy-start.5
  28.8 1.0 pad_maximum_fusion
  29.8 0.0 collective-permute-done.5.across_low
  29.8 3.1 %collective-permute-done.6.across_high = bf16[288,384]{1,0:T(8,128)(2,1)S(1)} collective-permute-done((bf16[288,384]{1,0:T(8,128)(2,1)S(1)}, bf16[288,384]{1,0:T(8,128)(2,1)S(1)}, u32[]{:S(2)}, u32[]{:S(2)}) %collective-permute-start.6) | collective-permute-done | bytes 221216 | tf_op jit(solution)/shard_map/ppermute | solution.py:29
  32.9 1.0 copy-done.1
  33.9 3.7 %head_projection.1 = (f32[256,384]{1,0:T(8,128)S(1)}, f32[256,384]{1,0:T(8,128)S(1)}) custom-call(s32[4]{0:T(128)S(1)} %pad_add_fusion.place_ref, bf16[576,384]{1,0:T(8,128)(2,1)S(1)} %bitcast.12, bf16[576,384]{1,0:T(8,128)(2,1)S(1)} %collective-permute-done.1.before, bf16[576,384]{1,0:T(8,128)(2,1)S(1)} %collective-permute-done.2.after, ...), custom_call_target="tpu_custom_call" | custom-call | flops 905969664 | bytes 5000000 | tf_op jit(solution)/shard_map/head_projection/pallas_call | solution.py:330
  37.6 1.9 %collective-permute-start.8 = (f32[256,384]{1,0:T(8,128)S(1)}, f32[256,384]{1,0:T(8,128)S(1)}, u32[]{:S(2)}, u32[]{:S(2)}) collective-permute-start(f32[256,384]{1,0:T(8,128)S(1)} %get-tuple-element.31), channel_id=1, source_target_pairs={{0,1},{1,0},{2,3},{3,2},{4,5},{5,4},{6,7},{7,6},{8,9},{9,8},{10,11... | collective-permute-start | bytes 1179656 | tf_op jit(solution)/shard_map/ppermute | solution.py:29
  39.5 3.4 %collective-permute-start.10 = (bf16[2,2,384,128]{3,2,1,0:T(8,128)(2,1)S(1)}, bf16[2,2,384,128]{3,2,1,0:T(8,128)(2,1)S(1)}, u32[]{:S(2)}, u32[]{:S(2)}) collective-permute-start(bf16[2,2,384,128]{3,2,1,0:T(8,128)(2,1)S(1)} %pad_maximum_fusion), channel_id=1, source_target_pairs={{0,24},{8,16},{16,8},{24,0},{32,56},{40,48},{48,40},{56,32},{64,88... | collective-permute-start | bytes 1179656 | tf_op jit(solution)/shard_map/ppermute | solution.py:29
  42.9 3.7 %collective-permute-start = (bf16[384,256]{1,0:T(8,128)(2,1)S(1)}, bf16[384,256]{1,0:T(8,128)(2,1)S(1)}, u32[]{:S(2)}, u32[]{:S(2)}) collective-permute-start(bf16[384,256]{1,0:T(8,128)(2,1)S(1)} %copy-done.2), channel_id=1, source_target_pairs={{0,8},{8,0},{16,24},{24,16},{32,40},{40,32},{48,56},{56,48},{64,72... | collective-permute-start | bytes 589832 | tf_op jit(solution)/shard_map/ppermute | solution.py:29
  46.6 0.0 collective-permute-done.8
  46.7 2.1 %collective-permute-start.9 = (bf16[256,384]{1,0:T(8,128)(2,1)S(1)}, bf16[256,384]{1,0:T(8,128)(2,1)S(1)}, u32[]{:S(2)}, u32[]{:S(2)}) collective-permute-start(bf16[256,384]{1,0:T(8,128)(2,1)S(1)} %add_convert_fusion.3.grad_ref), channel_id=1, source_target_pairs={{0,8},{8,0},{16,24},{24,16},{32,40},{40,32},{48,56},{56,48},{64,72... | collective-permute-start | bytes 589832 | tf_op jit(solution)/shard_map/ppermute | solution.py:29
  48.8 3.7 %collective-permute-done.other_query_ref = bf16[384,256]{1,0:T(8,128)(2,1)S(1)} collective-permute-done((bf16[384,256]{1,0:T(8,128)(2,1)S(1)}, bf16[384,256]{1,0:T(8,128)(2,1)S(1)}, u32[]{:S(2)}, u32[]{:S(2)}) %collective-permute-start) | collective-permute-done | bytes 196640 | tf_op jit(solution)/shard_map/ppermute | solution.py:29
  52.6 0.4 collective-permute-done.10.far
  52.9 5.4 %attention_stats.1 = (f32[1,1536]{1,0:T(1,128)S(1)}, f32[128,1536]{1,0:T(8,128)S(1)}) custom-call(s32[4]{0:T(128)S(1)} %pad_add_fusion.place_ref, s32[18]{0:T(128)S(1)} %copy-done.4, s32[18]{0:T(128)S(1)} %copy-done.5, bf16[384,256]{1,0:T(8,128)(2,1)S(1)} %copy-done.2, bf16[384,256]{1,0:T(8,128)(2,1)S(1)} %collective-permute-done.other_query_ref, ...), custom_call_target="tpu_custom_call" | custom-call | flops 1207959552 | bytes 3000000 | tf_op jit(solution)/shard_map/attention_stats/pallas_call | solution.py:309
  58.4 0.0 collective-permute-done.9.other_grad_ref
  58.4 0.1 partial_deltas.1.stats_ref
  58.5 0.0 copy-start.3
  58.5 3.8 %collective-permute-start.11 = (f32[8,1536]{1,0:T(8,128)S(1)}, f32[8,1536]{1,0:T(8,128)S(1)}, u32[]{:S(2)}, u32[]{:S(2)}) collective-permute-start(f32[8,1536]{1,0:T(8,128)S(1)} %partial_deltas.1.stats_ref), channel_id=1, source_target_pairs={{0,8},{8,0},{16,24},{24,16},{32,40},{40,32},{48,56},{56,48},{64,72... | collective-permute-start | bytes 147464 | tf_op jit(solution)/shard_map/ppermute | solution.py:29
  62.3 2.3 %collective-permute-done.11.other_stats_ref = f32[8,1536]{1,0:T(8,128)S(1)} collective-permute-done((f32[8,1536]{1,0:T(8,128)S(1)}, f32[8,1536]{1,0:T(8,128)S(1)}, u32[]{:S(2)}, u32[]{:S(2)}) %collective-permute-start.11) | collective-permute-done | bytes 49184 | tf_op jit(solution)/shard_map/ppermute | solution.py:29
  64.6 6.9 %far_grads.1 = (f32[128,1536]{1,0:T(8,128)S(1)}, bf16[384,256]{1,0:T(8,128)(2,1)S(1)}, bf16[384,256]{1,0:T(8,128)(2,1)S(1)}, bf16[384,256]{1,0:T(8,128)(2,1)S(1)}, f32[384,256]{1,0:T(8,128)S(1)}) custom-call(s32[4]{0:T(128)S(1)} %pad_add_fusion.place_ref, s32[18]{0:T(128)S(1)} %copy-done.4, s32[18]{0:T(128)S(1)} %copy-done.5, ...), custom_call_target="tpu_custom_call" | custom-call | flops 1887436800 | bytes 4000000 | tf_op jit(solution)/shard_map/far_grads/pallas_call | solution.py:369
  71.6 3.8 %collective-permute-start.13 = (bf16[384,256]{1,0:T(8,128)(2,1)S(1)}, bf16[384,256]{1,0:T(8,128)(2,1)S(1)}, u32[]{:S(2)}, u32[]{:S(2)}) collective-permute-start(bf16[384,256]{1,0:T(8,128)(2,1)S(1)} %get-tuple-element.40), channel_id=1, source_target_pairs={{0,24},{8,16},{16,8},{24,0},{32,56},{40,48},{48,40},{56,32},{64,88... | collective-permute-start | bytes 589832 | tf_op jit(solution)/shard_map/ppermute | solution.py:29
  75.4 1.9 %collective-permute-start.14 = (bf16[384,256]{1,0:T(8,128)(2,1)S(1)}, bf16[384,256]{1,0:T(8,128)(2,1)}, u32[]{:S(2)}, u32[]{:S(2)}) collective-permute-start(bf16[384,256]{1,0:T(8,128)(2,1)S(1)} %get-tuple-element.41), channel_id=1, source_target_pairs={{16,8},{24,0},{48,40},{56,32},{64,24},{72,16},{80,72},{88,64},{96,... | collective-permute-start | bytes 589832 | tf_op jit(solution)/shard_map/ppermute | solution.py:29
  77.3 2.0 %collective-permute-start.15 = (bf16[384,256]{1,0:T(8,128)(2,1)S(1)}, bf16[384,256]{1,0:T(8,128)(2,1)}, u32[]{:S(2)}, u32[]{:S(2)}) collective-permute-start(bf16[384,256]{1,0:T(8,128)(2,1)S(1)} %get-tuple-element.42), channel_id=1, source_target_pairs={{72,8},{88,24},{104,40},{120,56},{136,72},{152,88},{168,104},{184,... | collective-permute-start | bytes 589832 | tf_op jit(solution)/shard_map/ppermute | solution.py:29
  79.3 5.0 %near_grads.1 = (f32[384,256]{1,0:T(8,128)S(1)}, bf16[384,256]{1,0:T(8,128)(2,1)S(1)}, f32[384,256]{1,0:T(8,128)S(1)}, f32[384,256]{1,0:T(8,128)S(1)}) custom-call(s32[4]{0:T(128)S(1)} %pad_add_fusion.place_ref, s32[18]{0:T(128)S(1)} %copy-done.4, s32[18]{0:T(128)S(1)} %copy-done.5, bf16[384,256]{1,0:T(8,128)(2,1)S(1)} %copy-done.3, ...), custom_call_target="tpu_custom_call" | custom-call | flops 1132462080 | bytes 4000000 | tf_op jit(solution)/shard_map/near_grads/pallas_call | solution.py:369
  84.3 3.8 %collective-permute-start.12 = (bf16[384,256]{1,0:T(8,128)(2,1)S(1)}, bf16[384,256]{1,0:T(8,128)(2,1)S(1)}, u32[]{:S(2)}, u32[]{:S(2)}) collective-permute-start(bf16[384,256]{1,0:T(8,128)(2,1)S(1)} %get-tuple-element.37), channel_id=1, source_target_pairs={{0,8},{8,0},{16,24},{24,16},{32,40},{40,32},{48,56},{56,48},{64,72... | collective-permute-start | bytes 589832 | tf_op jit(solution)/shard_map/ppermute | solution.py:29
  88.2 0.0 collective-permute-done.13
  88.2 1.6 %collective-permute-done.15 = bf16[384,256]{1,0:T(8,128)(2,1)} collective-permute-done((bf16[384,256]{1,0:T(8,128)(2,1)S(1)}, bf16[384,256]{1,0:T(8,128)(2,1)}, u32[]{:S(2)}, u32[]{:S(2)}) %collective-permute-start.15) | collective-permute-done | bytes 196640 | tf_op jit(solution)/shard_map/ppermute | solution.py:29
  89.8 0.1 add_convert_fusion.1
  89.9 8.7 %collective-permute-start.16 = (bf16[384,256]{1,0:T(8,128)(2,1)S(1)}, bf16[384,256]{1,0:T(8,128)(2,1)S(1)}, u32[]{:S(2)}, u32[]{:S(2)}) collective-permute-start(bf16[384,256]{1,0:T(8,128)(2,1)S(1)} %add_convert_fusion.1), channel_id=1, source_target_pairs={{32,0},{40,8},{48,16},{56,24},{64,32},{72,40},{80,48},{88,56},{96,... | collective-permute-start | bytes 589832 | tf_op jit(solution)/shard_map/ppermute | solution.py:29
  98.6 0.7 add_convert_fusion.2
  99.3 9.2 %collective-permute-done.16 = bf16[384,256]{1,0:T(8,128)(2,1)S(1)} collective-permute-done((bf16[384,256]{1,0:T(8,128)(2,1)S(1)}, bf16[384,256]{1,0:T(8,128)(2,1)S(1)}, u32[]{:S(2)}, u32[]{:S(2)}) %collective-permute-start.16) | collective-permute-done | bytes 196640 | tf_op jit(solution)/shard_map/ppermute | solution.py:29
  108.5 1.1 %add_convert_fusion = bf16[384,256]{1,0:T(8,128)(2,1)S(1)} fusion(bf16[384,256]{1,0:T(8,128)(2,1)S(1)} %collective-permute-done.16, bf16[384,256]{1,0:T(8,128)(2,1)} %collective-permute-done.15, bf16[384,256]{1,0:T(8,128)(2,1)} %collective-permute-done.14, f32[384,256]{1,0:T(8,128)S(1)} %get-tuple-element.38, f32[384,256]{1,0:T(8,128)S(1)} %get-tuple-element.39, ...), kind=kLoop, calls=%fused_computation.1 | loop fusion | flops 884736 | bytes 1572865 | tf_op jit(solution)/shard_map/convert_element_type | solution.py:444
  109.7 0.7 fusion
  (14 shorter events, 0.1 us)
Async XLA Ops:
  0.6 32.3 %copy-start = (bf16[256,4608]{1,0:T(8,128)(2,1)S(1)}, bf16[256,4608]{1,0:T(8,128)(2,1)}, u32[]{:S(2)}) copy-start(bf16[256,4608]{1,0:T(8,128)(2,1)} %own_weight.1) | copy-start | bytes 7077892
  0.6 32.3 %collective-permute-start.7 = (bf16[256,4608]{1,0:T(8,128)(2,1)}, bf16[256,4608]{1,0:T(8,128)(2,1)}, u32[]{:S(2)}, u32[]{:S(2)}) collective-permute-start(bf16[256,4608]{1,0:T(8,128)(2,1)} %own_weight.1), channel_id=1, source_target_pairs={{0,1},{1,0},{2,3},{3,2},{4,5},{5,4},{6,7},{7,6},{8,9},{9,8},{10,11... | collective-permute-start | bytes 7077896 | tf_op jit(solution)/shard_map/ppermute | solution.py:29
  2.7 17.2 %collective-permute-start.1 = (bf16[576,384]{1,0:T(8,128)(2,1)}, bf16[576,384]{1,0:T(8,128)(2,1)S(1)}, u32[]{:S(2)}, u32[]{:S(2)}) collective-permute-start(bf16[576,384]{1,0:T(8,128)(2,1)} %bitcast.10), channel_id=1, source_target_pairs={{0,2},{1,3},{2,4},{3,5},{4,6},{5,7},{6,0},{7,1},{8,10},{9,11},{10,... | collective-permute-start | bytes 1327112 | tf_op jit(solution)/shard_map/ppermute | solution.py:29
  4.8 15.7 %collective-permute-start.2 = (bf16[576,384]{1,0:T(8,128)(2,1)}, bf16[576,384]{1,0:T(8,128)(2,1)S(1)}, u32[]{:S(2)}, u32[]{:S(2)}) collective-permute-start(bf16[576,384]{1,0:T(8,128)(2,1)} %bitcast.11), channel_id=1, source_target_pairs={{0,6},{1,7},{2,0},{3,1},{4,2},{5,3},{6,4},{7,5},{8,14},{9,15},{10,... | collective-permute-start | bytes 1327112 | tf_op jit(solution)/shard_map/ppermute | solution.py:29
  9.5 10.3 %collective-permute-start.3 = (bf16[2,384,128]{2,1,0:T(8,128)(2,1)S(1)}, bf16[2,384,128]{2,1,0:T(8,128)(2,1)}, u32[]{:S(2)}, u32[]{:S(2)}) collective-permute-start(bf16[2,384,128]{2,1,0:T(8,128)(2,1)S(1)} %pad_maximum_fusion.1.here), channel_id=1, source_target_pairs={{0,32},{8,40},{16,48},{24,56},{32,64},{40,72},{48,80},{56,88},{64,... | collective-permute-start | bytes 589832 | tf_op jit(solution)/shard_map/ppermute | solution.py:29
  13.4 14.4 %collective-permute-start.4 = (bf16[2,384,128]{2,1,0:T(8,128)(2,1)S(1)}, bf16[2,384,128]{2,1,0:T(8,128)(2,1)}, u32[]{:S(2)}, u32[]{:S(2)}) collective-permute-start(bf16[2,384,128]{2,1,0:T(8,128)(2,1)S(1)} %pad_maximum_fusion.1.here), channel_id=1, source_target_pairs={{8,72},{16,80},{24,88},{40,104},{48,112},{56,120},{72,136},{80,144... | collective-permute-start | bytes 589832 | tf_op jit(solution)/shard_map/ppermute | solution.py:29
  20.5 9.3 %collective-permute-start.5 = (bf16[288,384]{1,0:T(8,128)(2,1)S(1)}, bf16[288,384]{1,0:T(8,128)(2,1)S(1)}, u32[]{:S(2)}, u32[]{:S(2)}) collective-permute-start(bf16[288,384]{1,0:T(8,128)(2,1)S(1)} %slice.12), channel_id=1, source_target_pairs={{0,2},{1,3},{2,4},{3,5},{4,6},{5,7},{6,0},{7,1},{8,10},{9,11},{10,... | collective-permute-start | bytes 663560 | tf_op jit(solution)/shard_map/ppermute | solution.py:29
  23.3 9.6 %collective-permute-start.6 = (bf16[288,384]{1,0:T(8,128)(2,1)S(1)}, bf16[288,384]{1,0:T(8,128)(2,1)S(1)}, u32[]{:S(2)}, u32[]{:S(2)}) collective-permute-start(bf16[288,384]{1,0:T(8,128)(2,1)S(1)} %slice.13), channel_id=1, source_target_pairs={{0,6},{1,7},{2,0},{3,1},{4,2},{5,3},{6,4},{7,5},{8,14},{9,15},{10,... | collective-permute-start | bytes 663560 | tf_op jit(solution)/shard_map/ppermute | solution.py:29
  28.8 14.2 %copy-start.2 = (bf16[384,256]{1,0:T(8,128)(2,1)S(1)}, bf16[384,256]{1,0:T(8,128)(2,1)}, u32[]{:S(2)}) copy-start(bf16[384,256]{1,0:T(8,128)(2,1)} %query_ref.5) | copy-start | bytes 589828
  28.8 24.2 %copy-start.4 = (s32[18]{0:T(128)S(1)}, s32[18]{0:T(128)}, u32[]{:S(2)}) copy-start(s32[18]{0:T(128)} %lengths_ref.5) | copy-start | bytes 220
  28.8 24.2 %copy-start.5 = (s32[18]{0:T(128)S(1)}, s32[18]{0:T(128)}, u32[]{:S(2)}) copy-start(s32[18]{0:T(128)} %order_ref.5) | copy-start | bytes 220
  32.9 1.0 copy-start.1
  37.6 9.1 %collective-permute-start.8 = (f32[256,384]{1,0:T(8,128)S(1)}, f32[256,384]{1,0:T(8,128)S(1)}, u32[]{:S(2)}, u32[]{:S(2)}) collective-permute-start(f32[256,384]{1,0:T(8,128)S(1)} %get-tuple-element.31), channel_id=1, source_target_pairs={{0,1},{1,0},{2,3},{3,2},{4,5},{5,4},{6,7},{7,6},{8,9},{9,8},{10,11... | collective-permute-start | bytes 1179656 | tf_op jit(solution)/shard_map/ppermute | solution.py:29
  39.5 13.4 %collective-permute-start.10 = (bf16[2,2,384,128]{3,2,1,0:T(8,128)(2,1)S(1)}, bf16[2,2,384,128]{3,2,1,0:T(8,128)(2,1)S(1)}, u32[]{:S(2)}, u32[]{:S(2)}) collective-permute-start(bf16[2,2,384,128]{3,2,1,0:T(8,128)(2,1)S(1)} %pad_maximum_fusion), channel_id=1, source_target_pairs={{0,24},{8,16},{16,8},{24,0},{32,56},{40,48},{48,40},{56,32},{64,88... | collective-permute-start | bytes 1179656 | tf_op jit(solution)/shard_map/ppermute | solution.py:29
  42.9 9.6 %collective-permute-start = (bf16[384,256]{1,0:T(8,128)(2,1)S(1)}, bf16[384,256]{1,0:T(8,128)(2,1)S(1)}, u32[]{:S(2)}, u32[]{:S(2)}) collective-permute-start(bf16[384,256]{1,0:T(8,128)(2,1)S(1)} %copy-done.2), channel_id=1, source_target_pairs={{0,8},{8,0},{16,24},{24,16},{32,40},{40,32},{48,56},{56,48},{64,72... | collective-permute-start | bytes 589832 | tf_op jit(solution)/shard_map/ppermute | solution.py:29
  46.7 11.7 %collective-permute-start.9 = (bf16[256,384]{1,0:T(8,128)(2,1)S(1)}, bf16[256,384]{1,0:T(8,128)(2,1)S(1)}, u32[]{:S(2)}, u32[]{:S(2)}) collective-permute-start(bf16[256,384]{1,0:T(8,128)(2,1)S(1)} %add_convert_fusion.3.grad_ref), channel_id=1, source_target_pairs={{0,8},{8,0},{16,24},{24,16},{32,40},{40,32},{48,56},{56,48},{64,72... | collective-permute-start | bytes 589832 | tf_op jit(solution)/shard_map/ppermute | solution.py:29
  58.5 20.8 %copy-start.3 = (bf16[384,256]{1,0:T(8,128)(2,1)S(1)}, bf16[384,256]{1,0:T(8,128)(2,1)}, u32[]{:S(2)}) copy-start(bf16[384,256]{1,0:T(8,128)(2,1)} %query_ref.5) | copy-start | bytes 589828
  58.5 6.1 %collective-permute-start.11 = (f32[8,1536]{1,0:T(8,128)S(1)}, f32[8,1536]{1,0:T(8,128)S(1)}, u32[]{:S(2)}, u32[]{:S(2)}) collective-permute-start(f32[8,1536]{1,0:T(8,128)S(1)} %partial_deltas.1.stats_ref), channel_id=1, source_target_pairs={{0,8},{8,0},{16,24},{24,16},{32,40},{40,32},{48,56},{56,48},{64,72... | collective-permute-start | bytes 147464 | tf_op jit(solution)/shard_map/ppermute | solution.py:29
  71.6 16.6 %collective-permute-start.13 = (bf16[384,256]{1,0:T(8,128)(2,1)S(1)}, bf16[384,256]{1,0:T(8,128)(2,1)S(1)}, u32[]{:S(2)}, u32[]{:S(2)}) collective-permute-start(bf16[384,256]{1,0:T(8,128)(2,1)S(1)} %get-tuple-element.40), channel_id=1, source_target_pairs={{0,24},{8,16},{16,8},{24,0},{32,56},{40,48},{48,40},{56,32},{64,88... | collective-permute-start | bytes 589832 | tf_op jit(solution)/shard_map/ppermute | solution.py:29
  75.4 12.8 %collective-permute-start.14 = (bf16[384,256]{1,0:T(8,128)(2,1)S(1)}, bf16[384,256]{1,0:T(8,128)(2,1)}, u32[]{:S(2)}, u32[]{:S(2)}) collective-permute-start(bf16[384,256]{1,0:T(8,128)(2,1)S(1)} %get-tuple-element.41), channel_id=1, source_target_pairs={{16,8},{24,0},{48,40},{56,32},{64,24},{72,16},{80,72},{88,64},{96,... | collective-permute-start | bytes 589832 | tf_op jit(solution)/shard_map/ppermute | solution.py:29
  77.3 12.5 %collective-permute-start.15 = (bf16[384,256]{1,0:T(8,128)(2,1)S(1)}, bf16[384,256]{1,0:T(8,128)(2,1)}, u32[]{:S(2)}, u32[]{:S(2)}) collective-permute-start(bf16[384,256]{1,0:T(8,128)(2,1)S(1)} %get-tuple-element.42), channel_id=1, source_target_pairs={{72,8},{88,24},{104,40},{120,56},{136,72},{152,88},{168,104},{184,... | collective-permute-start | bytes 589832 | tf_op jit(solution)/shard_map/ppermute | solution.py:29
  84.3 14.3 %collective-permute-start.12 = (bf16[384,256]{1,0:T(8,128)(2,1)S(1)}, bf16[384,256]{1,0:T(8,128)(2,1)S(1)}, u32[]{:S(2)}, u32[]{:S(2)}) collective-permute-start(bf16[384,256]{1,0:T(8,128)(2,1)S(1)} %get-tuple-element.37), channel_id=1, source_target_pairs={{0,8},{8,0},{16,24},{24,16},{32,40},{40,32},{48,56},{56,48},{64,72... | collective-permute-start | bytes 589832 | tf_op jit(solution)/shard_map/ppermute | solution.py:29
  89.9 18.7 %collective-permute-start.16 = (bf16[384,256]{1,0:T(8,128)(2,1)S(1)}, bf16[384,256]{1,0:T(8,128)(2,1)S(1)}, u32[]{:S(2)}, u32[]{:S(2)}) collective-permute-start(bf16[384,256]{1,0:T(8,128)(2,1)S(1)} %add_convert_fusion.1), channel_id=1, source_target_pairs={{32,0},{40,8},{48,16},{56,24},{64,32},{72,40},{80,48},{88,56},{96,... | collective-permute-start | bytes 589832 | tf_op jit(solution)/shard_map/ppermute | solution.py:29

commit v5 on v3

--- a/solution.py
+++ b/solution.py
@@ -187,22 +187,13 @@
     out_ref[2:, :] = jnp.zeros((6, 2 * width), jnp.float32)
 
 
-def grads_kernel(
-    tasks, slots, place_ref, lengths_ref, order_ref, query_ref, other_query_ref, grad_ref, other_grad_ref,
-    stats_ref, other_stats_ref, here, back, back2, far, *refs,
+def operands_kernel(
+    place_ref, lengths_ref, order_ref, query_ref, other_query_ref, grad_ref, other_grad_ref,
+    starts_ref, query_t, grad_t, query_s, grad_s,
 ):
-    first = FAR in slots
-    if first:
-        acc, far_ref, refs = refs[0], refs[1], refs[2:]
-    else:
-        acc_in, query_grad_ref, other_query_grad_ref, here_ref, back_ref, back2_ref, acc, refs = *refs[:7], refs[7:]
-    (buffer, query_t, grad_t, query_s, grad_s, key_t, starts_ref, log_ref, delta_ref, prob_s, slope_s, kv_acc,
-     semaphores) = refs
     rows = query_ref.shape[0]
     width = 2 * rows
-    copies = load_keys((here, back, back2, far), buffer, semaphores)
-    base, x = place_ref[0], place_ref[1]
-    set_queries(base, x, lengths_ref, order_ref, rows, starts_ref)
+    set_queries(place_ref[0], place_ref[1], lengths_ref, order_ref, rows, starts_ref)
     on_lanes(query_ref, query_t, 0)
     on_lanes(other_query_ref, query_t, width)
     for i, (queries, grads) in enumerate(((query_ref, grad_ref), (other_query_ref, other_grad_ref))):
@@ -212,6 +203,23 @@
             grad_t[:, at : at + rows] = grad
             grad_s[at : at + rows, :] = grad.T
             query_s[at : at + rows, :] = queries[:, head * HD : (head + 1) * HD]
+
+
+def grads_kernel(
+    tasks, slots, place_ref, starts_ref, query_t, grad_t, query_s, grad_s,
+    stats_ref, other_stats_ref, here, back, back2, far, *refs,
+):
+    first = FAR in slots
+    if first:
+        acc, far_ref, refs = refs[0], refs[1], refs[2:]
+    else:
+        acc_in, query_grad_ref, other_query_grad_ref, here_ref, back_ref, back2_ref, acc, refs = *refs[:7], refs[7:]
+    buffer, key_t, log_ref, delta_ref, prob_s, slope_s, kv_acc, semaphores = refs
+    rows = key_t.shape[2]
+    width = 2 * rows
+    copies = load_keys((here, back, back2, far), buffer, semaphores)
+    base, x = place_ref[0], place_ref[1]
+    for i in range(2):
         lanes, mirrored = slice(i * width, (i + 1) * width), slice((1 - i) * width, (2 - i) * width)
         total = stats_ref[0:2, lanes] + other_stats_ref[0:2, mirrored]
         log_ref[:, lanes] = jnp.log2(total[0:1])
@@ -353,9 +361,25 @@
     )(sums, attended, grads, other_grads)
 
 
-def backward_grads(place, lengths, order, queries, other_queries, grads, other_grads, stats, other_stats, keys, acc):
+def gradient_operands(place, lengths, order, queries, other_queries, grads, other_grads):
     rows = queries.shape[0]
     width = 2 * rows
+    return pl.pallas_call(
+        operands_kernel,
+        out_shape=(like((1, 2 * width), jnp.int32),)
+        + (like((HD, 2 * width), jnp.bfloat16),) * 2
+        + (like((2 * width, HD), jnp.bfloat16),) * 2,
+        in_specs=[smem()] * 3 + [vmem()] * 4,
+        out_specs=(vmem(),) * 5,
+        compiler_params=params(),
+        cost_estimate=cost(8 * HD * width, 2_400_000),
+        name="gradient_operands",
+    )(place, lengths, order, queries, other_queries, grads, other_grads)
+
+
+def backward_grads(place, operands, stats, other_stats, keys, acc):
+    width = operands[0].shape[1] // 2
+    rows = width // 2
     first = acc is None
     tasks, slots = ((4, 5, 6, 7), (FAR_BACK, FAR)) if first else ((0, 1, 2, 3), (HERE, SECOND, BACK))
     pairs = len(tasks) * width * rows
@@ -368,16 +392,11 @@
     return pl.pallas_call(
         functools.partial(grads_kernel, tasks, slots),
         out_shape=out_shape,
-        in_specs=[smem()] * 3 + [vmem()] * 6 + [hbm()] * 4 + ([] if first else [vmem()]),
+        in_specs=[smem()] + [vmem()] * 7 + [hbm()] * 4 + ([] if first else [vmem()]),
         out_specs=(vmem(),) * len(out_shape),
         scratch_shapes=([] if first else [pltpu.VMEM((HD, 2 * width), jnp.float32)]) + [
             pltpu.VMEM((5, 2, rows, HD), jnp.bfloat16),
-            pltpu.VMEM((HD, 2 * width), jnp.bfloat16),
-            pltpu.VMEM((HD, 2 * width), jnp.bfloat16),
-            pltpu.VMEM((2 * width, HD), jnp.bfloat16),
-            pltpu.VMEM((2 * width, HD), jnp.bfloat16),
             pltpu.VMEM((2, HD, rows), jnp.bfloat16),
-            pltpu.VMEM((1, 2 * width), jnp.int32),
             pltpu.VMEM((1, 2 * width), jnp.float32),
             pltpu.VMEM((1, 2 * width), jnp.float32),
             pltpu.VMEM((2, rows, width), jnp.bfloat16),
@@ -389,8 +408,7 @@
         cost_estimate=cost(10 * pairs * HD, 4_000_000, 2 * pairs),
         name="far_grads" if first else "near_grads",
     )(
-        place, lengths, order, queries, other_queries, grads, other_grads, stats, other_stats, *keys,
-        *(() if first else (acc,)),
+        place, *operands, stats, other_stats, *keys, *(() if first else (acc,)),
     )
 
 
@@ -426,9 +444,10 @@
     stats = partial_deltas(sums, attended, grads, other_grads)
     other_stats = to_query_partner(stats)
 
-    common = (
-        place, doc_lengths, doc_order, query_rows, other_queries, grads, other_grads, stats, other_stats, keys
-    )
+    operands = gradient_operands(
+        place, doc_lengths, doc_order, query_rows, other_queries, grads, other_grads
+    )
+    common = (place, operands, stats, other_stats, keys)
     acc, far_grads = backward_grads(*common, None)
     far_grads = to_key_partner(far_grads).astype(jnp.float32)
     query_grads, other_query_grads, here_grads, back_grads, back2_grads = backward_grads(*common, acc)

time: 106 us -> 106 us (level)
  transfers between devices with their start and end apart: 16 -> 16, of which waited for: 7 -> 7; matrix products, arithmetic and copies ran while one was open for 4% -> 4% of each run, Pallas kernels for 11% -> 12%
where the time goes in v5:
time: 106 us; the launch traced here: 105 us
  starting transfers between devices  49.1 us (46%)
  waiting for transfers between devices  27.4 us (26%)
  Pallas kernels  21.9 us (21%)
  other arithmetic  4.07 us (4%)
  local copies, waits for them, and re-layouts  1.77 us (2%)
    ppermute x16, starting transfers between devices, permuted(): return lax.ppermute(block, axis, route)  49.1 us
    ppermute x16, waiting for transfers between devices, permuted(): return lax.ppermute(block, axis, route)  27.4 us
    pallas_call x2, Pallas kernels, backward_grads(): pl.pallas_call(functools.partial(grads_kernel, tasks, slots), out_shape=o...  11.9 us
    pallas_call x1, Pallas kernels, forward_stats(): pl.pallas_call(stats_kernel, out_shape=(like((1, 2 * width), jnp.float32)...  5.45 us
    pallas_call x1, Pallas kernels, project(): pl.pallas_call(project_kernel, out_shape=(like((heads, rows), jnp.float32...  3.66 us
  transfers between devices with their start and end apart: 16, of which 7 were waited for; matrix products, arithmetic and copies ran while one was open for 4% of the time, Pallas kernels for 12%

profile of v5, /device:TPU:250, one launch (start us, length us, event | category | flops | bytes accessed | tf_op | source)
XLA Modules:
  0.0 105.2 jit_solution(7486911269222870143)
XLA Ops:
  0.6 2.1 %collective-permute-start.7 = (bf16[256,4608]{1,0:T(8,128)(2,1)}, bf16[256,4608]{1,0:T(8,128)(2,1)}, u32[]{:S(2)}, u32[]{:S(2)}) collective-permute-start(bf16[256,4608]{1,0:T(8,128)(2,1)} %own_weight.1), channel_id=1, source_target_pairs={{0,1},{1,0},{2,3},{3,2},{4,5},{5,4},{6,7},{7,6},{8,9},{9,8},{10,11... | collective-permute-start | bytes 7077896 | tf_op jit(solution)/shard_map/ppermute | solution.py:29
  2.7 2.1 %collective-permute-start.1 = (bf16[576,384]{1,0:T(8,128)(2,1)}, bf16[576,384]{1,0:T(8,128)(2,1)S(1)}, u32[]{:S(2)}, u32[]{:S(2)}) collective-permute-start(bf16[576,384]{1,0:T(8,128)(2,1)} %bitcast.28), channel_id=1, source_target_pairs={{0,2},{1,3},{2,4},{3,5},{4,6},{5,7},{6,0},{7,1},{8,10},{9,11},{10,... | collective-permute-start | bytes 1327112 | tf_op jit(solution)/shard_map/ppermute | solution.py:29
  4.8 3.7 %collective-permute-start.2 = (bf16[576,384]{1,0:T(8,128)(2,1)}, bf16[576,384]{1,0:T(8,128)(2,1)S(1)}, u32[]{:S(2)}, u32[]{:S(2)}) collective-permute-start(bf16[576,384]{1,0:T(8,128)(2,1)} %bitcast.29), channel_id=1, source_target_pairs={{0,6},{1,7},{2,0},{3,1},{4,2},{5,3},{6,4},{7,5},{8,14},{9,15},{10,... | collective-permute-start | bytes 1327112 | tf_op jit(solution)/shard_map/ppermute | solution.py:29
  8.6 1.0 pad_maximum_fusion.1.here
  9.5 5.0 %collective-permute-start.3 = (bf16[2,384,128]{2,1,0:T(8,128)(2,1)S(1)}, bf16[2,384,128]{2,1,0:T(8,128)(2,1)}, u32[]{:S(2)}, u32[]{:S(2)}) collective-permute-start(bf16[2,384,128]{2,1,0:T(8,128)(2,1)S(1)} %pad_maximum_fusion.1.here), channel_id=1, source_target_pairs={{0,32},{8,40},{16,48},{24,56},{32,64},{40,72},{48,80},{56,88},{64,... | collective-permute-start | bytes 589832 | tf_op jit(solution)/shard_map/ppermute | solution.py:29
  14.6 3.4 %collective-permute-start.4 = (bf16[2,384,128]{2,1,0:T(8,128)(2,1)S(1)}, bf16[2,384,128]{2,1,0:T(8,128)(2,1)}, u32[]{:S(2)}, u32[]{:S(2)}) collective-permute-start(bf16[2,384,128]{2,1,0:T(8,128)(2,1)S(1)} %pad_maximum_fusion.1.here), channel_id=1, source_target_pairs={{8,72},{16,80},{24,88},{40,104},{48,112},{56,120},{72,136},{80,144... | collective-permute-start | bytes 589832 | tf_op jit(solution)/shard_map/ppermute | solution.py:29
  18.0 0.1 pad_add_fusion.place_ref
  18.1 3.4 %collective-permute-done.3.back = bf16[2,384,128]{2,1,0:T(8,128)(2,1)} collective-permute-done((bf16[2,384,128]{2,1,0:T(8,128)(2,1)S(1)}, bf16[2,384,128]{2,1,0:T(8,128)(2,1)}, u32[]{:S(2)}, u32[]{:S(2)}) %collective-permute-start.3) | collective-permute-done | bytes 196640 | tf_op jit(solution)/shard_map/ppermute | solution.py:29
  21.5 0.0 collective-permute-done.1.before
  21.5 0.0 collective-permute-done.2.after
  21.5 3.3 %collective-permute-start.5 = (bf16[288,384]{1,0:T(8,128)(2,1)S(1)}, bf16[288,384]{1,0:T(8,128)(2,1)S(1)}, u32[]{:S(2)}, u32[]{:S(2)}) collective-permute-start(bf16[288,384]{1,0:T(8,128)(2,1)S(1)} %slice.19), channel_id=1, source_target_pairs={{0,2},{1,3},{2,4},{3,5},{4,6},{5,7},{6,0},{7,1},{8,10},{9,11},{10,... | collective-permute-start | bytes 663560 | tf_op jit(solution)/shard_map/ppermute | solution.py:29
  24.9 2.5 %collective-permute-start.6 = (bf16[288,384]{1,0:T(8,128)(2,1)S(1)}, bf16[288,384]{1,0:T(8,128)(2,1)S(1)}, u32[]{:S(2)}, u32[]{:S(2)}) collective-permute-start(bf16[288,384]{1,0:T(8,128)(2,1)S(1)} %slice.20), channel_id=1, source_target_pairs={{0,6},{1,7},{2,0},{3,1},{4,2},{5,3},{6,4},{7,5},{8,14},{9,15},{10,... | collective-permute-start | bytes 663560 | tf_op jit(solution)/shard_map/ppermute | solution.py:29
  27.4 0.0 collective-permute-done.4.back2
  27.4 1.0 select_bitcast_fusion
  28.4 0.0 copy-start.2
  28.4 0.0 copy-start.3
  28.4 0.0 copy-start.4
  28.4 1.0 pad_maximum_fusion
  29.4 0.0 collective-permute-done.5.across_low
  29.4 4.5 %collective-permute-done.6.across_high = bf16[288,384]{1,0:T(8,128)(2,1)S(1)} collective-permute-done((bf16[288,384]{1,0:T(8,128)(2,1)S(1)}, bf16[288,384]{1,0:T(8,128)(2,1)S(1)}, u32[]{:S(2)}, u32[]{:S(2)}) %collective-permute-start.6) | collective-permute-done | bytes 221216 | tf_op jit(solution)/shard_map/ppermute | solution.py:29
  33.9 0.0 collective-permute-done.7.other_weight
  33.9 1.0 copy-done.1
  34.9 3.7 %head_projection.1 = (f32[256,384]{1,0:T(8,128)S(1)}, f32[256,384]{1,0:T(8,128)S(1)}) custom-call(s32[4]{0:T(128)S(1)} %pad_add_fusion.place_ref, bf16[576,384]{1,0:T(8,128)(2,1)S(1)} %bitcast.30, bf16[576,384]{1,0:T(8,128)(2,1)S(1)} %collective-permute-done.1.before, bf16[576,384]{1,0:T(8,128)(2,1)S(1)} %collective-permute-done.2.after, ...), custom_call_target="tpu_custom_call" | custom-call | flops 905969664 | bytes 5000000 | tf_op jit(solution)/shard_map/head_projection/pallas_call | solution.py:334
  38.6 1.9 %collective-permute-start.8 = (f32[256,384]{1,0:T(8,128)S(1)}, f32[256,384]{1,0:T(8,128)S(1)}, u32[]{:S(2)}, u32[]{:S(2)}) collective-permute-start(f32[256,384]{1,0:T(8,128)S(1)} %get-tuple-element.31), channel_id=1, source_target_pairs={{0,1},{1,0},{2,3},{3,2},{4,5},{5,4},{6,7},{7,6},{8,9},{9,8},{10,11... | collective-permute-start | bytes 1179656 | tf_op jit(solution)/shard_map/ppermute | solution.py:29
  40.5 3.4 %collective-permute-start.10 = (bf16[2,2,384,128]{3,2,1,0:T(8,128)(2,1)S(1)}, bf16[2,2,384,128]{3,2,1,0:T(8,128)(2,1)S(1)}, u32[]{:S(2)}, u32[]{:S(2)}) collective-permute-start(bf16[2,2,384,128]{3,2,1,0:T(8,128)(2,1)S(1)} %pad_maximum_fusion), channel_id=1, source_target_pairs={{0,24},{8,16},{16,8},{24,0},{32,56},{40,48},{48,40},{56,32},{64,88... | collective-permute-start | bytes 1179656 | tf_op jit(solution)/shard_map/ppermute | solution.py:29
  43.9 3.7 %collective-permute-start = (bf16[384,256]{1,0:T(8,128)(2,1)S(1)}, bf16[384,256]{1,0:T(8,128)(2,1)S(1)}, u32[]{:S(2)}, u32[]{:S(2)}) collective-permute-start(bf16[384,256]{1,0:T(8,128)(2,1)S(1)} %copy-done.2), channel_id=1, source_target_pairs={{0,8},{8,0},{16,24},{24,16},{32,40},{40,32},{48,56},{56,48},{64,72... | collective-permute-start | bytes 589832 | tf_op jit(solution)/shard_map/ppermute | solution.py:29
  47.7 2.1 %collective-permute-start.9 = (bf16[256,384]{1,0:T(8,128)(2,1)S(1)}, bf16[256,384]{1,0:T(8,128)(2,1)S(1)}, u32[]{:S(2)}, u32[]{:S(2)}) collective-permute-start(bf16[256,384]{1,0:T(8,128)(2,1)S(1)} %add_convert_fusion.1.grad_ref), channel_id=1, source_target_pairs={{0,8},{8,0},{16,24},{24,16},{32,40},{40,32},{48,56},{56,48},{64,72... | collective-permute-start | bytes 589832 | tf_op jit(solution)/shard_map/ppermute | solution.py:29
  49.9 3.7 %collective-permute-done.other_query_ref = bf16[384,256]{1,0:T(8,128)(2,1)S(1)} collective-permute-done((bf16[384,256]{1,0:T(8,128)(2,1)S(1)}, bf16[384,256]{1,0:T(8,128)(2,1)S(1)}, u32[]{:S(2)}, u32[]{:S(2)}) %collective-permute-start) | collective-permute-done | bytes 196640 | tf_op jit(solution)/shard_map/ppermute | solution.py:29
  53.6 0.4 collective-permute-done.10.far
  53.9 5.4 %attention_stats.1 = (f32[1,1536]{1,0:T(1,128)S(1)}, f32[128,1536]{1,0:T(8,128)S(1)}) custom-call(s32[4]{0:T(128)S(1)} %pad_add_fusion.place_ref, s32[18]{0:T(128)S(1)} %copy-done.3, s32[18]{0:T(128)S(1)} %copy-done.4, bf16[384,256]{1,0:T(8,128)(2,1)S(1)} %copy-done.2, bf16[384,256]{1,0:T(8,128)(2,1)S(1)} %collective-permute-done.other_query_ref, ...), custom_call_target="tpu_custom_call" | custom-call | flops 1207959552 | bytes 3000000 | tf_op jit(solution)/shard_map/attention_stats/pallas_call | solution.py:313
  59.4 0.1 partial_deltas.1.stats_ref
  59.5 3.5 %collective-permute-start.11 = (f32[8,1536]{1,0:T(8,128)S(1)}, f32[8,1536]{1,0:T(8,128)S(1)}, u32[]{:S(2)}, u32[]{:S(2)}) collective-permute-start(f32[8,1536]{1,0:T(8,128)S(1)} %partial_deltas.1.stats_ref), channel_id=1, source_target_pairs={{0,8},{8,0},{16,24},{24,16},{32,40},{40,32},{48,56},{56,48},{64,72... | collective-permute-start | bytes 147464 | tf_op jit(solution)/shard_map/ppermute | solution.py:29
  63.0 0.8 gradient_operands.1
  63.8 1.6 %collective-permute-done.11.other_stats_ref = f32[8,1536]{1,0:T(8,128)S(1)} collective-permute-done((f32[8,1536]{1,0:T(8,128)S(1)}, f32[8,1536]{1,0:T(8,128)S(1)}, u32[]{:S(2)}, u32[]{:S(2)}) %collective-permute-start.11) | collective-permute-done | bytes 49184 | tf_op jit(solution)/shard_map/ppermute | solution.py:29
  65.5 5.9 %far_grads.1 = (f32[128,1536]{1,0:T(8,128)S(1)}, bf16[2,384,256]{2,1,0:T(8,128)(2,1)S(1)}) custom-call(s32[4]{0:T(128)S(1)} %pad_add_fusion.place_ref, s32[1,1536]{1,0:T(1,128)S(1)} %get-tuple-element.32.starts_ref, bf16[128,1536]{1,0:T(8,128)(2,1)S(1)} %get-tuple-element.33.query_t, bf16[128,1536]{1,0:T(8,128)(2,1)S(1)} %get-tuple-element.34.grad_t, ...), custom_call_target="tpu_custom_call" | custom-call | flops 1509949440 | bytes 4000000 | tf_op jit(solution)/shard_map/far_grads/pallas_call | solution.py:392
  71.4 4.0 %collective-permute-start.13 = (bf16[2,384,256]{2,1,0:T(8,128)(2,1)S(1)}, bf16[2,384,256]{2,1,0:T(8,128)(2,1)S(1)}, u32[]{:S(2)}, u32[]{:S(2)}) collective-permute-start(bf16[2,384,256]{2,1,0:T(8,128)(2,1)S(1)} %get-tuple-element.44), channel_id=1, source_target_pairs={{0,24},{8,16},{16,8},{24,0},{32,56},{40,48},{48,40},{56,32},{64,88... | collective-permute-start | bytes 1179656 | tf_op jit(solution)/shard_map/ppermute | solution.py:29
  75.4 5.9 %near_grads.1 = (f32[384,256]{1,0:T(8,128)S(1)}, bf16[384,256]{1,0:T(8,128)(2,1)S(1)}, f32[384,256]{1,0:T(8,128)S(1)}, f32[384,256]{1,0:T(8,128)S(1)}, f32[384,256]{1,0:T(8,128)S(1)}) custom-call(s32[4]{0:T(128)S(1)} %pad_add_fusion.place_ref, s32[1,1536]{1,0:T(1,128)S(1)} %get-tuple-element.32.starts_ref, bf16[128,1536]{1,0:T(8,128)(2,1)S(1)} %get-tuple-element.33.query_t, ...), custom_call_target="tpu_custom_call" | custom-call | flops 1509949440 | bytes 4000000 | tf_op jit(solution)/shard_map/near_grads/pallas_call | solution.py:392
  81.3 4.5 %collective-permute-start.12 = (bf16[384,256]{1,0:T(8,128)(2,1)S(1)}, bf16[384,256]{1,0:T(8,128)(2,1)S(1)}, u32[]{:S(2)}, u32[]{:S(2)}) collective-permute-start(bf16[384,256]{1,0:T(8,128)(2,1)S(1)} %get-tuple-element.42), channel_id=1, source_target_pairs={{0,8},{8,0},{16,24},{24,16},{32,40},{40,32},{48,56},{56,48},{64,72... | collective-permute-start | bytes 589832 | tf_op jit(solution)/shard_map/ppermute | solution.py:29
  85.9 0.1 convert_element_type.30
  86.0 0.1 fusion.1
  86.1 1.9 %collective-permute-start.14 = (bf16[384,256]{1,0:T(8,128)(2,1)S(1)}, bf16[384,256]{1,0:T(8,128)(2,1)S(1)}, u32[]{:S(2)}, u32[]{:S(2)}) collective-permute-start(bf16[384,256]{1,0:T(8,128)(2,1)S(1)} %get-tuple-element.47), channel_id=1, source_target_pairs={{32,0},{40,8},{48,16},{56,24},{64,32},{72,40},{80,48},{88,56},{96,... | collective-permute-start | bytes 589832 | tf_op jit(solution)/shard_map/ppermute | solution.py:29
  88.0 1.9 %collective-permute-start.15 = (bf16[384,256]{1,0:T(8,128)(2,1)S(1)}, bf16[384,256]{1,0:T(8,128)(2,1)S(1)}, u32[]{:S(2)}, u32[]{:S(2)}) collective-permute-start(bf16[384,256]{1,0:T(8,128)(2,1)S(1)} %get-tuple-element.48), channel_id=1, source_target_pairs={{72,8},{80,16},{88,24},{104,40},{112,48},{120,56},{136,72},{144,80... | collective-permute-start | bytes 589832 | tf_op jit(solution)/shard_map/ppermute | solution.py:29
  89.9 0.0 collective-permute-done.12
  90.0 0.7 add_convert_fusion
  90.7 8.4 %collective-permute-done.14 = bf16[384,256]{1,0:T(8,128)(2,1)S(1)} collective-permute-done((bf16[384,256]{1,0:T(8,128)(2,1)S(1)}, bf16[384,256]{1,0:T(8,128)(2,1)S(1)}, u32[]{:S(2)}, u32[]{:S(2)}) %collective-permute-start.14) | collective-permute-done | bytes 196640 | tf_op jit(solution)/shard_map/ppermute | solution.py:29
  99.0 5.4 %collective-permute-done.15 = bf16[384,256]{1,0:T(8,128)(2,1)S(1)} collective-permute-done((bf16[384,256]{1,0:T(8,128)(2,1)S(1)}, bf16[384,256]{1,0:T(8,128)(2,1)S(1)}, u32[]{:S(2)}, u32[]{:S(2)}) %collective-permute-start.15) | collective-permute-done | bytes 196640 | tf_op jit(solution)/shard_map/ppermute | solution.py:29
  104.4 0.1 fusion.5
  104.5 0.7 fusion.6
  (12 shorter events, 0.1 us)
Async XLA Ops:
  0.6 33.3 %copy-start = (bf16[256,4608]{1,0:T(8,128)(2,1)S(1)}, bf16[256,4608]{1,0:T(8,128)(2,1)}, u32[]{:S(2)}) copy-start(bf16[256,4608]{1,0:T(8,128)(2,1)} %own_weight.1) | copy-start | bytes 7077892
  0.6 33.3 %collective-permute-start.7 = (bf16[256,4608]{1,0:T(8,128)(2,1)}, bf16[256,4608]{1,0:T(8,128)(2,1)}, u32[]{:S(2)}, u32[]{:S(2)}) collective-permute-start(bf16[256,4608]{1,0:T(8,128)(2,1)} %own_weight.1), channel_id=1, source_target_pairs={{0,1},{1,0},{2,3},{3,2},{4,5},{5,4},{6,7},{7,6},{8,9},{9,8},{10,11... | collective-permute-start | bytes 7077896 | tf_op jit(solution)/shard_map/ppermute | solution.py:29
  2.7 18.8 %collective-permute-start.1 = (bf16[576,384]{1,0:T(8,128)(2,1)}, bf16[576,384]{1,0:T(8,128)(2,1)S(1)}, u32[]{:S(2)}, u32[]{:S(2)}) collective-permute-start(bf16[576,384]{1,0:T(8,128)(2,1)} %bitcast.28), channel_id=1, source_target_pairs={{0,2},{1,3},{2,4},{3,5},{4,6},{5,7},{6,0},{7,1},{8,10},{9,11},{10,... | collective-permute-start | bytes 1327112 | tf_op jit(solution)/shard_map/ppermute | solution.py:29
  4.8 16.6 %collective-permute-start.2 = (bf16[576,384]{1,0:T(8,128)(2,1)}, bf16[576,384]{1,0:T(8,128)(2,1)S(1)}, u32[]{:S(2)}, u32[]{:S(2)}) collective-permute-start(bf16[576,384]{1,0:T(8,128)(2,1)} %bitcast.29), channel_id=1, source_target_pairs={{0,6},{1,7},{2,0},{3,1},{4,2},{5,3},{6,4},{7,5},{8,14},{9,15},{10,... | collective-permute-start | bytes 1327112 | tf_op jit(solution)/shard_map/ppermute | solution.py:29
  9.5 11.9 %collective-permute-start.3 = (bf16[2,384,128]{2,1,0:T(8,128)(2,1)S(1)}, bf16[2,384,128]{2,1,0:T(8,128)(2,1)}, u32[]{:S(2)}, u32[]{:S(2)}) collective-permute-start(bf16[2,384,128]{2,1,0:T(8,128)(2,1)S(1)} %pad_maximum_fusion.1.here), channel_id=1, source_target_pairs={{0,32},{8,40},{16,48},{24,56},{32,64},{40,72},{48,80},{56,88},{64,... | collective-permute-start | bytes 589832 | tf_op jit(solution)/shard_map/ppermute | solution.py:29
  14.6 12.8 %collective-permute-start.4 = (bf16[2,384,128]{2,1,0:T(8,128)(2,1)S(1)}, bf16[2,384,128]{2,1,0:T(8,128)(2,1)}, u32[]{:S(2)}, u32[]{:S(2)}) collective-permute-start(bf16[2,384,128]{2,1,0:T(8,128)(2,1)S(1)} %pad_maximum_fusion.1.here), channel_id=1, source_target_pairs={{8,72},{16,80},{24,88},{40,104},{48,112},{56,120},{72,136},{80,144... | collective-permute-start | bytes 589832 | tf_op jit(solution)/shard_map/ppermute | solution.py:29
  21.5 7.9 %collective-permute-start.5 = (bf16[288,384]{1,0:T(8,128)(2,1)S(1)}, bf16[288,384]{1,0:T(8,128)(2,1)S(1)}, u32[]{:S(2)}, u32[]{:S(2)}) collective-permute-start(bf16[288,384]{1,0:T(8,128)(2,1)S(1)} %slice.19), channel_id=1, source_target_pairs={{0,2},{1,3},{2,4},{3,5},{4,6},{5,7},{6,0},{7,1},{8,10},{9,11},{10,... | collective-permute-start | bytes 663560 | tf_op jit(solution)/shard_map/ppermute | solution.py:29
  24.9 9.0 %collective-permute-start.6 = (bf16[288,384]{1,0:T(8,128)(2,1)S(1)}, bf16[288,384]{1,0:T(8,128)(2,1)S(1)}, u32[]{:S(2)}, u32[]{:S(2)}) collective-permute-start(bf16[288,384]{1,0:T(8,128)(2,1)S(1)} %slice.20), channel_id=1, source_target_pairs={{0,6},{1,7},{2,0},{3,1},{4,2},{5,3},{6,4},{7,5},{8,14},{9,15},{10,... | collective-permute-start | bytes 663560 | tf_op jit(solution)/shard_map/ppermute | solution.py:29
  28.4 15.6 %copy-start.2 = (bf16[384,256]{1,0:T(8,128)(2,1)S(1)}, bf16[384,256]{1,0:T(8,128)(2,1)}, u32[]{:S(2)}) copy-start(bf16[384,256]{1,0:T(8,128)(2,1)} %query_ref.3) | copy-start | bytes 589828
  28.4 25.5 %copy-start.3 = (s32[18]{0:T(128)S(1)}, s32[18]{0:T(128)}, u32[]{:S(2)}) copy-start(s32[18]{0:T(128)} %lengths_ref.3) | copy-start | bytes 220
  28.4 25.5 %copy-start.4 = (s32[18]{0:T(128)S(1)}, s32[18]{0:T(128)}, u32[]{:S(2)}) copy-start(s32[18]{0:T(128)} %order_ref.3) | copy-start | bytes 220
  33.9 1.0 copy-start.1
  38.6 9.1 %collective-permute-start.8 = (f32[256,384]{1,0:T(8,128)S(1)}, f32[256,384]{1,0:T(8,128)S(1)}, u32[]{:S(2)}, u32[]{:S(2)}) collective-permute-start(f32[256,384]{1,0:T(8,128)S(1)} %get-tuple-element.31), channel_id=1, source_target_pairs={{0,1},{1,0},{2,3},{3,2},{4,5},{5,4},{6,7},{7,6},{8,9},{9,8},{10,11... | collective-permute-start | bytes 1179656 | tf_op jit(solution)/shard_map/ppermute | solution.py:29
  40.5 13.4 %collective-permute-start.10 = (bf16[2,2,384,128]{3,2,1,0:T(8,128)(2,1)S(1)}, bf16[2,2,384,128]{3,2,1,0:T(8,128)(2,1)S(1)}, u32[]{:S(2)}, u32[]{:S(2)}) collective-permute-start(bf16[2,2,384,128]{3,2,1,0:T(8,128)(2,1)S(1)} %pad_maximum_fusion), channel_id=1, source_target_pairs={{0,24},{8,16},{16,8},{24,0},{32,56},{40,48},{48,40},{56,32},{64,88... | collective-permute-start | bytes 1179656 | tf_op jit(solution)/shard_map/ppermute | solution.py:29
  43.9 9.6 %collective-permute-start = (bf16[384,256]{1,0:T(8,128)(2,1)S(1)}, bf16[384,256]{1,0:T(8,128)(2,1)S(1)}, u32[]{:S(2)}, u32[]{:S(2)}) collective-permute-start(bf16[384,256]{1,0:T(8,128)(2,1)S(1)} %copy-done.2), channel_id=1, source_target_pairs={{0,8},{8,0},{16,24},{24,16},{32,40},{40,32},{48,56},{56,48},{64,72... | collective-permute-start | bytes 589832 | tf_op jit(solution)/shard_map/ppermute | solution.py:29
  47.7 11.7 %collective-permute-start.9 = (bf16[256,384]{1,0:T(8,128)(2,1)S(1)}, bf16[256,384]{1,0:T(8,128)(2,1)S(1)}, u32[]{:S(2)}, u32[]{:S(2)}) collective-permute-start(bf16[256,384]{1,0:T(8,128)(2,1)S(1)} %add_convert_fusion.1.grad_ref), channel_id=1, source_target_pairs={{0,8},{8,0},{16,24},{24,16},{32,40},{40,32},{48,56},{56,48},{64,72... | collective-permute-start | bytes 589832 | tf_op jit(solution)/shard_map/ppermute | solution.py:29
  59.5 6.0 %collective-permute-start.11 = (f32[8,1536]{1,0:T(8,128)S(1)}, f32[8,1536]{1,0:T(8,128)S(1)}, u32[]{:S(2)}, u32[]{:S(2)}) collective-permute-start(f32[8,1536]{1,0:T(8,128)S(1)} %partial_deltas.1.stats_ref), channel_id=1, source_target_pairs={{0,8},{8,0},{16,24},{24,16},{32,40},{40,32},{48,56},{56,48},{64,72... | collective-permute-start | bytes 147464 | tf_op jit(solution)/shard_map/ppermute | solution.py:29
  71.4 14.4 %collective-permute-start.13 = (bf16[2,384,256]{2,1,0:T(8,128)(2,1)S(1)}, bf16[2,384,256]{2,1,0:T(8,128)(2,1)S(1)}, u32[]{:S(2)}, u32[]{:S(2)}) collective-permute-start(bf16[2,384,256]{2,1,0:T(8,128)(2,1)S(1)} %get-tuple-element.44), channel_id=1, source_target_pairs={{0,24},{8,16},{16,8},{24,0},{32,56},{40,48},{48,40},{56,32},{64,88... | collective-permute-start | bytes 1179656 | tf_op jit(solution)/shard_map/ppermute | solution.py:29
  81.3 8.6 %collective-permute-start.12 = (bf16[384,256]{1,0:T(8,128)(2,1)S(1)}, bf16[384,256]{1,0:T(8,128)(2,1)S(1)}, u32[]{:S(2)}, u32[]{:S(2)}) collective-permute-start(bf16[384,256]{1,0:T(8,128)(2,1)S(1)} %get-tuple-element.42), channel_id=1, source_target_pairs={{0,8},{8,0},{16,24},{24,16},{32,40},{40,32},{48,56},{56,48},{64,72... | collective-permute-start | bytes 589832 | tf_op jit(solution)/shard_map/ppermute | solution.py:29
  86.1 13.0 %collective-permute-start.14 = (bf16[384,256]{1,0:T(8,128)(2,1)S(1)}, bf16[384,256]{1,0:T(8,128)(2,1)S(1)}, u32[]{:S(2)}, u32[]{:S(2)}) collective-permute-start(bf16[384,256]{1,0:T(8,128)(2,1)S(1)} %get-tuple-element.47), channel_id=1, source_target_pairs={{32,0},{40,8},{48,16},{56,24},{64,32},{72,40},{80,48},{88,56},{96,... | collective-permute-start | bytes 589832 | tf_op jit(solution)/shard_map/ppermute | solution.py:29
  88.0 16.4 %collective-permute-start.15 = (bf16[384,256]{1,0:T(8,128)(2,1)S(1)}, bf16[384,256]{1,0:T(8,128)(2,1)S(1)}, u32[]{:S(2)}, u32[]{:S(2)}) collective-permute-start(bf16[384,256]{1,0:T(8,128)(2,1)S(1)} %get-tuple-element.48), channel_id=1, source_target_pairs={{72,8},{80,16},{88,24},{104,40},{112,48},{120,56},{136,72},{144,80... | collective-permute-start | bytes 589832 | tf_op jit(solution)/shard_map/ppermute | solution.py:29

commit v6 on v5

--- a/solution.py
+++ b/solution.py
@@ -66,15 +66,25 @@
     return keep
 
 
-def load_keys(refs, buffer, semaphores):
+BLOCKS_OF = ((HERE,), (HERE, BACK2), (BACK,), (BACK,), (FAR_BACK,), (FAR_BACK,), (FAR,), (FAR,))
+
+
+def load_keys(refs, buffer, semaphores, tasks):
     here, back, back2, far = refs
-    sources = [here, back, back2, far.at[0], far.at[1]]
-    copies = [
-        pltpu.make_async_copy(source, buffer.at[i], semaphores.at[i]) for i, source in enumerate(sources)
-    ]
-    for copy in copies:
-        copy.start()
-    return copies
+    sources = (here, back, back2, far.at[0], far.at[1])
+    pending = {}
+    for t in tasks:
+        for i in BLOCKS_OF[t]:
+            if i not in pending:
+                pending[i] = pltpu.make_async_copy(sources[i], buffer.at[i], semaphores.at[i])
+                pending[i].start()
+    return pending
+
+
+def wait_keys(pending, t):
+    for i in BLOCKS_OF[t]:
+        if i in pending:
+            pending.pop(i).wait()
 
 
 def set_queries(base, x, lengths_ref, order_ref, rows, starts_ref):
@@ -119,7 +129,7 @@
 ):
     rows = query_ref.shape[0]
     width = 2 * rows
-    copies = load_keys((here, back, back2, far), buffer, semaphores)
+    pending = load_keys((here, back, back2, far), buffer, semaphores, range(TASKS))
     base, x = place_ref[0], place_ref[1]
     set_queries(base, x, lengths_ref, order_ref, rows, starts_ref)
     on_lanes(query_ref, query_t, 0)
@@ -139,9 +149,8 @@
                 sums_ref[:, part] += jnp.sum(expo, axis=0, keepdims=True)
                 attended_ref[:, part] += dot(value_t[:, r : r + ROW_STEP], expo.astype(jnp.bfloat16))
 
-    for copy in copies:
-        copy.wait()
     for t in range(TASKS):
+        wait_keys(pending, t)
         block, key_base = task_of(t, base, x, rows)
         task(block, key_base, t % 2, t == 0)
 
@@ -217,7 +226,7 @@
     buffer, key_t, log_ref, delta_ref, prob_s, slope_s, kv_acc, semaphores = refs
     rows = key_t.shape[2]
     width = 2 * rows
-    copies = load_keys((here, back, back2, far), buffer, semaphores)
+    pending = load_keys((here, back, back2, far), buffer, semaphores, tasks)
     base, x = place_ref[0], place_ref[1]
     for i in range(2):
         lanes, mirrored = slice(i * width, (i + 1) * width), slice((1 - i) * width, (2 - i) * width)
@@ -251,9 +260,8 @@
         kv_acc[out, :, :HD] += dot(slope_s[store], query_s[lanes, :])
         kv_acc[out, :, HD:] += dot(prob_s[store], grad_s[lanes, :])
 
-    for copy in copies:
-        copy.wait()
     for t in tasks:
+        wait_keys(pending, t)
         pairwise(t)
         if t > tasks[0]:
             collect(t - 1)

time: 106 us -> 105 us (level)
  no operation moved by 1% of the time
where the time goes in v6:
time: 105 us
  starting transfers between devices  49.2 us (47%)
  waiting for transfers between devices  27.4 us (26%)
  Pallas kernels  21.2 us (20%)
  other arithmetic  4.07 us (4%)
  local copies, waits for them, and re-layouts  1.77 us (2%)
    ppermute x16, starting transfers between devices, permuted(): return lax.ppermute(block, axis, route)  49.2 us
    ppermute x16, waiting for transfers between devices, permuted(): return lax.ppermute(block, axis, route)  27.4 us
    pallas_call x2, Pallas kernels, backward_grads(): pl.pallas_call(functools.partial(grads_kernel, tasks, slots), out_shape=o...  10.8 us
    pallas_call x1, Pallas kernels, forward_stats(): pl.pallas_call(stats_kernel, out_shape=(like((1, 2 * width), jnp.float32)...  5.78 us
    pallas_call x1, Pallas kernels, project(): pl.pallas_call(project_kernel, out_shape=(like((heads, rows), jnp.float32...  3.66 us
  transfers between devices with their start and end apart: 16, of which 7 were waited for; matrix products, arithmetic and copies ran while one was open for 4% of the time, Pallas kernels for 12%

profile of v6, /device:TPU:250, one launch (start us, length us, event | category | flops | bytes accessed | tf_op | source)
XLA Modules:
  0.0 104.6 jit_solution(15748136663896147763)
XLA Ops:
  0.6 2.1 %collective-permute-start.7 = (bf16[256,4608]{1,0:T(8,128)(2,1)}, bf16[256,4608]{1,0:T(8,128)(2,1)}, u32[]{:S(2)}, u32[]{:S(2)}) collective-permute-start(bf16[256,4608]{1,0:T(8,128)(2,1)} %own_weight.1), channel_id=1, source_target_pairs={{0,1},{1,0},{2,3},{3,2},{4,5},{5,4},{6,7},{7,6},{8,9},{9,8},{10,11... | collective-permute-start | bytes 7077896 | tf_op jit(solution)/shard_map/ppermute | solution.py:29
  2.7 2.1 %collective-permute-start.1 = (bf16[576,384]{1,0:T(8,128)(2,1)}, bf16[576,384]{1,0:T(8,128)(2,1)S(1)}, u32[]{:S(2)}, u32[]{:S(2)}) collective-permute-start(bf16[576,384]{1,0:T(8,128)(2,1)} %bitcast.28), channel_id=1, source_target_pairs={{0,2},{1,3},{2,4},{3,5},{4,6},{5,7},{6,0},{7,1},{8,10},{9,11},{10,... | collective-permute-start | bytes 1327112 | tf_op jit(solution)/shard_map/ppermute | solution.py:29
  4.8 3.7 %collective-permute-start.2 = (bf16[576,384]{1,0:T(8,128)(2,1)}, bf16[576,384]{1,0:T(8,128)(2,1)S(1)}, u32[]{:S(2)}, u32[]{:S(2)}) collective-permute-start(bf16[576,384]{1,0:T(8,128)(2,1)} %bitcast.29), channel_id=1, source_target_pairs={{0,6},{1,7},{2,0},{3,1},{4,2},{5,3},{6,4},{7,5},{8,14},{9,15},{10,... | collective-permute-start | bytes 1327112 | tf_op jit(solution)/shard_map/ppermute | solution.py:29
  8.6 1.0 pad_maximum_fusion.1.here
  9.5 5.0 %collective-permute-start.3 = (bf16[2,384,128]{2,1,0:T(8,128)(2,1)S(1)}, bf16[2,384,128]{2,1,0:T(8,128)(2,1)}, u32[]{:S(2)}, u32[]{:S(2)}) collective-permute-start(bf16[2,384,128]{2,1,0:T(8,128)(2,1)S(1)} %pad_maximum_fusion.1.here), channel_id=1, source_target_pairs={{0,32},{8,40},{16,48},{24,56},{32,64},{40,72},{48,80},{56,88},{64,... | collective-permute-start | bytes 589832 | tf_op jit(solution)/shard_map/ppermute | solution.py:29
  14.6 3.4 %collective-permute-start.4 = (bf16[2,384,128]{2,1,0:T(8,128)(2,1)S(1)}, bf16[2,384,128]{2,1,0:T(8,128)(2,1)}, u32[]{:S(2)}, u32[]{:S(2)}) collective-permute-start(bf16[2,384,128]{2,1,0:T(8,128)(2,1)S(1)} %pad_maximum_fusion.1.here), channel_id=1, source_target_pairs={{8,72},{16,80},{24,88},{40,104},{48,112},{56,120},{72,136},{80,144... | collective-permute-start | bytes 589832 | tf_op jit(solution)/shard_map/ppermute | solution.py:29
  18.0 0.1 pad_add_fusion.place_ref
  18.1 3.4 %collective-permute-done.3.back = bf16[2,384,128]{2,1,0:T(8,128)(2,1)} collective-permute-done((bf16[2,384,128]{2,1,0:T(8,128)(2,1)S(1)}, bf16[2,384,128]{2,1,0:T(8,128)(2,1)}, u32[]{:S(2)}, u32[]{:S(2)}) %collective-permute-start.3) | collective-permute-done | bytes 196640 | tf_op jit(solution)/shard_map/ppermute | solution.py:29
  21.5 0.0 collective-permute-done.1.before
  21.5 0.0 collective-permute-done.2.after
  21.5 3.3 %collective-permute-start.5 = (bf16[288,384]{1,0:T(8,128)(2,1)S(1)}, bf16[288,384]{1,0:T(8,128)(2,1)S(1)}, u32[]{:S(2)}, u32[]{:S(2)}) collective-permute-start(bf16[288,384]{1,0:T(8,128)(2,1)S(1)} %slice.19), channel_id=1, source_target_pairs={{0,2},{1,3},{2,4},{3,5},{4,6},{5,7},{6,0},{7,1},{8,10},{9,11},{10,... | collective-permute-start | bytes 663560 | tf_op jit(solution)/shard_map/ppermute | solution.py:29
  24.9 2.5 %collective-permute-start.6 = (bf16[288,384]{1,0:T(8,128)(2,1)S(1)}, bf16[288,384]{1,0:T(8,128)(2,1)S(1)}, u32[]{:S(2)}, u32[]{:S(2)}) collective-permute-start(bf16[288,384]{1,0:T(8,128)(2,1)S(1)} %slice.20), channel_id=1, source_target_pairs={{0,6},{1,7},{2,0},{3,1},{4,2},{5,3},{6,4},{7,5},{8,14},{9,15},{10,... | collective-permute-start | bytes 663560 | tf_op jit(solution)/shard_map/ppermute | solution.py:29
  27.4 0.0 collective-permute-done.4.back2
  27.4 1.0 select_bitcast_fusion
  28.4 0.0 copy-start.2
  28.4 0.0 copy-start.3
  28.4 0.0 copy-start.4
  28.4 1.0 pad_maximum_fusion
  29.4 4.5 %collective-permute-done.6.across_high = bf16[288,384]{1,0:T(8,128)(2,1)S(1)} collective-permute-done((bf16[288,384]{1,0:T(8,128)(2,1)S(1)}, bf16[288,384]{1,0:T(8,128)(2,1)S(1)}, u32[]{:S(2)}, u32[]{:S(2)}) %collective-permute-start.6) | collective-permute-done | bytes 221216 | tf_op jit(solution)/shard_map/ppermute | solution.py:29
  33.9 0.0 collective-permute-done.7.other_weight
  33.9 1.0 copy-done.1
  34.9 3.7 %head_projection.1 = (f32[256,384]{1,0:T(8,128)S(1)}, f32[256,384]{1,0:T(8,128)S(1)}) custom-call(s32[4]{0:T(128)S(1)} %pad_add_fusion.place_ref, bf16[576,384]{1,0:T(8,128)(2,1)S(1)} %bitcast.30, bf16[576,384]{1,0:T(8,128)(2,1)S(1)} %collective-permute-done.1.before, bf16[576,384]{1,0:T(8,128)(2,1)S(1)} %collective-permute-done.2.after, ...), custom_call_target="tpu_custom_call" | custom-call | flops 905969664 | bytes 5000000 | tf_op jit(solution)/shard_map/head_projection/pallas_call | solution.py:342
  38.6 1.9 %collective-permute-start.8 = (f32[256,384]{1,0:T(8,128)S(1)}, f32[256,384]{1,0:T(8,128)S(1)}, u32[]{:S(2)}, u32[]{:S(2)}) collective-permute-start(f32[256,384]{1,0:T(8,128)S(1)} %get-tuple-element.31), channel_id=1, source_target_pairs={{0,1},{1,0},{2,3},{3,2},{4,5},{5,4},{6,7},{7,6},{8,9},{9,8},{10,11... | collective-permute-start | bytes 1179656 | tf_op jit(solution)/shard_map/ppermute | solution.py:29
  40.5 3.4 %collective-permute-start.10 = (bf16[2,2,384,128]{3,2,1,0:T(8,128)(2,1)S(1)}, bf16[2,2,384,128]{3,2,1,0:T(8,128)(2,1)S(1)}, u32[]{:S(2)}, u32[]{:S(2)}) collective-permute-start(bf16[2,2,384,128]{3,2,1,0:T(8,128)(2,1)S(1)} %pad_maximum_fusion), channel_id=1, source_target_pairs={{0,24},{8,16},{16,8},{24,0},{32,56},{40,48},{48,40},{56,32},{64,88... | collective-permute-start | bytes 1179656 | tf_op jit(solution)/shard_map/ppermute | solution.py:29
  43.9 3.7 %collective-permute-start = (bf16[384,256]{1,0:T(8,128)(2,1)S(1)}, bf16[384,256]{1,0:T(8,128)(2,1)S(1)}, u32[]{:S(2)}, u32[]{:S(2)}) collective-permute-start(bf16[384,256]{1,0:T(8,128)(2,1)S(1)} %copy-done.2), channel_id=1, source_target_pairs={{0,8},{8,0},{16,24},{24,16},{32,40},{40,32},{48,56},{56,48},{64,72... | collective-permute-start | bytes 589832 | tf_op jit(solution)/shard_map/ppermute | solution.py:29
  47.7 0.0 collective-permute-done.8
  47.7 2.1 %collective-permute-start.9 = (bf16[256,384]{1,0:T(8,128)(2,1)S(1)}, bf16[256,384]{1,0:T(8,128)(2,1)S(1)}, u32[]{:S(2)}, u32[]{:S(2)}) collective-permute-start(bf16[256,384]{1,0:T(8,128)(2,1)S(1)} %add_convert_fusion.1.grad_ref), channel_id=1, source_target_pairs={{0,8},{8,0},{16,24},{24,16},{32,40},{40,32},{48,56},{56,48},{64,72... | collective-permute-start | bytes 589832 | tf_op jit(solution)/shard_map/ppermute | solution.py:29
  49.9 3.7 %collective-permute-done.other_query_ref = bf16[384,256]{1,0:T(8,128)(2,1)S(1)} collective-permute-done((bf16[384,256]{1,0:T(8,128)(2,1)S(1)}, bf16[384,256]{1,0:T(8,128)(2,1)S(1)}, u32[]{:S(2)}, u32[]{:S(2)}) %collective-permute-start) | collective-permute-done | bytes 196640 | tf_op jit(solution)/shard_map/ppermute | solution.py:29
  53.6 0.4 collective-permute-done.10.far
  53.9 5.8 %attention_stats.1 = (f32[1,1536]{1,0:T(1,128)S(1)}, f32[128,1536]{1,0:T(8,128)S(1)}) custom-call(s32[4]{0:T(128)S(1)} %pad_add_fusion.place_ref, s32[18]{0:T(128)S(1)} %copy-done.3, s32[18]{0:T(128)S(1)} %copy-done.4, bf16[384,256]{1,0:T(8,128)(2,1)S(1)} %copy-done.2, bf16[384,256]{1,0:T(8,128)(2,1)S(1)} %collective-permute-done.other_query_ref, ...), custom_call_target="tpu_custom_call" | custom-call | flops 1207959552 | bytes 3000000 | tf_op jit(solution)/shard_map/attention_stats/pallas_call | solution.py:321
  59.7 0.1 partial_deltas.1.stats_ref
  59.8 3.5 %collective-permute-start.11 = (f32[8,1536]{1,0:T(8,128)S(1)}, f32[8,1536]{1,0:T(8,128)S(1)}, u32[]{:S(2)}, u32[]{:S(2)}) collective-permute-start(f32[8,1536]{1,0:T(8,128)S(1)} %partial_deltas.1.stats_ref), channel_id=1, source_target_pairs={{0,8},{8,0},{16,24},{24,16},{32,40},{40,32},{48,56},{56,48},{64,72... | collective-permute-start | bytes 147464 | tf_op jit(solution)/shard_map/ppermute | solution.py:29
  63.3 0.8 gradient_operands.1
  64.2 1.6 %collective-permute-done.11.other_stats_ref = f32[8,1536]{1,0:T(8,128)S(1)} collective-permute-done((f32[8,1536]{1,0:T(8,128)S(1)}, f32[8,1536]{1,0:T(8,128)S(1)}, u32[]{:S(2)}, u32[]{:S(2)}) %collective-permute-start.11) | collective-permute-done | bytes 49184 | tf_op jit(solution)/shard_map/ppermute | solution.py:29
  65.8 5.4 %far_grads.1 = (f32[128,1536]{1,0:T(8,128)S(1)}, bf16[2,384,256]{2,1,0:T(8,128)(2,1)S(1)}) custom-call(s32[4]{0:T(128)S(1)} %pad_add_fusion.place_ref, s32[1,1536]{1,0:T(1,128)S(1)} %get-tuple-element.32.starts_ref, bf16[128,1536]{1,0:T(8,128)(2,1)S(1)} %get-tuple-element.33.query_t, bf16[128,1536]{1,0:T(8,128)(2,1)S(1)} %get-tuple-element.34.grad_t, ...), custom_call_target="tpu_custom_call" | custom-call | flops 1509949440 | bytes 4000000 | tf_op jit(solution)/shard_map/far_grads/pallas_call | solution.py:400
  71.2 4.0 %collective-permute-start.13 = (bf16[2,384,256]{2,1,0:T(8,128)(2,1)S(1)}, bf16[2,384,256]{2,1,0:T(8,128)(2,1)S(1)}, u32[]{:S(2)}, u32[]{:S(2)}) collective-permute-start(bf16[2,384,256]{2,1,0:T(8,128)(2,1)S(1)} %get-tuple-element.44), channel_id=1, source_target_pairs={{0,24},{8,16},{16,8},{24,0},{32,56},{40,48},{48,40},{56,32},{64,88... | collective-permute-start | bytes 1179656 | tf_op jit(solution)/shard_map/ppermute | solution.py:29
  75.2 5.5 %near_grads.1 = (f32[384,256]{1,0:T(8,128)S(1)}, bf16[384,256]{1,0:T(8,128)(2,1)S(1)}, f32[384,256]{1,0:T(8,128)S(1)}, f32[384,256]{1,0:T(8,128)S(1)}, f32[384,256]{1,0:T(8,128)S(1)}) custom-call(s32[4]{0:T(128)S(1)} %pad_add_fusion.place_ref, s32[1,1536]{1,0:T(1,128)S(1)} %get-tuple-element.32.starts_ref, bf16[128,1536]{1,0:T(8,128)(2,1)S(1)} %get-tuple-element.33.query_t, ...), custom_call_target="tpu_custom_call" | custom-call | flops 1509949440 | bytes 4000000 | tf_op jit(solution)/shard_map/near_grads/pallas_call | solution.py:400
  80.7 4.5 %collective-permute-start.12 = (bf16[384,256]{1,0:T(8,128)(2,1)S(1)}, bf16[384,256]{1,0:T(8,128)(2,1)S(1)}, u32[]{:S(2)}, u32[]{:S(2)}) collective-permute-start(bf16[384,256]{1,0:T(8,128)(2,1)S(1)} %get-tuple-element.42), channel_id=1, source_target_pairs={{0,8},{8,0},{16,24},{24,16},{32,40},{40,32},{48,56},{56,48},{64,72... | collective-permute-start | bytes 589832 | tf_op jit(solution)/shard_map/ppermute | solution.py:29
  85.2 0.0 collective-permute-done.13
  85.2 0.1 convert_element_type.30
  85.3 0.1 fusion.1
  85.4 1.9 %collective-permute-start.14 = (bf16[384,256]{1,0:T(8,128)(2,1)S(1)}, bf16[384,256]{1,0:T(8,128)(2,1)S(1)}, u32[]{:S(2)}, u32[]{:S(2)}) collective-permute-start(bf16[384,256]{1,0:T(8,128)(2,1)S(1)} %get-tuple-element.47), channel_id=1, source_target_pairs={{32,0},{40,8},{48,16},{56,24},{64,32},{72,40},{80,48},{88,56},{96,... | collective-permute-start | bytes 589832 | tf_op jit(solution)/shard_map/ppermute | solution.py:29
  87.3 1.9 %collective-permute-start.15 = (bf16[384,256]{1,0:T(8,128)(2,1)S(1)}, bf16[384,256]{1,0:T(8,128)(2,1)S(1)}, u32[]{:S(2)}, u32[]{:S(2)}) collective-permute-start(bf16[384,256]{1,0:T(8,128)(2,1)S(1)} %get-tuple-element.48), channel_id=1, source_target_pairs={{72,8},{80,16},{88,24},{104,40},{112,48},{120,56},{136,72},{144,80... | collective-permute-start | bytes 589832 | tf_op jit(solution)/shard_map/ppermute | solution.py:29
  89.3 0.7 add_convert_fusion
  90.0 8.4 %collective-permute-done.14 = bf16[384,256]{1,0:T(8,128)(2,1)S(1)} collective-permute-done((bf16[384,256]{1,0:T(8,128)(2,1)S(1)}, bf16[384,256]{1,0:T(8,128)(2,1)S(1)}, u32[]{:S(2)}, u32[]{:S(2)}) %collective-permute-start.14) | collective-permute-done | bytes 196640 | tf_op jit(solution)/shard_map/ppermute | solution.py:29
  98.4 5.4 %collective-permute-done.15 = bf16[384,256]{1,0:T(8,128)(2,1)S(1)} collective-permute-done((bf16[384,256]{1,0:T(8,128)(2,1)S(1)}, bf16[384,256]{1,0:T(8,128)(2,1)S(1)}, u32[]{:S(2)}, u32[]{:S(2)}) %collective-permute-start.15) | collective-permute-done | bytes 196640 | tf_op jit(solution)/shard_map/ppermute | solution.py:29
  103.8 0.1 fusion.5
  103.9 0.7 fusion.6
  (12 shorter events, 0.1 us)
Async XLA Ops:
  0.6 33.3 %copy-start = (bf16[256,4608]{1,0:T(8,128)(2,1)S(1)}, bf16[256,4608]{1,0:T(8,128)(2,1)}, u32[]{:S(2)}) copy-start(bf16[256,4608]{1,0:T(8,128)(2,1)} %own_weight.1) | copy-start | bytes 7077892
  0.6 33.3 %collective-permute-start.7 = (bf16[256,4608]{1,0:T(8,128)(2,1)}, bf16[256,4608]{1,0:T(8,128)(2,1)}, u32[]{:S(2)}, u32[]{:S(2)}) collective-permute-start(bf16[256,4608]{1,0:T(8,128)(2,1)} %own_weight.1), channel_id=1, source_target_pairs={{0,1},{1,0},{2,3},{3,2},{4,5},{5,4},{6,7},{7,6},{8,9},{9,8},{10,11... | collective-permute-start | bytes 7077896 | tf_op jit(solution)/shard_map/ppermute | solution.py:29
  2.7 18.8 %collective-permute-start.1 = (bf16[576,384]{1,0:T(8,128)(2,1)}, bf16[576,384]{1,0:T(8,128)(2,1)S(1)}, u32[]{:S(2)}, u32[]{:S(2)}) collective-permute-start(bf16[576,384]{1,0:T(8,128)(2,1)} %bitcast.28), channel_id=1, source_target_pairs={{0,2},{1,3},{2,4},{3,5},{4,6},{5,7},{6,0},{7,1},{8,10},{9,11},{10,... | collective-permute-start | bytes 1327112 | tf_op jit(solution)/shard_map/ppermute | solution.py:29
  4.8 16.6 %collective-permute-start.2 = (bf16[576,384]{1,0:T(8,128)(2,1)}, bf16[576,384]{1,0:T(8,128)(2,1)S(1)}, u32[]{:S(2)}, u32[]{:S(2)}) collective-permute-start(bf16[576,384]{1,0:T(8,128)(2,1)} %bitcast.29), channel_id=1, source_target_pairs={{0,6},{1,7},{2,0},{3,1},{4,2},{5,3},{6,4},{7,5},{8,14},{9,15},{10,... | collective-permute-start | bytes 1327112 | tf_op jit(solution)/shard_map/ppermute | solution.py:29
  9.5 11.9 %collective-permute-start.3 = (bf16[2,384,128]{2,1,0:T(8,128)(2,1)S(1)}, bf16[2,384,128]{2,1,0:T(8,128)(2,1)}, u32[]{:S(2)}, u32[]{:S(2)}) collective-permute-start(bf16[2,384,128]{2,1,0:T(8,128)(2,1)S(1)} %pad_maximum_fusion.1.here), channel_id=1, source_target_pairs={{0,32},{8,40},{16,48},{24,56},{32,64},{40,72},{48,80},{56,88},{64,... | collective-permute-start | bytes 589832 | tf_op jit(solution)/shard_map/ppermute | solution.py:29
  14.6 12.8 %collective-permute-start.4 = (bf16[2,384,128]{2,1,0:T(8,128)(2,1)S(1)}, bf16[2,384,128]{2,1,0:T(8,128)(2,1)}, u32[]{:S(2)}, u32[]{:S(2)}) collective-permute-start(bf16[2,384,128]{2,1,0:T(8,128)(2,1)S(1)} %pad_maximum_fusion.1.here), channel_id=1, source_target_pairs={{8,72},{16,80},{24,88},{40,104},{48,112},{56,120},{72,136},{80,144... | collective-permute-start | bytes 589832 | tf_op jit(solution)/shard_map/ppermute | solution.py:29
  21.5 7.9 %collective-permute-start.5 = (bf16[288,384]{1,0:T(8,128)(2,1)S(1)}, bf16[288,384]{1,0:T(8,128)(2,1)S(1)}, u32[]{:S(2)}, u32[]{:S(2)}) collective-permute-start(bf16[288,384]{1,0:T(8,128)(2,1)S(1)} %slice.19), channel_id=1, source_target_pairs={{0,2},{1,3},{2,4},{3,5},{4,6},{5,7},{6,0},{7,1},{8,10},{9,11},{10,... | collective-permute-start | bytes 663560 | tf_op jit(solution)/shard_map/ppermute | solution.py:29
  24.9 9.0 %collective-permute-start.6 = (bf16[288,384]{1,0:T(8,128)(2,1)S(1)}, bf16[288,384]{1,0:T(8,128)(2,1)S(1)}, u32[]{:S(2)}, u32[]{:S(2)}) collective-permute-start(bf16[288,384]{1,0:T(8,128)(2,1)S(1)} %slice.20), channel_id=1, source_target_pairs={{0,6},{1,7},{2,0},{3,1},{4,2},{5,3},{6,4},{7,5},{8,14},{9,15},{10,... | collective-permute-start | bytes 663560 | tf_op jit(solution)/shard_map/ppermute | solution.py:29
  28.4 15.6 %copy-start.2 = (bf16[384,256]{1,0:T(8,128)(2,1)S(1)}, bf16[384,256]{1,0:T(8,128)(2,1)}, u32[]{:S(2)}) copy-start(bf16[384,256]{1,0:T(8,128)(2,1)} %query_ref.3) | copy-start | bytes 589828
  28.4 25.5 %copy-start.3 = (s32[18]{0:T(128)S(1)}, s32[18]{0:T(128)}, u32[]{:S(2)}) copy-start(s32[18]{0:T(128)} %lengths_ref.3) | copy-start | bytes 220
  28.4 25.5 %copy-start.4 = (s32[18]{0:T(128)S(1)}, s32[18]{0:T(128)}, u32[]{:S(2)}) copy-start(s32[18]{0:T(128)} %order_ref.3) | copy-start | bytes 220
  33.9 1.0 copy-start.1
  38.6 9.1 %collective-permute-start.8 = (f32[256,384]{1,0:T(8,128)S(1)}, f32[256,384]{1,0:T(8,128)S(1)}, u32[]{:S(2)}, u32[]{:S(2)}) collective-permute-start(f32[256,384]{1,0:T(8,128)S(1)} %get-tuple-element.31), channel_id=1, source_target_pairs={{0,1},{1,0},{2,3},{3,2},{4,5},{5,4},{6,7},{7,6},{8,9},{9,8},{10,11... | collective-permute-start | bytes 1179656 | tf_op jit(solution)/shard_map/ppermute | solution.py:29
  40.5 13.4 %collective-permute-start.10 = (bf16[2,2,384,128]{3,2,1,0:T(8,128)(2,1)S(1)}, bf16[2,2,384,128]{3,2,1,0:T(8,128)(2,1)S(1)}, u32[]{:S(2)}, u32[]{:S(2)}) collective-permute-start(bf16[2,2,384,128]{3,2,1,0:T(8,128)(2,1)S(1)} %pad_maximum_fusion), channel_id=1, source_target_pairs={{0,24},{8,16},{16,8},{24,0},{32,56},{40,48},{48,40},{56,32},{64,88... | collective-permute-start | bytes 1179656 | tf_op jit(solution)/shard_map/ppermute | solution.py:29
  43.9 9.6 %collective-permute-start = (bf16[384,256]{1,0:T(8,128)(2,1)S(1)}, bf16[384,256]{1,0:T(8,128)(2,1)S(1)}, u32[]{:S(2)}, u32[]{:S(2)}) collective-permute-start(bf16[384,256]{1,0:T(8,128)(2,1)S(1)} %copy-done.2), channel_id=1, source_target_pairs={{0,8},{8,0},{16,24},{24,16},{32,40},{40,32},{48,56},{56,48},{64,72... | collective-permute-start | bytes 589832 | tf_op jit(solution)/shard_map/ppermute | solution.py:29
  47.7 12.0 %collective-permute-start.9 = (bf16[256,384]{1,0:T(8,128)(2,1)S(1)}, bf16[256,384]{1,0:T(8,128)(2,1)S(1)}, u32[]{:S(2)}, u32[]{:S(2)}) collective-permute-start(bf16[256,384]{1,0:T(8,128)(2,1)S(1)} %add_convert_fusion.1.grad_ref), channel_id=1, source_target_pairs={{0,8},{8,0},{16,24},{24,16},{32,40},{40,32},{48,56},{56,48},{64,72... | collective-permute-start | bytes 589832 | tf_op jit(solution)/shard_map/ppermute | solution.py:29
  59.8 6.0 %collective-permute-start.11 = (f32[8,1536]{1,0:T(8,128)S(1)}, f32[8,1536]{1,0:T(8,128)S(1)}, u32[]{:S(2)}, u32[]{:S(2)}) collective-permute-start(f32[8,1536]{1,0:T(8,128)S(1)} %partial_deltas.1.stats_ref), channel_id=1, source_target_pairs={{0,8},{8,0},{16,24},{24,16},{32,40},{40,32},{48,56},{56,48},{64,72... | collective-permute-start | bytes 147464 | tf_op jit(solution)/shard_map/ppermute | solution.py:29
  71.2 14.0 %collective-permute-start.13 = (bf16[2,384,256]{2,1,0:T(8,128)(2,1)S(1)}, bf16[2,384,256]{2,1,0:T(8,128)(2,1)S(1)}, u32[]{:S(2)}, u32[]{:S(2)}) collective-permute-start(bf16[2,384,256]{2,1,0:T(8,128)(2,1)S(1)} %get-tuple-element.44), channel_id=1, source_target_pairs={{0,24},{8,16},{16,8},{24,0},{32,56},{40,48},{48,40},{56,32},{64,88... | collective-permute-start | bytes 1179656 | tf_op jit(solution)/shard_map/ppermute | solution.py:29
  80.7 8.6 %collective-permute-start.12 = (bf16[384,256]{1,0:T(8,128)(2,1)S(1)}, bf16[384,256]{1,0:T(8,128)(2,1)S(1)}, u32[]{:S(2)}, u32[]{:S(2)}) collective-permute-start(bf16[384,256]{1,0:T(8,128)(2,1)S(1)} %get-tuple-element.42), channel_id=1, source_target_pairs={{0,8},{8,0},{16,24},{24,16},{32,40},{40,32},{48,56},{56,48},{64,72... | collective-permute-start | bytes 589832 | tf_op jit(solution)/shard_map/ppermute | solution.py:29
  85.4 12.9 %collective-permute-start.14 = (bf16[384,256]{1,0:T(8,128)(2,1)S(1)}, bf16[384,256]{1,0:T(8,128)(2,1)S(1)}, u32[]{:S(2)}, u32[]{:S(2)}) collective-permute-start(bf16[384,256]{1,0:T(8,128)(2,1)S(1)} %get-tuple-element.47), channel_id=1, source_target_pairs={{32,0},{40,8},{48,16},{56,24},{64,32},{72,40},{80,48},{88,56},{96,... | collective-permute-start | bytes 589832 | tf_op jit(solution)/shard_map/ppermute | solution.py:29
  87.3 16.4 %collective-permute-start.15 = (bf16[384,256]{1,0:T(8,128)(2,1)S(1)}, bf16[384,256]{1,0:T(8,128)(2,1)S(1)}, u32[]{:S(2)}, u32[]{:S(2)}) collective-permute-start(bf16[384,256]{1,0:T(8,128)(2,1)S(1)} %get-tuple-element.48), channel_id=1, source_target_pairs={{72,8},{80,16},{88,24},{104,40},{112,48},{120,56},{136,72},{144,80... | collective-permute-start | bytes 589832 | tf_op jit(solution)/shard_map/ppermute | solution.py:29
